TPU v7x, 32 devices: a whole 2x2x4 slice. The times are simulated.
32 devices in a mesh: dp: 8 (over z, core), tensor: 4 (over y, x).
Axes of the slice: x: 2, y: 2, z: 4, core: 2. Of those that a mesh axis runs over, the one named last changes fastest.
Arguments:
- residual: bfloat16 [8192, 2048], P(('dp', 'tensor')), may hold values from -6 to 6
- segment_ids: int32 [8, 1024], P('dp'), may hold values from 0 to 16, as said below
- norm_gain: float32 [2048], replicated, may hold values from 0.1 to 1.9
- inner_weight: bfloat16 [2048, 2, 4096], P('dp', None, 'tensor'), may hold values from -0.125 to 0.125
- state_weight: bfloat16 [2048, 256], replicated, may hold values from -0.125 to 0.125
- step_weight: bfloat16 [2048, 64], P('dp', 'tensor'), may hold values from -0.125 to 0.125
- conv_weight: float32 [4, 4352], replicated, may hold values from -3 to 3
- conv_bias: float32 [4352], replicated, may hold values from -3 to 3
- step_bias: float32 [64], replicated, may hold values from -6 to -2.5
- decay_log: float32 [64], replicated, may hold values from 0 to 2.77
- skip_gain: float32 [64], replicated, may hold values from 0.5 to 2
- gated_gain: float32 [4096], replicated, may hold values from 0.1 to 1.9
- out_weight: bfloat16 [4096, 2048], P('tensor', 'dp'), may hold values from -0.09375 to 0.09375
- cotangent: bfloat16 [8192, 2048], P(('dp', 'tensor')), may hold values from -6 to 6
Outputs:
- block_out: float32 [8192, 2048], P(('dp', 'tensor'))
- residual_grad: float32 [8192, 2048], P(('dp', 'tensor'))
- norm_gain_grad: float32 [2048], replicated
- inner_weight_grad: float32 [2048, 2, 4096], P('dp', None, 'tensor')
- state_weight_grad: float32 [2048, 256], replicated
- step_weight_grad: float32 [2048, 64], P('dp', 'tensor')
- conv_weight_grad: float32 [4, 4352], replicated
- conv_bias_grad: float32 [4352], replicated
- step_bias_grad: float32 [64], replicated
- decay_log_grad: float32 [64], replicated
- skip_gain_grad: float32 [64], replicated
- gated_gain_grad: float32 [4096], replicated
- out_weight_grad: float32 [4096, 2048], P('tensor', 'dp')
Inputs may be any that keep to these rules, and one draw needn't show every extreme that they name: `segment_ids`: numbers start at 0 in each row and rise by one at each new document; each document has 60 to 800 tokens; some row has a document of exactly 800 tokens, and some row reaches the largest number.
All inputs are finite; a program needn't handle non-finite values.
Results may differ from a plain program's by a relative error of at most 0.014.
Values may be sent and summed in bfloat16 or wider, within the bound.
A program may use at most 192 MiB of HBM per device.

v0:
```python
from functools import partial

import jax
import jax.numpy as jnp
from jax import lax
from jax.sharding import PartitionSpec as P

BLOCK_LEN = 256


epsilon = 1e-05
highest = lax.Precision.HIGHEST


def conv_sequence(channels, segments, kernel, bias_row):
    length = channels.shape[0]
    tap_count = kernel.shape[0]
    result = bias_row + kernel[tap_count - 1] * channels
    for offset in range(1, tap_count):
        shifted = jnp.pad(channels, ((offset, 0), (0, 0)))[:length]
        earlier = jnp.pad(segments, (offset, 0), constant_values=-1)[:length]
        result = result + kernel[tap_count - 1 - offset] * jnp.where(
            (earlier == segments)[:, None], shifted, 0.0
        )
    return result


def scan_sequence(values, step_sizes, decay_rates, input_keys, input_queries, segments, block_size):
    length, head_count, head_width = values.shape
    states = input_keys.shape[1]
    block_count = length // block_size
    log_decay = (step_sizes * decay_rates).reshape(block_count, block_size, head_count)
    cumulative = jnp.cumsum(log_decay, axis=1)
    seg_blocks = segments.reshape(block_count, block_size)
    value_blocks = values.reshape(block_count, block_size, head_count, head_width)
    step_blocks = step_sizes.reshape(block_count, block_size, head_count)
    key_blocks = input_keys.reshape(block_count, block_size, states)
    query_blocks = input_queries.reshape(block_count, block_size, states)
    positions = jnp.arange(block_size)
    causal = positions[:, None] >= positions[None, :]
    allowed = (seg_blocks[:, :, None] == seg_blocks[:, None, :]) & causal[None]
    allowed_heads = allowed[..., None]
    differ = cumulative[:, :, None, :] - cumulative[:, None, :, :]
    decay_matrix = jnp.where(allowed_heads, jnp.exp(jnp.where(allowed_heads, differ, 0.0)), 0.0)
    intersection = jnp.einsum("ctn,csn->cts", query_blocks, key_blocks, precision=highest)
    mixing = decay_matrix * intersection[..., None] * step_blocks[:, None, :, :]
    inside = jnp.einsum("ctsh,cshp->cthp", mixing, value_blocks, precision=highest)
    last_seg = seg_blocks[:, block_size - 1]
    to_end = jnp.exp(cumulative[:, block_size - 1 :, :] - cumulative)
    keep_end = (seg_blocks == last_seg[:, None])[..., None]
    weights_end = jnp.where(keep_end, to_end * step_blocks, 0.0)
    local_states = jnp.einsum(
        "csh,cshp,csn->chpn", weights_end, value_blocks, key_blocks, precision=highest
    )
    whole_decay = jnp.exp(cumulative[:, block_size - 1, :])
    previous_seg = jnp.concatenate([jnp.full((1,), -1, jnp.int32), last_seg[:-1]])
    linked = last_seg == previous_seg

    def carry_step(carried, pieces):
        piece_local, piece_decay, piece_link = pieces
        factor = jnp.where(piece_link, piece_decay, 0.0)
        return (piece_local + factor[:, None, None] * carried, carried)

    start_state = jnp.zeros((head_count, head_width, states), jnp.float32)
    _, entering = lax.scan(carry_step, start_state, (local_states, whole_decay, linked))
    inflow = (seg_blocks == previous_seg[:, None])[..., None]
    weights_in = jnp.where(inflow, jnp.exp(cumulative), 0.0)
    outside = (
        jnp.einsum("ctn,chpn->cthp", query_blocks, entering, precision=highest)
        * weights_in[..., None]
    )
    return (inside + outside).reshape(length, head_count, head_width)


def state_mixer(
    gate_z,
    inner_x,
    state_bc,
    step_raw,
    kernel,
    kernel_bias,
    step_bias,
    decay_log,
    skip_gain,
    segments,
):
    seq_count, length = segments.shape
    head_count = step_raw.shape[1]
    inner_width = inner_x.shape[1]
    states = state_bc.shape[1] // 2
    head_width = inner_width // head_count
    channels = jnp.concatenate([inner_x, state_bc], axis=1).reshape(
        seq_count, length, inner_width + 2 * states
    )
    convolved = jax.vmap(conv_sequence, in_axes=(0, 0, None, None))(
        channels, segments, kernel, kernel_bias
    )
    active = jax.nn.silu(convolved)
    values = active[..., :inner_width].reshape(seq_count, length, head_count, head_width)
    input_keys = active[..., inner_width : inner_width + states]
    input_queries = active[..., inner_width + states :]
    step_sizes = jax.nn.softplus(step_raw.reshape(seq_count, length, head_count) + step_bias)
    decay_rates = -jnp.exp(decay_log)
    scanner = jax.vmap(partial(scan_sequence, block_size=BLOCK_LEN), in_axes=(0, 0, None, 0, 0, 0))
    scanned = scanner(values, step_sizes, decay_rates, input_keys, input_queries, segments)
    mixed_out = scanned + skip_gain[:, None] * values
    return mixed_out.reshape(seq_count * length, inner_width) * jax.nn.silu(gate_z)


def place_slice(whole, piece, offset):
    return lax.dynamic_update_slice(jnp.zeros_like(whole), piece, (offset,))


def per_device(
    residual,
    segment_ids,
    norm_gain,
    inner_weight,
    state_weight,
    step_weight,
    conv_weight,
    conv_bias,
    step_bias,
    decay_log,
    skip_gain,
    gated_gain,
    out_weight,
    cotangent,
):
    tensor_rank = lax.axis_index("tensor")
    model_width = residual.shape[1]
    local_inner = inner_weight.shape[2]
    local_heads = step_weight.shape[1]
    inner_width = gated_gain.shape[0]
    inner_start = tensor_rank * local_inner
    head_start = tensor_rank * local_heads
    contract_rows = (((0,), (0,)), ((), ()))
    contract_cols = (((1,), (1,)), ((), ()))
    stream = residual.astype(jnp.float32)
    scaling = lax.rsqrt(jnp.mean(stream * stream, axis=1, keepdims=True) + epsilon)
    normed = (stream * scaling * norm_gain).astype(jnp.bfloat16)
    gathered = lax.all_gather(normed, "tensor", axis=0, tiled=True)
    inner_all, step_all, out_all = (
        lax.all_gather(inner_weight, "dp", axis=0, tiled=True),
        lax.all_gather(step_weight, "dp", axis=0, tiled=True),
        lax.all_gather(out_weight, "dp", axis=1, tiled=True),
    )
    inner_mat = inner_all.reshape(model_width, 2 * local_inner)
    projected_zx = jnp.dot(gathered, inner_mat, preferred_element_type=jnp.float32)
    state_bc = jnp.dot(gathered, state_weight, preferred_element_type=jnp.float32)
    step_raw = jnp.dot(gathered, step_all, preferred_element_type=jnp.float32)
    kernel = jnp.concatenate(
        [
            lax.dynamic_slice_in_dim(conv_weight, inner_start, local_inner, 1),
            conv_weight[:, inner_width:],
        ],
        axis=1,
    )
    kernel_bias = jnp.concatenate(
        [lax.dynamic_slice_in_dim(conv_bias, inner_start, local_inner, 0), conv_bias[inner_width:]],
        axis=0,
    )
    bias_local = lax.dynamic_slice_in_dim(step_bias, head_start, local_heads, 0)
    decay_local = lax.dynamic_slice_in_dim(decay_log, head_start, local_heads, 0)
    skip_local = lax.dynamic_slice_in_dim(skip_gain, head_start, local_heads, 0)
    gain_local = lax.dynamic_slice_in_dim(gated_gain, inner_start, local_inner, 0)
    gated, pullback = jax.vjp(
        partial(state_mixer, segments=segment_ids),
        projected_zx[:, :local_inner],
        projected_zx[:, local_inner:],
        state_bc,
        step_raw,
        kernel,
        kernel_bias,
        bias_local,
        decay_local,
        skip_local,
    )
    squares = lax.psum(jnp.sum(gated * gated, axis=1), "tensor")
    scale_g = lax.rsqrt(squares / inner_width + epsilon)[:, None]
    normed_g = (gated * scale_g * gain_local).astype(jnp.bfloat16)
    projected = lax.psum_scatter(
        jnp.dot(normed_g, out_all, preferred_element_type=jnp.float32).astype(jnp.bfloat16),
        "tensor",
        scatter_dimension=0,
        tiled=True,
    ).astype(jnp.float32)
    block_out = stream + projected
    cotangent_all = lax.all_gather(cotangent, "tensor", axis=0, tiled=True)
    grad_normed_g = lax.dot_general(
        cotangent_all, out_all, contract_cols, preferred_element_type=jnp.float32
    )
    dot_part = jnp.sum(grad_normed_g * gain_local * gated, axis=1)
    dot_total = lax.psum(dot_part, "tensor")
    out_grad = lax.dot_general(
        normed_g, cotangent_all, contract_rows, preferred_element_type=jnp.float32
    )
    gain_grad_local = jnp.sum(grad_normed_g * gated * scale_g, axis=0)
    grad_gated = (
        scale_g * gain_local * grad_normed_g - gated * scale_g**3 * dot_total[:, None] / inner_width
    )
    (
        grad_z,
        grad_x,
        grad_bc,
        grad_step,
        grad_kernel,
        grad_kernel_bias,
        grad_step_bias,
        grad_decay,
        grad_skip,
    ) = pullback(grad_gated)
    grad_both = jnp.concatenate([grad_z, grad_x], axis=1).astype(jnp.bfloat16)
    grad_bc_low = grad_bc.astype(jnp.bfloat16)
    grad_step_low = grad_step.astype(jnp.bfloat16)
    inner_all, step_all = (
        lax.all_gather(inner_weight, "dp", axis=0, tiled=True),
        lax.all_gather(step_weight, "dp", axis=0, tiled=True),
    )
    inner_mat = inner_all.reshape(model_width, 2 * local_inner)
    total = lax.dot_general(grad_both, inner_mat, contract_cols, preferred_element_type=jnp.float32)
    total = total + lax.dot_general(
        grad_bc_low, state_weight, contract_cols, preferred_element_type=jnp.float32
    )
    grad_normed = lax.psum_scatter(
        (
            total
            + lax.dot_general(
                grad_step_low, step_all, contract_cols, preferred_element_type=jnp.float32
            )
        ).astype(jnp.bfloat16),
        "tensor",
        scatter_dimension=0,
        tiled=True,
    ).astype(jnp.float32)
    inner_grad = lax.dot_general(
        gathered, grad_both, contract_rows, preferred_element_type=jnp.float32
    ).reshape(model_width, 2, local_inner)
    step_grad = lax.dot_general(
        gathered, grad_step_low, contract_rows, preferred_element_type=jnp.float32
    )
    state_grad = lax.dot_general(
        gathered, grad_bc_low, contract_rows, preferred_element_type=jnp.float32
    )
    inner_sum, step_sum, out_sum = (
        lax.psum_scatter(
            inner_grad.astype(jnp.bfloat16), "dp", scatter_dimension=0, tiled=True
        ).astype(jnp.float32),
        lax.psum_scatter(
            step_grad.astype(jnp.bfloat16), "dp", scatter_dimension=0, tiled=True
        ).astype(jnp.float32),
        lax.psum_scatter(
            out_grad.astype(jnp.bfloat16), "dp", scatter_dimension=1, tiled=True
        ).astype(jnp.float32),
    )
    norm_part = jnp.sum(grad_normed * stream * scaling, axis=0)
    along_rows = jnp.sum(grad_normed * norm_gain * stream, axis=1, keepdims=True)
    residual_grad = (
        cotangent.astype(jnp.float32)
        + scaling * norm_gain * grad_normed
        - stream * scaling**3 * along_rows / model_width
    )
    kernel_full = lax.dynamic_update_slice(
        jnp.zeros_like(conv_weight), grad_kernel[:, :local_inner], (0, inner_start)
    )
    kernel_full = lax.dynamic_update_slice(
        kernel_full, grad_kernel[:, local_inner:], (0, inner_width)
    )
    kernel_bias_full = lax.dynamic_update_slice(
        place_slice(conv_bias, grad_kernel_bias[:local_inner], inner_start),
        grad_kernel_bias[local_inner:],
        (inner_width,),
    )
    step_bias_full = place_slice(step_bias, grad_step_bias, head_start)
    decay_full = place_slice(decay_log, grad_decay, head_start)
    skip_full = place_slice(skip_gain, grad_skip, head_start)
    gain_full = place_slice(gated_gain, gain_grad_local, inner_start)
    small_sums = lax.psum(
        (
            norm_part,
            state_grad,
            kernel_full,
            kernel_bias_full,
            step_bias_full,
            decay_full,
            skip_full,
            gain_full,
        ),
        ("dp", "tensor"),
    )
    return (
        block_out,
        residual_grad,
        small_sums[0],
        inner_sum,
        small_sums[1],
        step_sum,
        small_sums[2],
        small_sums[3],
        small_sums[4],
        small_sums[5],
        small_sums[6],
        small_sums[7],
        out_sum,
    )


def solution(mesh):
    placed = (
        P(("dp", "tensor"), None),
        P("dp", None),
        P(),
        P("dp", None, "tensor"),
        P(),
        P("dp", "tensor"),
        P(),
        P(),
        P(),
        P(),
        P(),
        P(),
        P("tensor", "dp"),
        P(("dp", "tensor"), None),
    )
    return jax.shard_map(
        per_device,
        mesh=mesh,
        in_specs=placed,
        out_specs=(
            P(("dp", "tensor"), None),
            P(("dp", "tensor"), None),
            P(),
            P("dp", None, "tensor"),
            P(),
            P("dp", "tensor"),
            P(),
            P(),
            P(),
            P(),
            P(),
            P(),
            P("tensor", "dp"),
        ),
        check_vma=False,
    )
```

profile of v0, /device:TPU:0, one launch (start us, length us, event | category | flops | bytes accessed | tf_op | source)
XLA Modules:
  0.0 1029.1 jit_solution(17535202165451741866)
XLA Ops:
  15.8 15.6 %all_gather.19 = bf16[2048,16]{0,1:T(8,128)(2,1)S(1)} all-gather(bf16[256,16]{0,1:T(8,128)(2,1)S(1)} %copy-done.72), channel_id=1, replica_groups=mesh['dp'=8,'tensor'=4] {'dp'}, dimensions={0}, use_global_device_ids=true | all-gather | bytes 73728 | tf_op jit(solution)/shard_map/all_gather | solution.py:145
  37.1 31.1 %all-gather.5.cloned.1.call-done = bf16[1024,2048]{1,0:T(8,128)(2,1)} async-done(((bf16[256,2048]{1,0:T(8,128)(2,1)}), bf16[1024,2048]{1,0:T(8,128)(2,1)}) %all-gather.5.cloned.1.call-update) | async-done | bytes 4194320 | tf_op jit(solution)/shard_map/all_gather | solution.py:142
  82.2 69.7 %all-gather.7.cloned.1.call-done = bf16[2048,2,1024]{2,1,0:T(2,128)(2,1)} async-done(((bf16[256,2,1024]{2,1,0:T(2,128)(2,1)}), bf16[2048,2,1024]{2,1,0:T(2,128)(2,1)}) %all-gather.7.cloned.1.call-update) | async-done | bytes 8388624 | tf_op jit(solution)/shard_map/all_gather | solution.py:144
  151.9 10.5 %copy.262 = bf16[256,8,2,1024]{3,1,2,0:T(8,128)(2,1)} copy(bf16[256,8,2,1024]{3,2,1,0:T(2,128)(2,1)} %bitcast.281) | data formatting | bytes 16777216
  162.3 12.5 %fusion.137 = f32[1024,2048]{1,0:T(8,128)S(1)} fusion(bf16[1024,2048]{1,0:T(8,128)(2,1)} %all-gather.5.cloned.1.call-done, bf16[2048,2048]{1,0:T(8,128)(2,1)} %bitcast.279), kind=kOutput, calls=%fused_computation.244 | convolution fusion | flops 8589934592 | bytes 20971520 | tf_op jit(solution)/shard_map/dot_general | solution.py:149
  212.9 32.1 %while.37 = (s32[]{:T(128)}, f32[1,16,64,128]{3,2,1,0:T(8,128)S(1)}, f32[4,1,16,64,128]{4,3,2,1,0:T(8,128)}, pred[4,1,16]{2,1,0:T(4,128)(4,1)}, f32[4,1,16,1,1]{...) while((s32[]{:T(128)}, ...), condition=%wide.region_4.5_spmd.clone, body=%wide.region_3.4_spmd.clone.sunk | while | flops 524323 | bytes 2625855 | solution.py:65
  252.2 21.2 %bitcast_add_fusion.3 = f32[1,4,256,16,64]{2,4,3,1,0:T(8,128)} fusion(f32[4,256,16,64]{1,3,2,0:T(8,128)S(1)} %fusion.69, f32[4,256,16]{1,2,0:T(8,128)S(1)} %get-tuple-element.491, f32[4,256,16]{1,2,0:T(8,128)S(1)} %bitcast.303, f32[4,256,256]{2,1,0:T(8,128)S(1)} %copy-done.28, f32[4,256,16]{1,2,0:T(8,128)S(1)} %copy-done.42, ...), kind=kOutput, calls=%fused_computation.85 | convolution fusion | flops 3244294144 | bytes 14090240 | tf_op jit(solution)/shard_map/jvp(vmap(ctsh,cshp->cthp))/dot_general | solution.py:47
  306.2 11.9 %multiply_reduce_fusion.6 = (f32[1024]{0:T(1024)}, f32[1024]{0:T(1024)S(1)}, f32[1024,1024]{1,0:T(8,128)}) fusion(f32[1024,1024]{1,0:T(8,128)} %get-tuple-element.459, f32[1024]{0:T(1024)S(1)} %get-tuple-element.482, f32[1024]{0:T(1024)S(1)} %copy-done.60, bf16[1024,2048]{1,0:T(8,128)(2,1)} %all-gather.11.cloned.1.call-done, ...), kind=kOutput, calls=%fused_computation.91 | convolution fusion | flops 4301256704 | bytes 16793600 | tf_op jit(solution)/shard_map/dot_general | solution.py:190
  326.0 11.6 %fusion.39 = (f32[1024]{0:T(1024)}, f32[1024,1024]{1,0:T(8,128)}, bf16[1024,1024]{1,0:T(8,128)(2,1)}) fusion(f32[1,1024,1280]{2,1,0:T(8,128)} %copy-done.1, f32[1024,2048]{1,0:T(8,128)} %copy-done.12, f32[1024]{0:T(1024)S(1)} %psum.71, f32[1024,1024]{1,0:T(8,128)} %get-tuple-element.459, f32[1024]{0:T(1024)S(1)} %get-tuple-element.481, ...), kind=kLoop, calls=%fused_computation.89 | loop fusion | flops 24116224 | bytes 27287552 | tf_op jit(solution)/shard_map/transpose(jvp())/reduce_sum | solution.py:106
  354.4 10.7 %fusion.85 = f32[4,256,128]{2,1,0:T(8,128)} fusion(f32[4,1,16,64,128]{4,3,2,1,0:T(8,128)} %get-tuple-element.635, f32[4,256,16,64]{1,0,3,2:T(4,128)} %reshape.822, f32[4,256,16]{1,2,0:T(8,128)S(1)} %get-tuple-element.491), kind=kOutput, calls=%fused_computation.146 | convolution fusion | flops 1611661312 | bytes 6881280 | tf_op jit(solution)/shard_map/transpose(jvp(vmap(ctn,chpn->cthp)))/dot_general | solution.py:69
  370.5 29.2 %fusion.8 = (f32[4,256,16]{1,2,0:T(8,128)}, f32[4,256,16]{1,2,0:T(8,128)}, f32[4,256,16]{1,2,0:T(8,128)}, f32[4,256,256]{2,1,0:T(8,128)}) fusion(f32[4,256,256]{2,1,0:T(8,128)S(1)} %copy-done.29, f32[4,256,16]{1,2,0:T(8,128)S(1)} %bitcast.304, f32[4,256,16]{1,2,0:T(8,128)S(1)} %copy-done.42, pred[4,256,256]{2,1,0:T(8,128)(4,1)S(1)} %compare_and_fusion, ...), kind=kOutput, calls=%fused_computation.27 | convolution fusion | flops 3283828736 | bytes 11075584 | tf_op jit(solution)/shard_map/transpose(jvp(vmap(ctsh,cshp->cthp)))/dot_general | solution.py:47
  401.3 14.0 %while.38 = (s32[]{:T(128)}, f32[1,16,64,128]{3,2,1,0:T(8,128)S(1)}, f32[4,1,16,64,128]{4,3,2,1,0:T(8,128)}, f32[4,1,16]{2,1,0:T(1,128)S(1)}, f32[4,1,16,64,128]...) while((s32[]{:T(128)}, ...), condition=%wide.region_13.14_spmd.clone, body=%wide.region_11.13_spmd.clone.sunk | while | flops 786436 | bytes 3147172 | solution.py:65
  420.8 16.8 %bitcast_add_fusion.2 = f32[1,4,256,16,64]{2,4,3,1,0:T(8,128)} fusion(f32[4,256,16,64]{1,3,2,0:T(8,128)S(1)} %convolution_bitcast_fusion, f32[4,256,16]{1,2,0:T(8,128)S(1)} %bitcast.290, f32[4,256,16]{1,2,0:T(8,128)S(1)} %bitcast.305, f32[4,256,256]{2,1,0:T(8,128)S(1)} %copy-done.30, f32[4,256,16]{1,2,0:T(8,128)S(1)} %copy-done.42, ...), kind=kOutput, calls=%fused_computation.84 | convolution fusion | flops 3244294144 | bytes 14090240 | tf_op jit(solution)/shard_map/transpose(jvp(vmap(ctsh,cshp->cthp)))/dot_general | solution.py:47
  504.9 13.7 %convolution_convert_fusion = bf16[2048,2048]{0,1:T(8,128)(2,1)} fusion(bf16[1024,2048]{1,0:T(8,128)(2,1)} %all-gather.5.cloned.1.call-done, bf16[1024,1024]{1,0:T(8,128)(2,1)S(1)} %split.10, bf16[1024,1024]{1,0:T(8,128)(2,1)} %get-tuple-element.466), kind=kOutput, calls=%fused_computation.42 | convolution fusion | flops 8602517504 | bytes 16777216 | tf_op jit(solution)/shard_map/dot_general | solution.py:236
  518.6 21.4 %copy.239 = bf16[2048,2,1024]{2,1,0:T(2,128)(2,1)} copy(bf16[2048,2,1024]{0,2,1:T(8,128)(2,1)} %bitcast.282) | data formatting | bytes 16777216 | tf_op jit(solution)/shard_map/convert_element_type | solution.py:247
  540.6 10.9 %convolution_convert_fusion.1 = bf16[1024,2048]{1,0:T(8,128)(2,1)} fusion(bf16[1024,2048]{1,0:T(8,128)(2,1)} %all-gather.11.cloned.1.call-done, f32[1024,1024]{1,0:T(8,128)} %get-tuple-element.459, f32[1024]{0:T(1024)S(1)} %copy-done.61, f32[1024]{0:T(1024)S(1)} %copy-done.59), kind=kOutput, calls=%fused_computation.108 | convolution fusion | flops 4300210176 | bytes 12591104 | tf_op jit(solution)/shard_map/dot_general | solution.py:195
  553.9 12.3 %fusion.54 = f32[1024,2048]{1,0:T(8,128)S(1)} fusion(bf16[2048,2048]{1,0:T(8,128)(2,1)} %bitcast.280, bf16[1024,1024]{1,0:T(8,128)(2,1)S(1)} %split.10, bf16[1024,1024]{1,0:T(8,128)(2,1)} %get-tuple-element.466), kind=kOutput, calls=%fused_computation.118 | convolution fusion | flops 8598323200 | bytes 20971520 | tf_op jit(solution)/shard_map/dot_general | solution.py:221
  569.6 10.0 convolution_convert_fusion.2
  589.9 123.7 %all-reduce.24.cloned.1.call-done = bf16[2048,2,1024]{2,1,0:T(2,128)(2,1)} async-done(((bf16[2048,2,1024]{2,1,0:T(2,128)(2,1)}), bf16[2048,2,1024]{2,1,0:T(2,128)(2,1)}) %all-reduce.24.cloned.1.call-update) | async-done | bytes 8388624
  716.9 49.3 %reduce-scatter.11.cloned.1.call-done = bf16[1024,256]{1,0:T(8,128)(2,1)} async-done(((bf16[1024,2048]{1,0:T(8,128)(2,1)}), bf16[1024,256]{1,0:T(8,128)(2,1)}) %reduce-scatter.11.cloned.1.call-update) | async-done | bytes 524304 | tf_op jit(solution)/shard_map/reduce_scatter | solution.py:252
  768.2 52.0 %reduce-scatter.7.cloned.1.call-done = bf16[256,2048]{1,0:T(8,128)(2,1)} async-done(((bf16[1024,2048]{1,0:T(8,128)(2,1)}), bf16[256,2048]{1,0:T(8,128)(2,1)}) %reduce-scatter.7.cloned.1.call-update) | async-done | bytes 1048592 | tf_op jit(solution)/shard_map/reduce_scatter | solution.py:225
  822.1 40.8 %all-reduce.19 = (f32[2048]{0:T(1024)}, f32[4352]{0:T(1024)}, f32[64]{0:T(128)}, f32[64]{0:T(128)}, f32[64]{0:T(128)}, /*index=5*/f32[4096]{0:T(1024)}) all-reduce(f32[2048]{0:T(1024)S(1)} %get-tuple-element.400, f32[4352]{0:T(1024)S(1)} %constant_dynamic-update-slice_fusion.3, ...), channel_id=1, replica_groups=mesh['dp'=8,'tensor'=4] {'dp','tensor'}, use_global_device_ids=true, to_apply=%region_24.25 | all-reduce | flops 10688 | bytes 85504 | tf_op jit(solution)/shard_map/psum | solution.py:278
  862.9 13.3 %reduce-scatter.5.cloned.1.call-done = bf16[256,2048]{1,0:T(8,128)(2,1)} async-done(((bf16[1024,2048]{1,0:T(8,128)(2,1)}), bf16[256,2048]{1,0:T(8,128)(2,1)}) %reduce-scatter.5.cloned.1.call-update) | async-done | bytes 1048592 | tf_op jit(solution)/shard_map/reduce_scatter | solution.py:182
  880.7 137.3 %all-reduce.26.cloned.1.call-done = (f32[2048,256]{1,0:T(8,128)}, f32[4,4352]{1,0:T(4,128)}) async-done(((f32[2048,256]{1,0:T(8,128)}, f32[4,4352]{1,0:T(4,128)}), (f32[2048,256]{1,0:T(8,128)}, f32[4,4352]{1,0:T(4,128)})) %all-reduce.26.cloned.1.call-update) | async-done | bytes 2166800 | tf_op jit(solution)/shard_map/psum | solution.py:278
  (386 shorter events, 287.3 us)
Async XLA Ops:
  7.2 70.8 %copy-start = (bf16[2048,256]{1,0:T(8,128)(2,1)S(1)}, bf16[2048,256]{1,0:T(8,128)(2,1)}, u32[]{:S(2)}) copy-start(bf16[2048,256]{1,0:T(8,128)(2,1)} %param.22) | copy-start | bytes 3145732
  7.2 26.4 %slice-start.2 = ((f32[4,4352]{1,0:T(4,128)}), f32[4,256]{1,0:T(4,128)S(1)}, s32[]{:S(2)}) async-start(f32[4,4352]{1,0:T(4,128)} %param.24), calls=%async_computation.16 | async-start | bytes 8192 | tf_op jit(solution)/shard_map/slice | solution.py:155
  7.2 27.0 %slice-start.3 = ((f32[4352]{0:T(1024)}), f32[256]{0:T(256)S(1)}, s32[]{:S(2)}) async-start(f32[4352]{0:T(1024)} %param.25), calls=%async_computation.17 | async-start | bytes 2048 | tf_op jit(solution)/shard_map/slice | solution.py:160
  7.3 25.5 %copy-start.83 = (f32[64]{0:T(128)S(1)}, f32[64]{0:T(128)}, u32[]{:S(2)}) copy-start(f32[64]{0:T(128)} %param.28) | copy-start | bytes 772
  7.3 60.9 %all-gather.5.cloned.1.call-start = ((), (), s32[]{:S(2)}) async-start(), calls=%async_computation.4 | async-start | bytes 5242880 | tf_op jit(solution)/shard_map/all_gather | solution.py:142
  12.6 139.2 %all-gather.7.cloned.1.call-start = ((), (), s32[]{:S(2)}) async-start(), calls=%async_computation.5 | async-start | bytes 9437184 | tf_op jit(solution)/shard_map/all_gather | solution.py:144
  13.4 292.8 %all-gather.11.cloned.1.call-start = ((), (), s32[]{:S(2)}) async-start(), calls=%async_computation.8 | async-start | bytes 5242880 | tf_op jit(solution)/shard_map/all_gather | solution.py:189
  14.1 292.1 %all-gather.9.cloned.1.call-start = ((), (), s32[]{:S(2)}) async-start(), calls=%async_computation.6 | async-start | bytes 4718592 | tf_op jit(solution)/shard_map/all_gather | solution.py:146
  14.7 573.8 %reduce-scatter.9.cloned.1.call-start = ((), (), s32[]{:S(2)}) async-start(), calls=%async_computation.10 | async-start | bytes 73728 | tf_op jit(solution)/shard_map/reduce_scatter | solution.py:249
  15.7 56.5 %copy-start.75 = (f32[16]{0:T(128)}, f32[16]{0:T(128)S(1)}, u32[]{:S(2)}) copy-start(f32[16]{0:T(128)S(1)} %fusion.123) | copy-start | bytes 196
  31.4 43.9 %copy-start.31 = (bf16[2048,16]{0,1:T(8,128)(2,1)}, bf16[2048,16]{0,1:T(8,128)(2,1)S(1)}, u32[]{:S(2)}) copy-start(bf16[2048,16]{0,1:T(8,128)(2,1)S(1)} %all_gather.19) | copy-start | bytes 196612
  35.3 42.0 %copy-start.68 = (pred[4,256]{1,0:T(4,128)(4,1)}, pred[4,256]{1,0:T(4,128)(4,1)S(1)}, u32[]{:S(2)}) copy-start(pred[4,256]{1,0:T(4,128)(4,1)S(1)} %get-tuple-element.483) | copy-start | bytes 3076
  35.3 42.0 %copy-start.70 = (pred[4,256]{1,0:T(4,128)(4,1)}, pred[4,256]{1,0:T(4,128)(4,1)S(1)}, u32[]{:S(2)}) copy-start(pred[4,256]{1,0:T(4,128)(4,1)S(1)} %get-tuple-element.484) | copy-start | bytes 3076
  82.1 97.9 %copy-start.17 = (f32[1024,256]{1,0:T(8,128)}, f32[1024,256]{1,0:T(8,128)S(1)}, u32[]{:S(2)}) copy-start(f32[1024,256]{1,0:T(8,128)S(1)} %fusion.138) | copy-start | bytes 3145732
  504.9 208.8 %all-reduce.24.cloned.1.call-start = ((), (), s32[]{:S(2)}) async-start(), calls=%async_computation.12 | async-start | bytes 16777216
  540.0 226.2 %reduce-scatter.11.cloned.1.call-start = ((), (), s32[]{:S(2)}) async-start(), calls=%async_computation.11 | async-start | bytes 4718592 | tf_op jit(solution)/shard_map/reduce_scatter | solution.py:252
  551.5 268.7 %reduce-scatter.7.cloned.1.call-start = ((), (), s32[]{:S(2)}) async-start(), calls=%async_computation.9 | async-start | bytes 5242880 | tf_op jit(solution)/shard_map/reduce_scatter | solution.py:225
  569.5 306.7 %reduce-scatter.5.cloned.1.call-start = ((), (), s32[]{:S(2)}) async-start(), calls=%async_computation.7 | async-start | bytes 5242880 | tf_op jit(solution)/shard_map/reduce_scatter | solution.py:182
  579.7 438.4 %all-reduce.26.cloned.1.call-start = ((), (), s32[]{:S(2)}) async-start(), calls=%async_computation.13 | async-start | bytes 4333568 | tf_op jit(solution)/shard_map/psum | solution.py:278
  588.4 231.9 %copy-start.15 = (bf16[256,2048]{1,0:T(8,128)(2,1)S(1)}, bf16[256,2048]{1,0:T(8,128)(2,1)}, u32[]{:S(2)}) copy-start(bf16[256,2048]{1,0:T(8,128)(2,1)} %param.18) | copy-start | bytes 3145732
  588.4 231.9 %copy-start.39 = (f32[2048]{0:T(1024)S(1)}, f32[2048]{0:T(1024)}, u32[]{:S(2)}) copy-start(f32[2048]{0:T(1024)} %param.20) | copy-start | bytes 24580
  588.4 231.9 %copy-start.55 = (f32[256]{0:T(256)S(1)}, f32[256]{0:T(256)}, u32[]{:S(2)}) copy-start(f32[256]{0:T(256)} %copy-done.54) | copy-start | bytes 3076
  588.4 287.8 %copy-start.22 = (bf16[256,2048]{1,0:T(8,128)(2,1)S(1)}, bf16[256,2048]{1,0:T(8,128)(2,1)}, u32[]{:S(2)}) copy-start(bf16[256,2048]{1,0:T(8,128)(2,1)} %param.31) | copy-start | bytes 3145732
  588.4 287.8 %copy-start.77 = (f32[256]{0:T(256)S(1)}, f32[256]{0:T(256)}, u32[]{:S(2)}) copy-start(f32[256]{0:T(256)} %get-tuple-element.485) | copy-start | bytes 3076
  (75 other events, 421.4 us)
Sparse Core Ops, SparseCore 0:
  12.7 55.3 all-gather.4
  69.8 82.0 all-gather.6
  153.7 51.2 all-gather.10
  206.4 47.7 all-gather.8
  505.0 27.9 reduce-scatter.8
  540.1 173.4 all-reduce.23
  716.0 50.1 reduce-scatter.10
  769.4 50.8 reduce-scatter.6
  823.2 52.9 reduce-scatter.4
  883.2 134.8 all-reduce.25
where the time goes:
time: 1030 us
  waiting for transfers between devices  479 us (47%)
  matrix products  201 us (20%)
  local copies, waits for them, and re-layouts  138 us (13%)
  other arithmetic  120 us (12%)
  blocking collectives  74.3 us (7%)
  between operations  16.5 us (2%)
    psum x1, waiting for transfers between devices, per_device(): lax.psum((norm_part, state_grad, kernel_full, kernel_bias_full, step_bias...  137 us
    unnamed x11, waiting for transfers between devices  126 us
    all_gather x1, waiting for transfers between devices, per_device(): lax.all_gather(inner_weight, 'dp', axis=0, tiled=True)  69.7 us
    dot_general x3, matrix products, scan_sequence(): jnp.einsum('ctsh,cshp->cthp', mixing, value_blocks, precision=highest)  67.1 us
    reduce_scatter x1, waiting for transfers between devices, per_device(): lax.psum_scatter((total + lax.dot_general(grad_step_low, step_all, contra...  52 us
    reduce_scatter x1, waiting for transfers between devices, per_device(): lax.psum_scatter(out_grad.astype(jnp.bfloat16), 'dp', scatter_dimension=1...  49.3 us
    psum x1, blocking collectives, per_device(): lax.psum((norm_part, state_grad, kernel_full, kernel_bias_full, step_bias...  40.8 us
    all_gather x1, waiting for transfers between devices, per_device(): gathered = lax.all_gather(normed, 'tensor', axis=0, tiled=True)  31.1 us
  transfers between devices with their start and end apart: 10, of which 7 were waited for; matrix products, arithmetic and copies ran while one was open for 24% of the time, Pallas kernels for 0%

commit v1 on v0

v1 whole, which is shorter than its diff:
```python
import functools
import jax
import jax.numpy as jnp
from jax import lax
from jax.experimental import pallas as pl
from jax.experimental.pallas import tpu as pltpu
from jax.sharding import PartitionSpec as P

LANES = 128
BLOCK = 128
WIDTH = 64
VMEM_BYTES = 56 * 1024 * 1024
f32, bf16 = jnp.float32, jnp.bfloat16
ROWS0 = (((0,), (0,)), ((), ()))
COLS1 = (((1,), (1,)), ((), ()))


def mm(a, b):
    return jnp.dot(a, b, preferred_element_type=f32)


def mm_tn(a, b):
    return lax.dot_general(a, b, ROWS0, preferred_element_type=f32)


def mm_nt(a, b):
    return lax.dot_general(a, b, COLS1, preferred_element_type=f32)


def sigmoid(v):
    return 0.5 + 0.5 * jnp.tanh(0.5 * v)


def two_parts(v, low_lanes):
    high = v.astype(bf16)
    return jnp.where(low_lanes, (v - high.astype(f32)).astype(bf16), high)


def head_sums(v, spread):
    high = v.astype(bf16)
    low = (v - high.astype(f32)).astype(bf16)
    return mm_nt(high, spread) + mm_nt(low, spread)


def shifted_masks(seg_ext, seg):
    n = seg.shape[0]
    return [None] + [seg_ext[8 - k : 8 - k + n] == seg for k in (1, 2, 3)]


def convolve(tail, part, masks, taps):
    n = part.shape[0]
    ext = jnp.concatenate([tail, part], axis=0)
    shifts = [part] + [
        jnp.where(masks[k], ext[8 - k : 8 - k + n], 0.0) for k in (1, 2, 3)
    ]
    total = taps[4:5] + taps[3:4] * part
    for k in (1, 2, 3):
        total = total + taps[3 - k : 4 - k] * shifts[k]
    return total, shifts


def wide(v):
    return jnp.concatenate([v, v], axis=1)


def step_state(raw, params, seg, prev_seg, end_seg, n):
    row = lax.broadcasted_iota(jnp.int32, (n, n), 0)
    col = lax.broadcasted_iota(jnp.int32, (n, n), 1)
    v = raw + params[0:1]
    dt = jnp.maximum(v, 0.0) + jnp.log1p(jnp.exp(-jnp.abs(v)))
    a = params[1:2]
    cum = jnp.dot(
        (row >= col).astype(f32), dt * a, precision=lax.Precision.HIGHEST, preferred_element_type=f32
    )
    last = cum[n - 1 : n]
    into = jnp.where(seg == prev_seg, jnp.exp(cum), 0.0)
    onto = jnp.where(seg == end_seg, jnp.exp(last - cum), 0.0)
    through = jnp.where(end_seg == prev_seg, jnp.exp(last), 0.0)
    bias = jnp.where((row >= col) & (seg == jnp.transpose(seg)), 0.0, -1e30)
    return v, dt, a, cum, into, onto, through, bias


def scan_fwd_kernel(
    blocks, x_ref, bc_ref, st_ref, seg_ref, tapx_ref, tapbc_ref, par_ref, spread_ref, skip_ref,
    y_ref, h_ref, state, tail_x, tail_bc, tail_seg,
):
    n = BLOCK
    block = pl.program_id(1)

    @pl.when(block == 0)
    def _():
        state[...] = jnp.zeros_like(state)
        tail_x[...] = jnp.zeros_like(tail_x)
        tail_bc[...] = jnp.zeros_like(tail_bc)
        tail_seg[...] = jnp.full_like(tail_seg, -1)

    seg = seg_ref[...]
    masks = shifted_masks(jnp.concatenate([tail_seg[...], seg], axis=0), seg)
    prev_seg, end_seg = tail_seg[7:8], seg[n - 1 : n]
    v, dt, a, cum, into, onto, through, bias = step_state(
        st_ref[...], par_ref[...], seg, prev_seg, end_seg, n
    )
    cum_t = jnp.transpose(cum)
    low_lanes = lax.broadcasted_iota(jnp.int32, (n, LANES), 1) >= LANES // 2
    spread = spread_ref[...]
    dt_w = mm(two_parts(dt, low_lanes), spread)
    into_w = mm(two_parts(into, low_lanes), spread)
    onto_w = mm(two_parts(onto, low_lanes), spread)
    through_w = mm(two_parts(jnp.broadcast_to(through, (8, LANES)), low_lanes[:8]), spread)[0:1]
    bc_masks = [None] + [wide(m) for m in masks[1:]]
    conv_bc, _ = convolve(tail_bc[...], bc_ref[...], bc_masks, tapbc_ref[...])
    act_bc = conv_bc * sigmoid(conv_bc)
    b, c = act_bc[:, :LANES].astype(bf16), act_bc[:, LANES:].astype(bf16)
    cross = mm_nt(c, b)
    entering = state[...].astype(bf16)
    h_ref[...] = entering
    first_half = lax.broadcasted_iota(jnp.int32, (n, LANES), 1) < WIDTH
    for pair in range(x_ref.shape[1] // LANES):
        sl = slice(pair * LANES, (pair + 1) * LANES)
        conv, _ = convolve(tail_x[:, sl], x_ref[:, sl], masks, tapx_ref[:, sl])
        xs = conv * sigmoid(conv)
        xd = xs * dt_w[:, sl]
        outside = mm(c, entering[:, sl]) * into_w[:, sl]
        mixes = []
        for h in (2 * pair, 2 * pair + 1):
            decay = jnp.exp(cum[:, h : h + 1] - cum_t[h : h + 1, :] + bias)
            mixes.append((decay * cross).astype(bf16))
        stacked = jnp.concatenate(
            [jnp.where(first_half, xd, 0.0), jnp.where(first_half, 0.0, xd)], axis=0
        ).astype(bf16)
        inside = mm(jnp.concatenate(mixes, axis=1), stacked)
        y_ref[:, sl] = inside + outside + skip_ref[0:1, sl] * xs
        local = mm_tn(b, (onto_w[:, sl] * xd).astype(bf16))
        state[:, sl] = through_w[:, sl] * state[:, sl] + local
    tail_x[...] = x_ref[n - 8 :, :]
    tail_bc[...] = bc_ref[n - 8 :, :]
    tail_seg[...] = seg_ref[n - 8 :, :]


def scan_forward(x, bc, st, seg, tapx, tapbc, par, spread, skip, nseq):
    tokens, width = x.shape
    n = BLOCK
    blocks = tokens // nseq // n
    at = lambda s, i: (s * blocks + i, 0)
    whole = lambda s, i: (0, 0)
    states = LANES
    return pl.pallas_call(
        functools.partial(scan_fwd_kernel, blocks),
        grid=(nseq, blocks),
        in_specs=[
            pl.BlockSpec((n, width), at),
            pl.BlockSpec((n, 2 * states), at),
            pl.BlockSpec((n, LANES), at),
            pl.BlockSpec((n, LANES), at),
            pl.BlockSpec(tapx.shape, whole),
            pl.BlockSpec(tapbc.shape, whole),
            pl.BlockSpec(par.shape, whole),
            pl.BlockSpec(spread.shape, whole),
            pl.BlockSpec(skip.shape, whole),
        ],
        out_specs=[pl.BlockSpec((n, width), at), pl.BlockSpec((states, width), at)],
        out_shape=[
            jax.ShapeDtypeStruct((tokens, width), f32),
            jax.ShapeDtypeStruct((tokens // n * states, width), bf16),
        ],
        scratch_shapes=[
            pltpu.VMEM((states, width), f32),
            pltpu.VMEM((8, width), f32),
            pltpu.VMEM((8, 2 * states), f32),
            pltpu.VMEM((8, LANES), jnp.int32),
        ],
        compiler_params=pltpu.CompilerParams(vmem_limit_bytes=VMEM_BYTES),
        cost_estimate=pl.CostEstimate(
            flops=tokens * width * 1000, bytes_accessed=tokens * width * 12, transcendentals=0
        ),
        name="scan_forward",
    )(x, bc, st, seg, tapx, tapbc, par, spread, skip)


def fold(v):
    total = v[0:8]
    for r in range(8, v.shape[0], 8):
        total = total + v[r : r + 8]
    return total


def scan_bwd_kernel(
    blocks, x_ref, xt_ref, bc_ref, bct_ref, st_ref, seg_ref, segt_ref, gy_ref, y_ref, h_ref,
    tapx_ref, tapbc_ref, par_ref, spread_ref, skip_ref,
    gx_ref, gbc_ref, gst_ref, gtapx_ref, gtapbc_ref, gpar_ref,
    gstate, head_x, head_bc, head_seg,
):
    n = BLOCK
    step = pl.program_id(1)
    block = blocks - 1 - step

    @pl.when((step == 0) & (pl.program_id(0) == 0))
    def _():
        gtapx_ref[...] = jnp.zeros_like(gtapx_ref)
        gtapbc_ref[...] = jnp.zeros_like(gtapbc_ref)
        gpar_ref[...] = jnp.zeros_like(gpar_ref)

    @pl.when(step == 0)
    def _():
        gstate[...] = jnp.zeros_like(gstate)
        head_x[...] = jnp.zeros_like(head_x)
        head_bc[...] = jnp.zeros_like(head_bc)
        head_seg[...] = jnp.full_like(head_seg, -1)

    seg = seg_ref[...]
    first = block == 0
    seg_tail = jnp.where(first, -1, segt_ref[...])
    masks = shifted_masks(jnp.concatenate([seg_tail, seg], axis=0), seg)
    seg_next = jnp.concatenate([seg, head_seg[...]], axis=0)
    ahead = [None] + [seg_next[k : k + n] == seg for k in (1, 2, 3)]
    prev_seg, end_seg = seg_tail[7:8], seg[n - 1 : n]
    v, dt, a, cum, into, onto, through, bias = step_state(
        st_ref[...], par_ref[...], seg, prev_seg, end_seg, n
    )
    cum_t = jnp.transpose(cum)
    low_lanes = lax.broadcasted_iota(jnp.int32, (n, LANES), 1) >= LANES // 2
    spread = spread_ref[...]
    dt_w = mm(two_parts(dt, low_lanes), spread)
    into_w = mm(two_parts(into, low_lanes), spread)
    onto_w = mm(two_parts(onto, low_lanes), spread)
    through_w = mm(two_parts(jnp.broadcast_to(through, (8, LANES)), low_lanes[:8]), spread)[0:1]
    bc_masks = [None] + [wide(m) for m in masks[1:]]
    tail_bc = jnp.where(first, 0.0, bct_ref[...])
    conv_bc, shifts_bc = convolve(tail_bc, bc_ref[...], bc_masks, tapbc_ref[...])
    sig_bc = sigmoid(conv_bc)
    act_bc = conv_bc * sig_bc
    b, c = act_bc[:, :LANES].astype(bf16), act_bc[:, LANES:].astype(bf16)
    cross = mm_nt(c, b)
    first_half = lax.broadcasted_iota(jnp.int32, (n, LANES), 1) < WIDTH
    halves = lambda t: jnp.concatenate(
        [jnp.where(first_half, t, 0.0), jnp.where(first_half, 0.0, t)], axis=0
    ).astype(bf16)

    gcross = jnp.zeros((n, n), f32)
    gb = jnp.zeros((n, LANES), f32)
    gc = jnp.zeros((n, LANES), f32)
    sum_q = jnp.zeros((n, LANES), f32)
    sum_state = jnp.zeros((n, LANES), f32)
    sum_dt = jnp.zeros((n, LANES), f32)
    sum_skip = jnp.zeros((8, LANES), f32)
    sum_last = jnp.zeros((8, LANES), f32)
    for pair in range(x_ref.shape[1] // LANES):
        sl = slice(pair * LANES, (pair + 1) * LANES)
        tail_x = jnp.where(first, 0.0, xt_ref[:, sl])
        part = x_ref[:, sl]
        taps = tapx_ref[:, sl]
        conv, shifts = convolve(tail_x, part, masks, taps)
        sig = sigmoid(conv)
        xs = conv * sig
        xd = xs * dt_w[:, sl]
        xd_low = xd.astype(bf16)
        gy = gy_ref[:, sl]
        gy_low = gy.astype(bf16)
        skip = skip_ref[0:1, sl]
        inner = y_ref[:, sl] - skip * xs
        spread_p = spread[:, sl]
        gstate_low = gstate[:, sl].astype(bf16)
        before = h_ref[:, sl]
        gy_into = (gy * into_w[:, sl]).astype(bf16)
        xd_onto = (xd * onto_w[:, sl]).astype(bf16)
        gc = gc + mm_nt(gy_into, before)
        gb = gb + mm_nt(xd_onto, gstate_low)
        g_state = onto_w[:, sl] * mm(b, gstate_low)
        sum_last = sum_last + head_sums(
            fold(gstate[:, sl] * (through_w[:, sl] * before.astype(f32))), spread_p
        )
        gstate[:, sl] = through_w[:, sl] * gstate[:, sl] + mm_tn(c, gy_into)
        gy_halves = halves(gy)
        gmix = mm_nt(gy_halves, xd_low)
        mixes = []
        for i, h in enumerate((2 * pair, 2 * pair + 1)):
            decay = jnp.exp(cum[:, h : h + 1] - cum_t[h : h + 1, :] + bias)
            mixes.append((decay * cross).astype(bf16))
            gcross = gcross + decay * gmix[i * n : (i + 1) * n]
        g_inside = mm_tn(jnp.concatenate(mixes, axis=0), gy_halves)
        gxd = g_inside + g_state
        xd_r, gy_r = xd_low.astype(f32), gy_low.astype(f32)
        sum_q = sum_q + head_sums(gy_r * inner - xd_r * gxd, spread_p)
        sum_state = sum_state + head_sums(xd_r * g_state, spread_p)
        sum_dt = sum_dt + head_sums(xs * gxd, spread_p)
        sum_skip = sum_skip + head_sums(fold(gy * xs), spread_p)
        gxs = dt_w[:, sl] * gxd + skip * gy
        gconv = gxs * (sig * (1.0 + conv * (1.0 - sig)))
        ext = jnp.concatenate([gconv, head_x[:, sl]], axis=0)
        gu = taps[3:4] * gconv
        for k in (1, 2, 3):
            gu = gu + taps[3 - k : 4 - k] * jnp.where(ahead[k], ext[k : k + n], 0.0)
        gx_ref[:, sl] = gu.astype(bf16)
        for k in range(4):
            row = 8 * (3 - k)
            gtapx_ref[row : row + 8, sl] += fold(gconv * shifts[k])
        gtapx_ref[32:40, sl] += fold(gconv)
        head_x[:, sl] = gconv[0:8]
    gcross_low = gcross.astype(bf16)
    gc = gc + mm(gcross_low, b)
    gb = gb + mm_tn(gcross_low, c)
    gconv = jnp.concatenate([gb, gc], axis=1) * (sig_bc * (1.0 + conv_bc * (1.0 - sig_bc)))
    ext = jnp.concatenate([gconv, head_bc[...]], axis=0)
    taps = tapbc_ref[...]
    gu = taps[3:4] * gconv
    for k in (1, 2, 3):
        gu = gu + taps[3 - k : 4 - k] * jnp.where(wide(ahead[k]), ext[k : k + n], 0.0)
    gbc_ref[...] = gu
    for k in range(4):
        row = 8 * (3 - k)
        gtapbc_ref[row : row + 8, :] += fold(gconv * shifts_bc[k])
    gtapbc_ref[32:40, :] += fold(gconv)
    head_bc[...] = gconv[0:8]
    head_seg[...] = seg[0:8]
    rows = lax.broadcasted_iota(jnp.int32, (n, n), 0)
    cols = lax.broadcasted_iota(jnp.int32, (n, n), 1)
    after = jnp.dot(
        (cols >= rows).astype(f32), sum_q, precision=lax.Precision.HIGHEST, preferred_element_type=f32
    )
    edge = jnp.sum(sum_state, axis=0, keepdims=True) + jnp.sum(sum_last, axis=0, keepdims=True)
    glog = after + edge
    gdt = sum_dt + a * glog
    gst = gdt * sigmoid(v)
    gst_ref[...] = gst.astype(bf16)
    gpar_ref[0:8] += fold(gst)
    gpar_ref[8:16] += fold(a * dt * glog)
    gpar_ref[16:24] += sum_skip


def scan_backward(x, bc, st, seg, gy, y, h, tapx, tapbc, par, spread, skip, nseq):
    tokens, width = x.shape
    n = BLOCK
    blocks = tokens // nseq // n
    at = lambda s, i: (s * blocks + blocks - 1 - i, 0)
    tail = lambda s, i: (jnp.maximum((s * blocks + blocks - 1 - i) * (n // 8) - 1, 0), 0)
    whole = lambda s, i: (0, 0)
    states = LANES
    return pl.pallas_call(
        functools.partial(scan_bwd_kernel, blocks),
        grid=(nseq, blocks),
        in_specs=[
            pl.BlockSpec((n, width), at),
            pl.BlockSpec((8, width), tail),
            pl.BlockSpec((n, 2 * states), at),
            pl.BlockSpec((8, 2 * states), tail),
            pl.BlockSpec((n, LANES), at),
            pl.BlockSpec((n, LANES), at),
            pl.BlockSpec((8, LANES), tail),
            pl.BlockSpec((n, width), at),
            pl.BlockSpec((n, width), at),
            pl.BlockSpec((states, width), at),
            pl.BlockSpec(tapx.shape, whole),
            pl.BlockSpec(tapbc.shape, whole),
            pl.BlockSpec(par.shape, whole),
            pl.BlockSpec(spread.shape, whole),
            pl.BlockSpec(skip.shape, whole),
        ],
        out_specs=[
            pl.BlockSpec((n, width), at),
            pl.BlockSpec((n, 2 * states), at),
            pl.BlockSpec((n, LANES), at),
            pl.BlockSpec((40, width), whole),
            pl.BlockSpec((40, 2 * states), whole),
            pl.BlockSpec((24, LANES), whole),
        ],
        out_shape=[
            jax.ShapeDtypeStruct((tokens, width), bf16),
            jax.ShapeDtypeStruct((tokens, 2 * states), f32),
            jax.ShapeDtypeStruct((tokens, LANES), bf16),
            jax.ShapeDtypeStruct((40, width), f32),
            jax.ShapeDtypeStruct((40, 2 * states), f32),
            jax.ShapeDtypeStruct((24, LANES), f32),
        ],
        scratch_shapes=[
            pltpu.VMEM((states, width), f32),
            pltpu.VMEM((8, width), f32),
            pltpu.VMEM((8, 2 * states), f32),
            pltpu.VMEM((8, LANES), jnp.int32),
        ],
        compiler_params=pltpu.CompilerParams(vmem_limit_bytes=VMEM_BYTES),
        cost_estimate=pl.CostEstimate(
            flops=tokens * width * 3000, bytes_accessed=tokens * width * 20, transcendentals=0
        ),
        name="scan_backward",
    )(x, x, bc, bc, st, seg, seg, gy, y, h, tapx, tapbc, par, spread, skip)


def spread_matrix(heads):
    row = lax.broadcasted_iota(jnp.int32, (LANES, heads * WIDTH), 0)
    col = lax.broadcasted_iota(jnp.int32, (LANES, heads * WIDTH), 1)
    return (row % (LANES // 2) == col // WIDTH).astype(bf16)


def on_lanes(v):
    half = jnp.pad(v, [(0, 0)] * (v.ndim - 1) + [(0, LANES // 2 - v.shape[-1])])
    return jnp.concatenate([half, half], axis=-1)


epsilon = 1e-05


def placed_at(whole, piece, offset):
    start = (0,) * (len(whole) - 1) + (offset,)
    return lax.dynamic_update_slice(jnp.zeros(whole, piece.dtype), piece, start)


def per_device(
    residual, segment_ids, norm_gain, inner_weight, state_weight, step_weight, conv_weight,
    conv_bias, step_bias, decay_log, skip_gain, gated_gain, out_weight, cotangent,
):
    rank = lax.axis_index("tensor")
    model_width = residual.shape[1]
    width = inner_weight.shape[2]
    heads = step_weight.shape[1]
    inner_width = gated_gain.shape[0]
    nseq, length = segment_ids.shape
    tokens = nseq * length
    inner_start, head_start = rank * width, rank * heads
    stream = residual.astype(f32)
    scaling = lax.rsqrt(jnp.mean(stream * stream, axis=1, keepdims=True) + epsilon)
    normed = (stream * scaling * norm_gain).astype(bf16)
    normed_all = lax.all_gather(normed, "tensor", axis=0, tiled=True)
    wx = lax.all_gather(
        jnp.concatenate([inner_weight[:, 1], on_lanes(step_weight)], axis=1), "dp", axis=0, tiled=True
    )
    wz = lax.all_gather(inner_weight[:, 0], "dp", axis=0, tiled=True)
    wo = lax.all_gather(out_weight, "dp", axis=1, tiled=True)
    cot_all = lax.all_gather(cotangent, "tensor", axis=0, tiled=True)
    taps = jnp.concatenate([conv_weight, conv_bias[None], jnp.zeros((3, conv_bias.shape[0]), f32)], axis=0)
    tapx = lax.dynamic_slice_in_dim(taps, inner_start, width, 1)
    tapbc = taps[:, inner_width:]
    local = lambda v: lax.dynamic_slice_in_dim(v, head_start, heads, 0)
    rates = -jnp.exp(local(decay_log))
    par = jnp.concatenate(
        [on_lanes(local(step_bias)[None]), on_lanes(rates[None]), jnp.zeros((6, LANES), f32)], axis=0
    )
    skip = jnp.broadcast_to(jnp.repeat(local(skip_gain), WIDTH)[None], (8, width))
    gain = lax.dynamic_slice_in_dim(gated_gain, inner_start, width, 0)
    spread = spread_matrix(heads)
    seg = jnp.broadcast_to(segment_ids.reshape(tokens, 1), (tokens, LANES))

    xst = mm(normed_all, wx)
    bc = mm(normed_all, state_weight)
    x, st = xst[:, :width], xst[:, width:]
    y, h = scan_forward(x, bc, st, seg, tapx, tapbc, par, spread, skip, nseq)
    z = mm(normed_all, wz)
    sig = jax.nn.sigmoid(z)
    silu = z * sig
    gated = y * silu
    gng = mm_nt(cot_all, wo)
    sums = lax.psum(
        jnp.stack([jnp.sum(gated * gated, axis=1), jnp.sum(gng * gain * gated, axis=1)]), "tensor"
    )
    scale_g = lax.rsqrt(sums[0] / inner_width + epsilon)[:, None]
    normed_g = (gated * scale_g * gain).astype(bf16)
    grad_gated = scale_g * gain * gng - gated * (scale_g**3 * sums[1][:, None] / inner_width)
    gain_grad = jnp.sum(gng * gated * scale_g, axis=0)
    gz = (grad_gated * y * (sig * (1.0 + z * (1.0 - sig)))).astype(bf16)
    gy = grad_gated * silu
    scatter = lambda v, axis, dim: lax.psum_scatter(
        v.astype(bf16), axis, scatter_dimension=dim, tiled=True
    ).astype(f32)
    block_out = stream + scatter(mm(normed_g, wo), "tensor", 0)
    out_grad = scatter(mm_tn(normed_g, cot_all), "dp", 1)
    z_grad = scatter(mm_tn(normed_all, gz), "dp", 0)
    gx, gbc, gst, gtapx, gtapbc, gpar = scan_backward(
        x, bc, st, seg, gy, y, h, tapx, tapbc, par, spread, skip, nseq
    )
    gbc = gbc.astype(bf16)
    gxs = jnp.concatenate([gx, gst * (lax.broadcasted_iota(jnp.int32, (1, LANES), 1) < LANES // 2)], axis=1)
    total = mm_nt(gz, wz) + mm_nt(gxs, wx) + mm_nt(gbc, state_weight)
    grad_normed = scatter(total, "tensor", 0)
    x_grad = scatter(mm_tn(normed_all, gxs), "dp", 0)
    state_grad = scatter(mm_tn(normed_all, gbc), ("dp", "tensor"), 0)
    state_grad = lax.all_gather(state_grad, ("dp", "tensor"), axis=0, tiled=True)
    gtapx = gtapx.reshape(5, 8, -1).sum(1)
    gtapbc = gtapbc.reshape(5, 8, -1).sum(1)
    gpar = gpar.reshape(3, 8, -1).sum(1)[:, :heads]
    gtaps = jnp.concatenate(
        [placed_at((5, inner_width), gtapx, inner_start), gtapbc], axis=1
    )
    gpars = placed_at((3, step_bias.shape[0]), gpar, head_start)
    ggain = placed_at((1, inner_width), gain_grad[None], inner_start)
    gtaps, gpars, ggain = lax.psum((gtaps, gpars, ggain), ("dp", "tensor"))
    norm_grad = lax.psum(jnp.sum(grad_normed * stream * scaling, axis=0), ("dp", "tensor"))
    along = jnp.sum(grad_normed * norm_gain * stream, axis=1, keepdims=True)
    residual_grad = (
        cotangent.astype(f32)
        + scaling * norm_gain * grad_normed
        - stream * (scaling**3 * along / model_width)
    )
    inner_grad = jnp.stack([z_grad, x_grad[:, :width]], axis=1)
    return (
        block_out, residual_grad, norm_grad, inner_grad, state_grad,
        x_grad[:, width : width + heads], gtaps[:4], gtaps[4], gpars[0], gpars[1], gpars[2],
        ggain[0], out_grad,
    )


def solution(mesh):
    rows, both = P("dp", "tensor"), P(("dp", "tensor"), None)
    inner, out = P("dp", None, "tensor"), P("tensor", "dp")
    return jax.shard_map(
        per_device,
        mesh=mesh,
        in_specs=(
            both, P("dp", None), P(), inner, P(), rows, P(), P(), P(), P(), P(), P(), out, both,
        ),
        out_specs=(both, both, P(), inner, P(), rows, P(), P(), P(), P(), P(), P(), out),
        check_vma=False,
    )
```

time: 1030 us -> 960 us (0.932)
  waiting for transfers between devices: 479 us -> 677 us
  local copies, waits for them, and re-layouts: 138 us -> 24.4 us
  matrix products: 201 us -> 97.8 us
  other arithmetic: 120 us -> 28.3 us
  Pallas kernels: 0 us -> 58.8 us
  blocking collectives: 74.3 us -> 51.7 us
    reduce_scatter x4 -> x6, waiting for transfers between devices: 115 us -> 348 us  [per_device(): lax.psum_scatter(v.astype(bf16), axis, scatter_dimension=dim, tiled=True)]
    all_gather x4 -> x6, waiting for transfers between devices: 101 us -> 267 us  [the longest x1 59.5 us: per_device(): lax.all_gather(state_grad, ('dp', 'tensor'), axis=0, tiled=True)]
    unnamed x11 -> x13, waiting for transfers between devices: 126 us -> 1.24 us
    dot_general x24 -> x12, matrix products: 201 us -> 97.8 us  [the longest x4 33.4 us: mm(): return jnp.dot(a, b, preferred_element_type=f32)]
    psum x1, waiting for transfers between devices: 137 us -> 60.2 us  [per_device(): gtaps, gpars, ggain = lax.psum((gtaps, gpars, ggain), ('dp', 'tensor'))]
    pallas_call x0 -> x2, Pallas kernels: none -> 58.8 us  [the longest x1 44.2 us: scan_backward(): pl.pallas_call(functools.partial(scan_bwd_kernel, blocks), grid=(nseq, bl...]
    reshape x12 -> x0, local copies, waits for them, and re-layouts: 43.9 us -> none  [the longest x4 27.1 us: scan_sequence(): return (inside + outside).reshape(length, head_count, head_width)]
    reduce_sum x12 -> x4, other arithmetic: 37.4 us -> 1.95 us  [the longest x1 1.87 us: per_device(): jnp.sum(grad_normed * stream * scaling, axis=0)]
  transfers between devices with their start and end apart: 10 -> 13, of which waited for: 7 -> 13; matrix products, arithmetic and copies ran while one was open for 24% -> 11% of each run, Pallas kernels for 0% -> 2%
where the time goes in v1:
time: 960 us; the launch traced here: 954 us
  waiting for transfers between devices  677 us (71%)
  matrix products  97.8 us (10%)
  Pallas kernels  58.8 us (6%)
  blocking collectives  51.7 us (5%)
  other arithmetic  28.3 us (3%)
  local copies, waits for them, and re-layouts  24.4 us (3%)
  between operations  14.5 us (2%)
    reduce_scatter x6, waiting for transfers between devices, per_device(): lax.psum_scatter(v.astype(bf16), axis, scatter_dimension=dim, tiled=True)  348 us
    psum x1, waiting for transfers between devices, per_device(): gtaps, gpars, ggain = lax.psum((gtaps, gpars, ggain), ('dp', 'tensor'))  60.2 us
    all_gather x1, waiting for transfers between devices, per_device(): lax.all_gather(state_grad, ('dp', 'tensor'), axis=0, tiled=True)  59.5 us
    all_gather x1, waiting for transfers between devices, per_device(): wo = lax.all_gather(out_weight, 'dp', axis=1, tiled=True)  49.3 us
    all_gather x1, waiting for transfers between devices, per_device(): normed_all = lax.all_gather(normed, 'tensor', axis=0, tiled=True)  46.3 us
    all_gather x1, waiting for transfers between devices, per_device(): wz = lax.all_gather(inner_weight[:, 0], 'dp', axis=0, tiled=True)  44.9 us
    pallas_call x1, Pallas kernels, scan_backward(): pl.pallas_call(functools.partial(scan_bwd_kernel, blocks), grid=(nseq, bl...  44.2 us
    all_gather x1, waiting for transfers between devices, per_device(): lax.all_gather(jnp.concatenate([inner_weight[:, 1], on_lanes(step_weight)...  42.7 us
  transfers between devices with their start and end apart: 13, of which 13 were waited for; matrix products, arithmetic and copies ran while one was open for 11% of the time, Pallas kernels for 2%

profile of v1, /device:TPU:0, one launch (start us, length us, event | category | flops | bytes accessed | tf_op | source)
XLA Modules:
  0.0 953.8 jit_solution(13685300620007184537)
XLA Ops:
  20.7 46.3 %all-gather.8.cloned.1.call-done = bf16[1024,2048]{1,0:T(8,128)(2,1)} async-done(((bf16[256,2048]{1,0:T(8,128)(2,1)}), bf16[1024,2048]{1,0:T(8,128)(2,1)}) %all-gather.8.cloned.1.call-update) | async-done | bytes 4194320 | tf_op jit(solution)/shard_map/all_gather | solution.py:422
  71.4 44.9 %all-gather.18.cloned.1.call-done = bf16[2048,1,1024]{2,0,1:T(8,128)(2,1)} async-done(((bf16[256,1,1024]{2,0,1:T(8,128)(2,1)}), bf16[2048,1,1024]{2,0,1:T(8,128)(2,1)}) %all-gather.18.cloned.1.call-update) | async-done | bytes 4194320 | tf_op jit(solution)/shard_map/all_gather | solution.py:426
  116.4 10.0 %fusion.2 = f32[1024,1024]{1,0:T(8,128)} fusion(bf16[1024,2048]{1,0:T(8,128)(2,1)} %all-gather.8.cloned.1.call-done, bf16[2048,1,1024]{2,0,1:T(8,128)(2,1)} %all-gather.18.cloned.1.call-done), kind=kOutput, calls=%fused_computation.10 | convolution fusion | flops 4294967296 | bytes 12582912 | tf_op jit(solution)/shard_map/dot_general | solution.py:19
  126.4 42.7 %all-gather.10.cloned.1.call-done = bf16[2048,1152]{1,0:T(8,128)(2,1)} async-done(((bf16[256,1152]{1,0:T(8,128)(2,1)}), bf16[2048,1152]{1,0:T(8,128)(2,1)}) %all-gather.10.cloned.1.call-update) | async-done | bytes 4718608 | tf_op jit(solution)/shard_map/all_gather | solution.py:423
  169.0 8.9 fusion.33
  183.0 14.6 %scan_forward.1 = (f32[1024,1024]{1,0:T(8,128)}, bf16[1024,1024]{1,0:T(8,128)(2,1)}) custom-call(f32[1024,1024]{1,0:T(8,128)} %slice.60.x_ref.xt_ref, f32[1024,256]{1,0:T(8,128)} %fusion.34.bc_ref.bct_ref, f32[1024,128]{1,0:T(8,128)} %slice.61.st_ref, s32[1024,128]{1,0:T(8,128)} %broadcast_in_dim.54.seg_ref.segt_ref, ...), custom_call_target="tpu_custom_call" | custom-call | flops 1048576000 | bytes 12582912 | tf_op jit(solution)/shard_map/scan_forward/pallas_call | solution.py:147
  197.7 24.6 %all-gather.12.cloned.1.call-done = bf16[1024,2048]{1,0:T(8,128)(2,1)} async-done(((bf16[256,2048]{1,0:T(8,128)(2,1)}), bf16[1024,2048]{1,0:T(8,128)(2,1)}) %all-gather.12.cloned.1.call-update) | async-done | bytes 4194320 | tf_op jit(solution)/shard_map/all_gather | solution.py:428
  222.3 49.3 %all-gather.14.cloned.1.call-done = bf16[1024,2048]{1,0:T(8,128)(2,1)} async-done(((bf16[1024,256]{1,0:T(8,128)(2,1)}), bf16[1024,2048]{1,0:T(8,128)(2,1)}) %all-gather.14.cloned.1.call-update) | async-done | bytes 4194320 | tf_op jit(solution)/shard_map/all_gather | solution.py:427
  271.6 13.9 %multiply_reduce_fusion.2 = (f32[1024]{0:T(1024)S(1)}, f32[1024]{0:T(1024)S(1)}, f32[1024,1024]{1,0:T(8,128)}, f32[1024,1024]{1,0:T(8,128)}) fusion(f32[1024]{0:T(1024)S(1)} %dynamic_slice.19, f32[1024,1024]{1,0:T(8,128)} %get-tuple-element.21.y_ref, f32[1024,1024]{1,0:T(8,128)} %fusion.2, bf16[1024,2048]{1,0:T(8,128)(2,1)} %all-gather.12.cloned.1.call-done, ...), kind=kOutput, calls=%fused_computation.17 | convolution fusion | flops 4305451008 | bytes 25178112 | tf_op jit(solution)/shard_map/dot_general | solution.py:27
  285.5 10.0 %psum.35 = f32[2,1024]{1,0:T(2,128)S(1)} all-reduce(f32[2,1024]{1,0:T(2,128)S(1)} %pad_maximum_fusion.5), channel_id=1, replica_groups=mesh['dp'=8,'tensor'=4] {'tensor'}, use_global_device_ids=true, to_apply=%region_3.4 | all-reduce | flops 2048 | bytes 16384 | tf_op jit(solution)/shard_map/psum | solution.py:451
  295.5 8.9 fusion.13
  304.4 44.2 %scan_backward.1 = (bf16[1024,1024]{1,0:T(8,128)(2,1)}, f32[1024,256]{1,0:T(8,128)}, bf16[1024,128]{1,0:T(8,128)(2,1)}, f32[40,1024]{1,0:T(8,128)}, f32[40,256]{1,0:T(8,128)}, /*index=5*/f32[24,128]{1,0:T(8,128)}) custom-call(f32[1024,1024]{1,0:T(8,128)} %slice.60.x_ref.xt_ref, f32[1024,1024]{1,0:T(8,128)} %slice.60.x_ref.xt_ref, ...), custom_call_target="tpu_custom_call" | custom-call | flops 3145728000 | bytes 20971520 | tf_op jit(solution)/shard_map/scan_backward/pallas_call | solution.py:338
  353.2 130.8 %reduce-scatter.15.cloned.1.call-done = bf16[64,256]{1,0:T(8,128)(2,1)} async-done(((bf16[2048,256]{1,0:T(8,128)(2,1)}), bf16[64,256]{1,0:T(8,128)(2,1)}) %reduce-scatter.15.cloned.1.call-update) | async-done | bytes 32784 | tf_op jit(solution)/shard_map/reduce_scatter | solution.py:460
  485.9 10.3 %convolution_convert_fusion.1 = bf16[1024,2048]{1,0:T(8,128)(2,1)} fusion(bf16[1024,2048]{1,0:T(8,128)(2,1)} %all-gather.12.cloned.1.call-done, f32[1024,1024]{1,0:T(8,128)} %get-tuple-element.62, f32[1024]{0:T(1024)S(1)} %bitcast.54, f32[1024]{0:T(1024)S(1)} %dynamic_slice.19), kind=kOutput, calls=%fused_computation.20 | convolution fusion | flops 4300210176 | bytes 12591104 | tf_op jit(solution)/shard_map/dot_general | solution.py:23
  523.5 10.1 %convolution_convert_fusion.3 = bf16[1024,2048]{1,0:T(8,128)(2,1)} fusion(bf16[1024,2048]{1,0:T(8,128)(2,1)} %all-gather.14.cloned.1.call-done, f32[1024,1024]{1,0:T(8,128)} %get-tuple-element.62, f32[1024]{0:T(1024)S(1)} %bitcast.55, f32[1024]{0:T(1024)S(1)} %dynamic_slice.19), kind=kOutput, calls=%fused_computation.22 | convolution fusion | flops 4300210176 | bytes 12591104 | tf_op jit(solution)/shard_map/dot_general | solution.py:19
  535.3 10.7 %convolution_convert_fusion = bf16[2048,1152]{1,0:T(8,128)(2,1)} fusion(bf16[1024,2048]{1,0:T(8,128)(2,1)} %all-gather.8.cloned.1.call-done, bf16[1024,128]{1,0:T(8,128)(2,1)S(1)} %copy-done.7, bf16[1024,1024]{1,0:T(8,128)(2,1)S(1)} %copy-done.20), kind=kOutput, calls=%fused_computation.1 | convolution fusion | flops 4838916096 | bytes 11272192 | tf_op jit(solution)/shard_map/dot_general | solution.py:23
  547.2 60.2 %all-reduce.6.cloned.1.call-done = f32[5,4352]{1,0:T(8,128)} async-done(((f32[5,4352]{1,0:T(8,128)}), f32[5,4352]{1,0:T(8,128)}) %all-reduce.6.cloned.1.call-update) | async-done | bytes 87056 | tf_op jit(solution)/shard_map/psum | solution.py:484
  610.5 59.5 %all-gather.16.cloned.1.call-done = f32[2048,256]{1,0:T(8,128)} async-done(((f32[64,256]{1,0:T(8,128)}), f32[2048,256]{1,0:T(8,128)}) %all-gather.16.cloned.1.call-update) | async-done | bytes 2097168 | tf_op jit(solution)/shard_map/all_gather | solution.py:475
  670.0 51.3 %reduce-scatter.17.cloned.1.call-done = bf16[1024,256]{1,0:T(8,128)(2,1)} async-done(((bf16[1024,2048]{1,0:T(8,128)(2,1)}), bf16[1024,256]{1,0:T(8,128)(2,1)}) %reduce-scatter.17.cloned.1.call-update) | async-done | bytes 524304 | tf_op jit(solution)/shard_map/reduce_scatter | solution.py:460
  723.4 51.9 %reduce-scatter.9.cloned.1.call-done = bf16[256,2048]{1,0:T(8,128)(2,1)} async-done(((bf16[1024,2048]{1,0:T(8,128)(2,1)}), bf16[256,2048]{1,0:T(8,128)(2,1)}) %reduce-scatter.9.cloned.1.call-update) | async-done | bytes 1048592 | tf_op jit(solution)/shard_map/reduce_scatter | solution.py:460
  777.1 41.7 %all-reduce.3 = (f32[2048]{0:T(1024)}, f32[3,64]{1,0:T(4,128)S(1)}, f32[4096]{0:T(1024)}) all-reduce(f32[2048]{0:T(1024)S(1)} %get-tuple-element.57, f32[3,64]{1,0:T(4,128)S(1)} %dynamic_update_slice.10, f32[4096]{0:T(1024)S(1)} %dynamic_update_slice.12), channel_id=1, replica_groups=mesh['dp'=8,'tensor'=4] {'dp','tensor'}, use_global_device_ids=true, to_apply=%region_8.9 | all-reduce | flops 6336 | bytes 50688 | tf_op jit(solution)/shard_map/psum | solution.py:485
  819.3 9.3 reduce-scatter.11.cloned.1.call-done
  829.8 52.5 %reduce-scatter.7.cloned.1.call-done = bf16[256,2048]{1,0:T(8,128)(2,1)} async-done(((bf16[1024,2048]{1,0:T(8,128)(2,1)}), bf16[256,2048]{1,0:T(8,128)(2,1)}) %reduce-scatter.7.cloned.1.call-update) | async-done | bytes 1048592 | tf_op jit(solution)/shard_map/reduce_scatter | solution.py:460
  887.2 52.5 %reduce-scatter.13.cloned.1.call-done = bf16[256,1152]{1,0:T(8,128)(2,1)} async-done(((bf16[2048,1152]{1,0:T(8,128)(2,1)}), bf16[256,1152]{1,0:T(8,128)(2,1)}) %reduce-scatter.13.cloned.1.call-update) | async-done | bytes 589840 | tf_op jit(solution)/shard_map/reduce_scatter | solution.py:460
  (141 shorter events, 80.1 us)
Async XLA Ops:
  7.2 59.8 %copy-start = (bf16[2048,256]{1,0:T(8,128)(2,1)S(1)}, bf16[2048,256]{1,0:T(8,128)(2,1)}, u32[]{:S(2)}) copy-start(bf16[2048,256]{1,0:T(8,128)(2,1)} %param.18) | copy-start | bytes 3145732
  7.2 4.3 copy-start.2
  7.2 59.8 %all-gather.8.cloned.1.call-start = ((), (), s32[]{:S(2)}) async-start(), calls=%async_computation.6 | async-start | bytes 5242880 | tf_op jit(solution)/shard_map/all_gather | solution.py:422
  11.5 104.9 %all-gather.18.cloned.1.call-start = ((), (), s32[]{:S(2)}) async-start(), calls=%async_computation.18 | async-start | bytes 4718592 | tf_op jit(solution)/shard_map/all_gather | solution.py:426
  13.1 4.1 copy-start.10
  14.1 155.0 %all-gather.10.cloned.1.call-start = ((), (), s32[]{:S(2)}) async-start(), calls=%async_computation.7 | async-start | bytes 5308416 | tf_op jit(solution)/shard_map/all_gather | solution.py:423
  15.4 206.8 %all-gather.12.cloned.1.call-start = ((), (), s32[]{:S(2)}) async-start(), calls=%async_computation.8 | async-start | bytes 5242880 | tf_op jit(solution)/shard_map/all_gather | solution.py:428
  16.0 255.5 %all-gather.14.cloned.1.call-start = ((), (), s32[]{:S(2)}) async-start(), calls=%async_computation.9 | async-start | bytes 4718592 | tf_op jit(solution)/shard_map/all_gather | solution.py:427
  16.6 467.4 %reduce-scatter.15.cloned.1.call-start = ((), (), s32[]{:S(2)}) async-start(), calls=%async_computation.14 | async-start | bytes 1081344 | tf_op jit(solution)/shard_map/reduce_scatter | solution.py:460
  177.9 4.1 copy-start.15
  304.4 44.2 %copy-start.18 = (bf16[1024,2048]{1,0:T(8,128)(2,1)S(1)}, bf16[1024,2048]{1,0:T(8,128)(2,1)}, u32[]{:S(2)}) copy-start(bf16[1024,2048]{1,0:T(8,128)(2,1)} %all-gather.8.cloned.1.call-done) | copy-start | bytes 12582916
  352.3 255.0 %all-reduce.6.cloned.1.call-start = ((), (), s32[]{:S(2)}) async-start(), calls=%async_computation.16 | async-start | bytes 278528 | tf_op jit(solution)/shard_map/psum | solution.py:484
  353.2 316.8 %all-gather.16.cloned.1.call-start = ((), (), s32[]{:S(2)}) async-start(), calls=%async_computation.15 | async-start | bytes 2162688 | tf_op jit(solution)/shard_map/all_gather | solution.py:475
  485.5 235.8 %reduce-scatter.17.cloned.1.call-start = ((), (), s32[]{:S(2)}) async-start(), calls=%async_computation.17 | async-start | bytes 4718592 | tf_op jit(solution)/shard_map/reduce_scatter | solution.py:460
  496.2 279.0 %reduce-scatter.9.cloned.1.call-start = ((), (), s32[]{:S(2)}) async-start(), calls=%async_computation.11 | async-start | bytes 5242880 | tf_op jit(solution)/shard_map/reduce_scatter | solution.py:460
  497.2 6.6 copy-start.6
  497.2 6.6 copy-start.19
  503.8 7.6 copy-start.4
  514.8 313.9 %reduce-scatter.11.cloned.1.call-start = ((), (), s32[]{:S(2)}) async-start(), calls=%async_computation.12 | async-start | bytes 4718592 | tf_op jit(solution)/shard_map/reduce_scatter | solution.py:460
  523.3 359.0 %reduce-scatter.7.cloned.1.call-start = ((), (), s32[]{:S(2)}) async-start(), calls=%async_computation.10 | async-start | bytes 5242880 | tf_op jit(solution)/shard_map/reduce_scatter | solution.py:460
  533.6 406.1 %reduce-scatter.13.cloned.1.call-start = ((), (), s32[]{:S(2)}) async-start(), calls=%async_computation.13 | async-start | bytes 5308416 | tf_op jit(solution)/shard_map/reduce_scatter | solution.py:460
  546.0 229.3 %copy-start.1 = (bf16[256,2048]{1,0:T(8,128)(2,1)S(1)}, bf16[256,2048]{1,0:T(8,128)(2,1)}, u32[]{:S(2)}) copy-start(bf16[256,2048]{1,0:T(8,128)(2,1)} %param.14) | copy-start | bytes 3145732
  546.0 229.3 %copy-start.9 = (f32[2048]{0:T(1024)S(1)}, f32[2048]{0:T(1024)}, u32[]{:S(2)}) copy-start(f32[2048]{0:T(1024)} %param.16) | copy-start | bytes 24580
  941.2 4.5 copy-start.3
  (11 other events, 29.5 us)
Sparse Core Ops, SparseCore 0:
  11.6 55.3 all-gather.7
  69.2 47.1 all-gather.17
  118.6 50.4 all-gather.9
  170.7 51.5 all-gather.11
  223.7 47.7 all-gather.13
  352.4 131.5 reduce-scatter.14
  491.1 116.2 all-reduce.5
  611.2 58.7 all-gather.15
  672.4 48.8 reduce-scatter.16
  724.4 50.8 reduce-scatter.8
  777.5 51.0 reduce-scatter.10
  831.4 50.8 reduce-scatter.6
  884.7 54.9 reduce-scatter.12

commit v2 on v1

--- a/solution.py
+++ b/solution.py
@@ -396,12 +396,721 @@
     return jnp.concatenate([half, half], axis=-1)
 
 
+MESH = pl.DeviceIdType.MESH
+
+
+def place():
+    dp, rank = lax.axis_index("dp"), lax.axis_index("tensor")
+    return dp // 2, dp % 2, rank
+
+
+def remote(src, dst, send, recv, dp, rank):
+    return pltpu.make_async_remote_copy(
+        src_ref=src, dst_ref=dst, send_sem=send, recv_sem=recv, device_id=(dp, rank),
+        device_id_type=MESH,
+    )
+
+
+def greet(chips, ranks, line=True, tensor=True):
+    chip, core, rank = place()
+    sem = pltpu.get_barrier_semaphore()
+    me = chip * 2 + core
+
+    def signal(dp, r):
+        pl.semaphore_signal(sem, inc=1, device_id=(dp, r), device_id_type=MESH)
+
+    if line:
+        signal(chip * 2 + 1 - core, rank)
+        for step in (1, -1):
+            @pl.when((chip + step >= 0) & (chip + step < chips))
+            def _():
+                signal(me + 2 * step, rank)
+    if tensor:
+        for k in range(1, ranks):
+            signal(me, lax.rem(rank + k, ranks))
+    count = ranks - 1 if tensor else 0
+    if line:
+        count = count + 1 + (chip + chips - 1) // chips + (2 * chips - 2 - chip) // chips
+    pl.semaphore_wait(sem, count)
+
+
+class LineGather:
+    sems = 4
+
+    def __init__(self, own, slots, send, recv, local, chips):
+        self.own, self.slots, self.send, self.recv, self.local = own, slots, send, recv, local
+        self.chips = chips
+        self.chip, self.core, self.rank = place()
+        self.me = self.chip * 2 + self.core
+        self.partner = self.chip * 2 + 1 - self.core
+        self.steps = chips
+
+    @staticmethod
+    def scratch(chips):
+        n = 2 * chips
+        return [
+            pltpu.SemaphoreType.DMA((3, n)), pltpu.SemaphoreType.DMA((n,)), pltpu.SemaphoreType.DMA,
+        ]
+
+    def copy(self, way, origin, src=None):
+        target = (self.me + 2, self.me - 2, self.partner)[way]
+        slot = self.slots.at[origin]
+        return remote(
+            slot if src is None else src, slot, self.send.at[way, origin], self.recv.at[origin],
+            target, self.rank,
+        )
+
+    def pass_on(self, way, origin, src=None, wait=False):
+        def go():
+            copy = self.copy(way, origin, src)
+            copy.wait_send() if wait else copy.start()
+
+        if way == 0:
+            pl.when(self.chip + 1 < self.chips)(go)
+        elif way == 1:
+            pl.when(self.chip > 0)(go)
+        else:
+            go()
+
+    def step(self, k):
+        if k == 0:
+            for way in (0, 1, 2):
+                self.pass_on(way, self.me, self.own)
+            pltpu.make_async_copy(self.own, self.slots.at[self.me], self.local).start()
+            return
+        for way, origin, there in (
+            (0, self.me - 2 * k, self.chip - k >= 0),
+            (1, self.me + 2 * k, self.chip + k < self.chips),
+        ):
+            @pl.when(there)
+            def _():
+                self.copy(2, origin).wait_recv()
+                self.pass_on(way, origin)
+                self.pass_on(2, origin)
+
+    def finish(self):
+        pltpu.make_async_copy(self.own, self.slots.at[self.me], self.local).wait()
+        for way in (0, 1, 2):
+            self.pass_on(way, self.me, self.own, wait=True)
+        self.copy(2, self.partner).wait_recv()
+        for k in range(1, self.chips):
+            for way, there, shift in ((0, self.chip - k >= 0, -k), (1, self.chip + k < self.chips, k)):
+                @pl.when(there)
+                def _():
+                    origin = self.me + 2 * shift
+                    self.pass_on(way, origin, wait=True)
+                    self.pass_on(2, origin, wait=True)
+                    self.copy(2, self.partner + 2 * shift).wait_recv()
+
+
+class TensorGather:
+    def __init__(self, own, slots, send, recv, local, ranks):
+        self.own, self.slots, self.send, self.recv, self.local = own, slots, send, recv, local
+        self.ranks = ranks
+        chip, core, self.rank = place()
+        self.me = chip * 2 + core
+        self.rows = own.shape[0] // 2
+        self.steps = 2
+
+    @staticmethod
+    def scratch(ranks):
+        return [
+            pltpu.SemaphoreType.DMA((ranks,)), pltpu.SemaphoreType.DMA((ranks,)), pltpu.SemaphoreType.DMA,
+        ]
+
+    def near(self, k, src=None):
+        x = self.rank % 2
+        y = self.rank // 2
+        across = (y * 2 + 1 - x, (1 - y) * 2 + x)
+        if k < 2:
+            return remote(
+                self.own if src is None else src, self.slots.at[self.rank], self.send.at[k],
+                self.recv.at[k], self.me, across[k],
+            )
+        half = self.slots.at[across[k - 2], pl.ds((k - 2) * self.rows, self.rows)]
+        return remote(half, half, self.send.at[k], self.recv.at[k], self.me, across[3 - k])
+
+    def direct(self, k):
+        return remote(
+            self.own, self.slots.at[self.rank], self.send.at[k], self.recv.at[k], self.me,
+            lax.rem(self.rank + k, self.ranks),
+        )
+
+    def step(self, k):
+        if k == 0:
+            if self.ranks == 4:
+                self.near(0).start()
+                self.near(1).start()
+            else:
+                for j in range(1, self.ranks):
+                    self.direct(j).start()
+            pltpu.make_async_copy(self.own, self.slots.at[self.rank], self.local).start()
+        elif self.ranks == 4:
+            for j in (0, 1):
+                self.near(j).wait_recv()
+                self.near(2 + j).start()
+
+    def finish(self):
+        pltpu.make_async_copy(self.own, self.slots.at[self.rank], self.local).wait()
+        if self.ranks == 4:
+            for j in (0, 1):
+                self.near(j).wait_send()
+                self.near(2 + j).wait()
+        else:
+            for j in range(1, self.ranks):
+                self.direct(j).wait()
+
+
+def add_rows(target, others):
+    rows = target.shape[0]
+    slab = 32 if rows % 32 == 0 else 16
+
+    @pl.loop(0, rows // slab)
+    def _(i):
+        at = pl.ds(pl.multiple_of(i * slab, slab), slab)
+        total = target[at].astype(f32)
+        for other in others:
+            total = total + other[at].astype(f32)
+        target[at] = total.astype(target.dtype)
+
+
+class LineScatter:
+    def __init__(self, parts, out, mine, swap, up, down, send, recv, local, chips):
+        self.parts, self.out, self.mine, self.swap, self.up, self.down = parts, out, mine, swap, up, down
+        self.send, self.recv, self.local, self.chips = send, recv, local, chips
+        self.chip, self.core, self.rank = place()
+        self.me = self.chip * 2 + self.core
+        self.partner = self.chip * 2 + 1 - self.core
+        self.steps = chips
+
+    @staticmethod
+    def scratch(chips, shape):
+        return [pltpu.VMEM((chips,) + shape, bf16)] * 4 + [
+            pltpu.SemaphoreType.DMA((3, chips)), pltpu.SemaphoreType.DMA((3, chips)),
+            pltpu.SemaphoreType.DMA((chips,)),
+        ]
+
+    def order(self):
+        n = self.chips
+        return [c for k in range(n // 2) for c in (n - 1 - k, k)]
+
+    def over(self, c):
+        return remote(
+            self.parts.at[2 * c + 1 - self.core], self.swap.at[c], self.send.at[2, c],
+            self.recv.at[2, c], self.partner, self.rank,
+        )
+
+    def load(self, c):
+        return pltpu.make_async_copy(
+            self.parts.at[2 * c + self.core], self.mine.at[c], self.local.at[c]
+        )
+
+    def along(self, way, c, first=False):
+        buffer = (self.up, self.down)[way]
+        src = self.mine.at[c] if first else buffer.at[c]
+        return remote(
+            src, buffer.at[c], self.send.at[way, c], self.recv.at[way, c],
+            self.me + (2, -2)[way], self.rank,
+        )
+
+    def step(self, k):
+        n, chip = self.chips, self.chip
+        if k == 0:
+            for c in self.order():
+                self.over(c).start()
+                self.load(c).start()
+            return
+        if k == 1:
+            for c in self.order():
+                self.over(c).wait()
+                self.load(c).wait()
+                add_rows(self.mine.at[c], [self.swap.at[c]])
+
+                @pl.when((chip == 0) & (c > 0))
+                def _():
+                    self.along(0, c, True).start()
+
+                @pl.when((chip == n - 1) & (c < n - 1))
+                def _():
+                    self.along(1, c, True).start()
+            return
+        t = k - 1
+        c = n - 1 - (t - chip)
+
+        @pl.when((chip > 0) & (t >= chip) & (c > chip))
+        def _():
+            self.along(0, c).wait_recv()
+            add_rows(self.up.at[c], [self.mine.at[c]])
+            self.along(0, c).start()
+
+        d = t - (n - 1 - chip)
+
+        @pl.when((chip < n - 1) & (d >= 0) & (d < chip))
+        def _():
+            self.along(1, d).wait_recv()
+            add_rows(self.down.at[d], [self.mine.at[d]])
+            self.along(1, d).start()
+
+    def finish(self):
+        n, chip = self.chips, self.chip
+        out, mine, up, down = self.out, self.mine.at[chip], self.up.at[chip], self.down.at[chip]
+
+        @pl.when(chip > 0)
+        def _():
+            self.along(0, chip).wait_recv()
+
+        @pl.when(chip < n - 1)
+        def _():
+            self.along(1, chip).wait_recv()
+
+        rows = out.shape[0]
+        slab = 16
+        has_up, has_down = chip > 0, chip < n - 1
+
+        @pl.when(has_up & has_down)
+        def _():
+            add_rows(mine, [up])
+
+        @pl.loop(0, rows // slab)
+        def _(i):
+            at = pl.ds(pl.multiple_of(i * slab, slab), slab)
+            out[at] = mine[at].astype(f32)
+
+        other = [(has_down, down), (has_up & jnp.logical_not(has_down), up)]
+        for there, buffer in other:
+            @pl.when(there)
+            def _():
+                @pl.loop(0, rows // slab)
+                def _(i):
+                    at = pl.ds(pl.multiple_of(i * slab, slab), slab)
+                    out[at] += buffer[at].astype(f32)
+
+        for c in range(n):
+            @pl.when((chip < n - 1) & (c > chip))
+            def _():
+                self.along(0, c).wait_send()
+
+            @pl.when((chip > 0) & (c < chip))
+            def _():
+                self.along(1, c).wait_send()
+
+
+class TensorScatter:
+    def __init__(self, parts, out, mine, land, send, recv, local, ranks):
+        self.parts, self.out, self.mine, self.land = parts, out, mine, land
+        self.send, self.recv, self.local, self.ranks = send, recv, local, ranks
+        chip, core, self.rank = place()
+        self.me = chip * 2 + core
+        self.steps = 1
+
+    @staticmethod
+    def scratch(ranks, shape):
+        return [
+            pltpu.VMEM(shape, bf16), pltpu.VMEM((ranks,) + shape, bf16),
+            pltpu.SemaphoreType.DMA((ranks,)), pltpu.SemaphoreType.DMA((ranks,)),
+            pltpu.SemaphoreType.DMA,
+        ]
+
+    def load(self):
+        return pltpu.make_async_copy(self.parts.at[self.rank], self.mine, self.local)
+
+    def copy(self, k):
+        to = lax.rem(self.rank + k, self.ranks)
+        return remote(
+            self.parts.at[to], self.land.at[k], self.send.at[k], self.recv.at[k], self.me, to
+        )
+
+    def step(self, k):
+        for j in range(1, self.ranks):
+            self.copy(j).start()
+        self.load().start()
+
+    def finish(self):
+        self.load().wait()
+        for j in range(1, self.ranks):
+            self.copy(j).wait()
+        slab = 16
+
+        @pl.loop(0, self.out.shape[0] // slab)
+        def _(i):
+            at = pl.ds(pl.multiple_of(i * slab, slab), slab)
+            total = self.mine[at].astype(f32)
+            for j in range(1, self.ranks):
+                total = total + self.land[j, at].astype(f32)
+            self.out[at] = total
+
+
+def run_all(jobs):
+    for k in range(max(job.steps for job in jobs)):
+        for job in jobs:
+            if k < job.steps:
+                job.step(k)
+    for job in jobs:
+        job.finish()
+
+
+def params(number):
+    return pltpu.CompilerParams(
+        collective_id=number, has_side_effects=True, vmem_limit_bytes=VMEM_BYTES
+    )
+
+
+ANY = pl.BlockSpec(memory_space=pl.ANY)
+ONCHIP = pl.BlockSpec(memory_space=pltpu.VMEM)
+
+
+def gather_kernel(chips, ranks, line, tensor, *refs):
+    n = line + tensor
+    ins, outs, rest = refs[:n], refs[n : 2 * n], refs[2 * n :]
+    greet(chips, ranks)
+    jobs = []
+    for i in range(n):
+        cls, size = (LineGather, chips) if i < line else (TensorGather, ranks)
+        jobs.append(cls(ins[i], outs[i], *rest[3 * i : 3 * i + 3], size))
+    run_all(jobs)
+
+
+def gather(number, chips, ranks, line, tensor):
+    arrays = list(line) + list(tensor)
+    scratch = []
+    shapes = []
+    for i, v in enumerate(arrays):
+        cls, size, count = (
+            (LineGather, chips, 2 * chips) if i < len(line) else (TensorGather, ranks, ranks)
+        )
+        scratch += cls.scratch(size)
+        shapes.append(jax.ShapeDtypeStruct((count,) + v.shape, v.dtype))
+    return pl.pallas_call(
+        functools.partial(gather_kernel, chips, ranks, len(line), len(tensor)),
+        in_specs=[ANY] * len(arrays),
+        out_specs=[ANY] * len(arrays),
+        out_shape=shapes,
+        scratch_shapes=scratch,
+        compiler_params=params(number),
+        name="gather",
+    )(*arrays)
+
+
+def scatter_kernel(chips, ranks, line, tensor, *refs):
+    n = line + tensor
+    ins, outs, rest = refs[:n], refs[n : 2 * n], list(refs[2 * n :])
+    greet(chips, ranks)
+    jobs = []
+    for i in range(n):
+        cls, size, take = (LineScatter, chips, 7) if i < line else (TensorScatter, ranks, 5)
+        jobs.append(cls(ins[i], outs[i], *rest[:take], size))
+        rest = rest[take:]
+    if line:
+        jobs[0].steps = chips
+    run_all(jobs)
+
+
+def scatter(number, chips, ranks, line, tensor):
+    arrays = list(line) + list(tensor)
+    scratch = []
+    shapes = []
+    for i, v in enumerate(arrays):
+        cls, size = (LineScatter, chips) if i < len(line) else (TensorScatter, ranks)
+        scratch += cls.scratch(size, v.shape[1:])
+        shapes.append(jax.ShapeDtypeStruct(v.shape[1:], f32))
+    return pl.pallas_call(
+        functools.partial(scatter_kernel, chips, ranks, len(line), len(tensor)),
+        in_specs=[ANY] * len(arrays),
+        out_specs=[ONCHIP] * len(arrays),
+        out_shape=shapes,
+        scratch_shapes=scratch,
+        compiler_params=params(number),
+        name="scatter",
+    )(*arrays)
+
+
+def sum_kernel(chips, ranks, shared, own_ref, out_ref, land, land_r, send, recv, send_r, recv_r):
+    chip, core, rank = place()
+    me = chip * 2 + core
+    devices = 2 * chips
+    sem = pltpu.get_barrier_semaphore()
+    for k in range(1, devices):
+        pl.semaphore_signal(
+            sem, inc=1, device_id=(lax.rem(me + k, devices), rank), device_id_type=MESH
+        )
+    for k in range(1, ranks):
+        pl.semaphore_signal(
+            sem, inc=1, device_id=(me, lax.rem(rank + k, ranks)), device_id_type=MESH
+        )
+    pl.semaphore_wait(sem, devices + ranks - 2)
+    first = [
+        remote(own_ref, land.at[me], send.at[k], recv.at[k], lax.rem(me + k, devices), rank)
+        for k in range(1, devices)
+    ]
+    for copy in first:
+        copy.start()
+    land[me] = own_ref[...]
+    for copy in first:
+        copy.wait_recv()
+    total = land[0]
+    for k in range(1, devices):
+        total = total + land[k]
+    land_r[rank] = total
+    second = [
+        remote(
+            land_r.at[rank], land_r.at[rank], send_r.at[k], recv_r.at[k], me,
+            lax.rem(rank + k, ranks),
+        )
+        for k in range(1, ranks)
+    ]
+    for copy in second:
+        copy.start()
+    for copy in first:
+        copy.wait_send()
+    for copy in second:
+        copy.wait()
+    whole = land_r[0, :shared]
+    for r in range(1, ranks):
+        whole = whole + land_r[r, :shared]
+    for r in range(ranks):
+        out_ref[r, :shared] = whole
+        out_ref[r, shared:] = land_r[r, shared:]
+
+
+def small_sums(number, chips, ranks, pack, shared):
+    shape = pack.shape
+    return pl.pallas_call(
+        functools.partial(sum_kernel, chips, ranks, shared),
+        in_specs=[ONCHIP],
+        out_specs=ONCHIP,
+        out_shape=jax.ShapeDtypeStruct((ranks,) + shape, f32),
+        scratch_shapes=[
+            pltpu.VMEM((2 * chips,) + shape, f32),
+            pltpu.VMEM((ranks,) + shape, f32),
+            pltpu.SemaphoreType.DMA((2 * chips,)),
+            pltpu.SemaphoreType.DMA((2 * chips,)),
+            pltpu.SemaphoreType.DMA((ranks,)),
+            pltpu.SemaphoreType.DMA((ranks,)),
+        ],
+        compiler_params=params(number),
+        name="small_sums",
+    )(pack)
+
+
+def scan_gather_kernel(blocks, total, chips, ranks, line, tensor, *refs):
+    n = line + tensor
+    own, ins = refs[:9], refs[9 : 9 + n]
+    outs, slots = refs[9 + n : 11 + n], refs[11 + n : 11 + 2 * n]
+    scratch, rest = refs[11 + 2 * n : 15 + 2 * n], refs[15 + 2 * n :]
+    now = pl.program_id(0) * blocks + pl.program_id(1)
+
+    @pl.when(now == 0)
+    def _():
+        greet(chips, ranks)
+
+    jobs = []
+    for i in range(n):
+        cls, size = (LineGather, chips) if i < line else (TensorGather, ranks)
+        jobs.append(cls(ins[i], slots[i], *rest[3 * i : 3 * i + 3], size))
+
+    @pl.when(now == 0)
+    def _():
+        for job in jobs:
+            job.step(0)
+
+    scan_fwd_kernel(blocks, *own, *outs, *scratch)
+
+    @pl.when(now == total - 1)
+    def _():
+        most = max(job.steps for job in jobs)
+        for k in range(1, most):
+            for job in jobs:
+                if k < job.steps:
+                    job.step(k)
+        for job in jobs:
+            job.finish()
+
+
+def scan_forward_gather(
+    number, chips, ranks, line, tensor, x, bc, st, seg, tapx, tapbc, par, spread, skip, nseq
+):
+    tokens, width = x.shape
+    n = BLOCK
+    blocks = tokens // nseq // n
+    at = lambda s, i: (s * blocks + i, 0)
+    whole = lambda s, i: (0, 0)
+    states = LANES
+    arrays = list(line) + list(tensor)
+    sems, shapes = [], []
+    for i, v in enumerate(arrays):
+        cls, size, count = (
+            (LineGather, chips, 2 * chips) if i < len(line) else (TensorGather, ranks, ranks)
+        )
+        sems += cls.scratch(size)
+        shapes.append(jax.ShapeDtypeStruct((count,) + v.shape, v.dtype))
+    return pl.pallas_call(
+        functools.partial(
+            scan_gather_kernel, blocks, nseq * blocks, chips, ranks, len(line), len(tensor)
+        ),
+        grid=(nseq, blocks),
+        in_specs=[
+            pl.BlockSpec((n, width), at),
+            pl.BlockSpec((n, 2 * states), at),
+            pl.BlockSpec((n, LANES), at),
+            pl.BlockSpec((n, LANES), at),
+            pl.BlockSpec(tapx.shape, whole),
+            pl.BlockSpec(tapbc.shape, whole),
+            pl.BlockSpec(par.shape, whole),
+            pl.BlockSpec(spread.shape, whole),
+            pl.BlockSpec(skip.shape, whole),
+        ]
+        + [ANY] * len(arrays),
+        out_specs=[pl.BlockSpec((n, width), at), pl.BlockSpec((states, width), at)]
+        + [ANY] * len(arrays),
+        out_shape=[
+            jax.ShapeDtypeStruct((tokens, width), f32),
+            jax.ShapeDtypeStruct((tokens // n * states, width), bf16),
+        ]
+        + shapes,
+        scratch_shapes=[
+            pltpu.VMEM((states, width), f32),
+            pltpu.VMEM((8, width), f32),
+            pltpu.VMEM((8, 2 * states), f32),
+            pltpu.VMEM((8, LANES), jnp.int32),
+        ]
+        + sems,
+        compiler_params=params(number),
+        name="scan_forward",
+    )(x, bc, st, seg, tapx, tapbc, par, spread, skip, *arrays)
+
+
+def scan_scatter_kernel(blocks, total, chips, ranks, line, *refs):
+    ins = refs[:15]
+    parts, near = refs[15 : 15 + line], refs[15 + line]
+    refs = refs[16 + line :]
+    outs, refs = refs[:6], refs[6:]
+    sums, near_sum, gbc_slots = refs[:line], refs[line], refs[line + 1]
+    refs = refs[line + 2 :]
+    scratch, gbc_own, refs = refs[:4], refs[4], refs[5:]
+    now = pl.program_id(0) * blocks + pl.program_id(1)
+
+    @pl.when(now == 0)
+    def _():
+        greet(chips, ranks)
+
+    jobs = []
+    for i in range(line):
+        jobs.append(LineScatter(parts[i], sums[i], *refs[7 * i : 7 * i + 7], chips))
+    refs = refs[7 * line :]
+    across = TensorScatter(near, near_sum, *refs[:5], ranks)
+    around = TensorGather(gbc_own, gbc_slots, *refs[5:], ranks)
+
+    @pl.when(now == 0)
+    def _():
+        across.step(0)
+        for job in jobs:
+            job.step(0)
+
+    @pl.when(now == 1)
+    def _():
+        for job in jobs:
+            job.step(1)
+
+    for k in range(2, chips):
+        if 2 * k < total - 1:
+            @pl.when(now == 2 * k)
+            def _():
+                jobs[0].step(k)
+
+    scan_bwd_kernel(blocks, *ins, *outs, *scratch)
+    row = pl.multiple_of(
+        (pl.program_id(0) * blocks + blocks - 1 - pl.program_id(1)) * BLOCK, BLOCK
+    )
+    gbc_own[pl.ds(row, BLOCK), :] = outs[1][...].astype(bf16)
+
+    @pl.when(now == total - 1)
+    def _():
+        around.step(0)
+        for k in range(2, chips):
+            for i, job in enumerate(jobs):
+                if i > 0 or 2 * k >= total - 1:
+                    job.step(k)
+        across.finish()
+        around.step(1)
+        around.finish()
+        for job in jobs:
+            job.finish()
+
+
+def scan_backward_scatter(
+    number, chips, ranks, line, near,
+    x, bc, st, seg, gy, y, h, tapx, tapbc, par, spread, skip, nseq,
+):
+    tokens, width = x.shape
+    n = BLOCK
+    blocks = tokens // nseq // n
+    at = lambda s, i: (s * blocks + blocks - 1 - i, 0)
+    tail = lambda s, i: (jnp.maximum((s * blocks + blocks - 1 - i) * (n // 8) - 1, 0), 0)
+    whole = lambda s, i: (0, 0)
+    states = LANES
+    sems = []
+    for v in line:
+        sems += LineScatter.scratch(chips, v.shape[1:])
+    sems += TensorScatter.scratch(ranks, near.shape[1:])
+    sems += TensorGather.scratch(ranks)
+    return pl.pallas_call(
+        functools.partial(scan_scatter_kernel, blocks, nseq * blocks, chips, ranks, len(line)),
+        grid=(nseq, blocks),
+        in_specs=[
+            pl.BlockSpec((n, width), at),
+            pl.BlockSpec((8, width), tail),
+            pl.BlockSpec((n, 2 * states), at),
+            pl.BlockSpec((8, 2 * states), tail),
+            pl.BlockSpec((n, LANES), at),
+            pl.BlockSpec((n, LANES), at),
+            pl.BlockSpec((8, LANES), tail),
+            pl.BlockSpec((n, width), at),
+            pl.BlockSpec((n, width), at),
+            pl.BlockSpec((states, width), at),
+            pl.BlockSpec(tapx.shape, whole),
+            pl.BlockSpec(tapbc.shape, whole),
+            pl.BlockSpec(par.shape, whole),
+            pl.BlockSpec(spread.shape, whole),
+            pl.BlockSpec(skip.shape, whole),
+        ]
+        + [ANY] * (len(line) + 1),
+        out_specs=[
+            pl.BlockSpec((n, width), at),
+            pl.BlockSpec((n, 2 * states), at),
+            pl.BlockSpec((n, LANES), at),
+            pl.BlockSpec((40, width), whole),
+            pl.BlockSpec((40, 2 * states), whole),
+            pl.BlockSpec((24, LANES), whole),
+        ]
+        + [pl.BlockSpec(v.shape[1:], whole) for v in line]
+        + [pl.BlockSpec(near.shape[1:], whole), ANY],
+        out_shape=[
+            jax.ShapeDtypeStruct((tokens, width), bf16),
+            jax.ShapeDtypeStruct((tokens, 2 * states), f32),
+            jax.ShapeDtypeStruct((tokens, LANES), bf16),
+            jax.ShapeDtypeStruct((40, width), f32),
+            jax.ShapeDtypeStruct((40, 2 * states), f32),
+            jax.ShapeDtypeStruct((24, LANES), f32),
+        ]
+        + [jax.ShapeDtypeStruct(v.shape[1:], f32) for v in line]
+        + [
+            jax.ShapeDtypeStruct(near.shape[1:], f32),
+            jax.ShapeDtypeStruct((ranks, tokens, 2 * states), bf16),
+        ],
+        scratch_shapes=[
+            pltpu.VMEM((states, width), f32),
+            pltpu.VMEM((8, width), f32),
+            pltpu.VMEM((8, 2 * states), f32),
+            pltpu.VMEM((8, LANES), jnp.int32),
+            pltpu.VMEM((tokens, 2 * states), bf16),
+        ]
+        + sems,
+        compiler_params=params(number),
+        name="scan_backward",
+    )(x, x, bc, bc, st, seg, seg, gy, y, h, tapx, tapbc, par, spread, skip, *line, near)
+
+
 epsilon = 1e-05
-
-
-def placed_at(whole, piece, offset):
-    start = (0,) * (len(whole) - 1) + (offset,)
-    return lax.dynamic_update_slice(jnp.zeros(whole, piece.dtype), piece, start)
 
 
 def per_device(
@@ -419,13 +1128,10 @@
     stream = residual.astype(f32)
     scaling = lax.rsqrt(jnp.mean(stream * stream, axis=1, keepdims=True) + epsilon)
     normed = (stream * scaling * norm_gain).astype(bf16)
-    normed_all = lax.all_gather(normed, "tensor", axis=0, tiled=True)
-    wx = lax.all_gather(
-        jnp.concatenate([inner_weight[:, 1], on_lanes(step_weight)], axis=1), "dp", axis=0, tiled=True
-    )
-    wz = lax.all_gather(inner_weight[:, 0], "dp", axis=0, tiled=True)
-    wo = lax.all_gather(out_weight, "dp", axis=1, tiled=True)
-    cot_all = lax.all_gather(cotangent, "tensor", axis=0, tiled=True)
+    chips, ranks = lax.axis_size("dp") // 2, lax.axis_size("tensor")
+    wx_own = jnp.concatenate([inner_weight[:, 1], on_lanes(step_weight)], axis=1)
+    wx, normed_all = gather(1, chips, ranks, [wx_own], [normed])
+    wx, normed_all = wx.reshape(model_width, width + LANES), normed_all.reshape(tokens, model_width)
     taps = jnp.concatenate([conv_weight, conv_bias[None], jnp.zeros((3, conv_bias.shape[0]), f32)], axis=0)
     tapx = lax.dynamic_slice_in_dim(taps, inner_start, width, 1)
     tapbc = taps[:, inner_width:]
@@ -442,12 +1148,17 @@
     xst = mm(normed_all, wx)
     bc = mm(normed_all, state_weight)
     x, st = xst[:, :width], xst[:, width:]
-    y, h = scan_forward(x, bc, st, seg, tapx, tapbc, par, spread, skip, nseq)
+    y, h, wz, wo, cot_all = scan_forward_gather(
+        2, chips, ranks, [inner_weight[:, 0], out_weight.T], [cotangent],
+        x, bc, st, seg, tapx, tapbc, par, spread, skip, nseq,
+    )
+    wz, wo = wz.reshape(model_width, width), wo.reshape(model_width, width)
+    cot_all = cot_all.reshape(tokens, model_width)
     z = mm(normed_all, wz)
     sig = jax.nn.sigmoid(z)
     silu = z * sig
     gated = y * silu
-    gng = mm_nt(cot_all, wo)
+    gng = mm(cot_all, wo)
     sums = lax.psum(
         jnp.stack([jnp.sum(gated * gated, axis=1), jnp.sum(gng * gain * gated, axis=1)]), "tensor"
     )
@@ -457,32 +1168,54 @@
     gain_grad = jnp.sum(gng * gated * scale_g, axis=0)
     gz = (grad_gated * y * (sig * (1.0 + z * (1.0 - sig)))).astype(bf16)
     gy = grad_gated * silu
-    scatter = lambda v, axis, dim: lax.psum_scatter(
-        v.astype(bf16), axis, scatter_dimension=dim, tiled=True
-    ).astype(f32)
-    block_out = stream + scatter(mm(normed_g, wo), "tensor", 0)
-    out_grad = scatter(mm_tn(normed_g, cot_all), "dp", 1)
-    z_grad = scatter(mm_tn(normed_all, gz), "dp", 0)
-    gx, gbc, gst, gtapx, gtapbc, gpar = scan_backward(
-        x, bc, st, seg, gy, y, h, tapx, tapbc, par, spread, skip, nseq
-    )
-    gbc = gbc.astype(bf16)
-    gxs = jnp.concatenate([gx, gst * (lax.broadcasted_iota(jnp.int32, (1, LANES), 1) < LANES // 2)], axis=1)
-    total = mm_nt(gz, wz) + mm_nt(gxs, wx) + mm_nt(gbc, state_weight)
-    grad_normed = scatter(total, "tensor", 0)
-    x_grad = scatter(mm_tn(normed_all, gxs), "dp", 0)
-    state_grad = scatter(mm_tn(normed_all, gbc), ("dp", "tensor"), 0)
-    state_grad = lax.all_gather(state_grad, ("dp", "tensor"), axis=0, tiled=True)
+    devices = 2 * chips
+    parts = lambda v, count: v.astype(bf16).reshape(count, v.shape[0] // count, v.shape[1])
+    gx, _, gst, gtapx, gtapbc, gpar, z_grad, out_grad, projected, gbc = scan_backward_scatter(
+        3, chips, ranks,
+        [parts(mm_tn(normed_all, gz), devices), parts(mm_tn(cot_all, normed_g), devices)],
+        parts(mm_nt(normed_g, wo), ranks),
+        x, bc, st, seg, gy, y, h, tapx, tapbc, par, spread, skip, nseq,
+    )
+    block_out = stream + projected
+    gbc_own = lax.dynamic_index_in_dim(gbc, rank, 0, keepdims=False)
+    gbc = jnp.sum(gbc.astype(f32), axis=0).astype(bf16)
+    low = lax.broadcasted_iota(jnp.int32, (1, LANES), 1) < LANES // 2
+    gst = jnp.where(low, gst, 0)
+    gxs = jnp.concatenate([gx, gst], axis=1)
+    depth = model_width // ranks
+    rows = lax.dynamic_slice_in_dim(normed_all, rank * depth, depth, 1)
+    per = depth * state_weight.shape[1] // model_width
+    state_part = jnp.pad(
+        mm_tn(rows, gbc).astype(bf16).reshape(model_width, per), ((0, 0), (LANES // 2, LANES // 2 - per))
+    )
+    grads = mm_tn(normed_all, gxs).astype(bf16)
+    grads = jnp.concatenate([grads[:, :width], grads[:, width:] + state_part], axis=1)
+    total = mm_nt(gz, wz) + mm_nt(gxs, wx) + mm_nt(gbc_own, state_weight)
+    x_grad, grad_normed = scatter(
+        4, chips, ranks, [parts(grads, devices)], [parts(total, ranks)]
+    )
+    own_state = x_grad[:, width + LANES // 2 : width + LANES // 2 + per]
+    own_state = own_state.astype(bf16).reshape(depth // devices, state_weight.shape[1])
+    state_grad = lax.all_gather(own_state, ("tensor", "dp"), axis=0, tiled=True).astype(f32)
     gtapx = gtapx.reshape(5, 8, -1).sum(1)
     gtapbc = gtapbc.reshape(5, 8, -1).sum(1)
     gpar = gpar.reshape(3, 8, -1).sum(1)[:, :heads]
-    gtaps = jnp.concatenate(
-        [placed_at((5, inner_width), gtapx, inner_start), gtapbc], axis=1
-    )
-    gpars = placed_at((3, step_bias.shape[0]), gpar, head_start)
-    ggain = placed_at((1, inner_width), gain_grad[None], inner_start)
-    gtaps, gpars, ggain = lax.psum((gtaps, gpars, ggain), ("dp", "tensor"))
-    norm_grad = lax.psum(jnp.sum(grad_normed * stream * scaling, axis=0), ("dp", "tensor"))
+    norm_grad = jnp.sum(grad_normed * stream * scaling, axis=0)
+    flat = lambda v: v.reshape(-1, LANES)
+    mine = [gtapx, gain_grad[None], jnp.pad(gpar, ((0, 5), (0, LANES - heads)))]
+    ours = [norm_grad[None], gtapbc, jnp.zeros((3, 2 * LANES), f32)]
+    shared = sum(v.size for v in ours) // LANES
+    sums = small_sums(
+        5, chips, ranks, jnp.concatenate([flat(v) for v in ours + mine], axis=0), shared
+    )
+    ours, mine = sums[0, :shared], sums[:, shared:]
+    norm_grad = ours[: model_width // LANES].reshape(-1)
+    gtapbc = ours[model_width // LANES :].reshape(8, -1)[:5]
+    count = width // LANES
+    gtapx = mine[:, : 5 * count].reshape(ranks, 5, width).transpose(1, 0, 2).reshape(5, inner_width)
+    gain_grad = mine[:, 5 * count : 6 * count].reshape(inner_width)
+    gpars = mine[:, 6 * count : 6 * count + 3, :heads].transpose(1, 0, 2).reshape(3, -1)
+    gtaps = jnp.concatenate([gtapx, gtapbc], axis=1)
     along = jnp.sum(grad_normed * norm_gain * stream, axis=1, keepdims=True)
     residual_grad = (
         cotangent.astype(f32)
@@ -493,7 +1226,7 @@
     return (
         block_out, residual_grad, norm_grad, inner_grad, state_grad,
         x_grad[:, width : width + heads], gtaps[:4], gtaps[4], gpars[0], gpars[1], gpars[2],
-        ggain[0], out_grad,
+        gain_grad, out_grad.T,
     )
 
 

time: 960 us -> 515 us (0.54)
  waiting for transfers between devices: 677 us -> 9.85 us
  Pallas kernels: 58.8 us -> 299 us
  blocking collectives: 51.7 us -> 9.2 us
  local copies, waits for them, and re-layouts: 24.4 us -> 50.1 us
    reduce_scatter x6 -> x0, waiting for transfers between devices: 348 us -> none  [per_device(): lax.psum_scatter(v.astype(bf16), axis, scatter_dimension=dim, tiled=True)]
    all_gather x6 -> x1, waiting for transfers between devices: 267 us -> 9.84 us  [per_device(): lax.all_gather(own_state, ('tensor', 'dp'), axis=0, tiled=True).astype(f32)]
    pallas_call x2 -> x5, Pallas kernels: 58.8 us -> 299 us  [the longest x1 82.3 us: scan_backward_scatter(): pl.pallas_call(functools.partial(scan_scatter_kernel, blocks, nseq * bloc...]
    psum x1 -> x0, waiting for transfers between devices: 60.2 us -> none  [per_device(): gtaps, gpars, ggain = lax.psum((gtaps, gpars, ggain), ('dp', 'tensor'))]
    psum x1 -> x0, blocking collectives: 41.7 us -> none  [per_device(): lax.psum(jnp.sum(grad_normed * stream * scaling, axis=0), ('dp', 'tensor'))]
    dot_general x4, matrix products: 33 us -> 22.1 us  [mm_tn(): return lax.dot_general(a, b, ROWS0, preferred_element_type=f32)]
    concatenate x1 -> x2, local copies, waits for them, and re-layouts: 0.07 us -> 11 us  [the longest x1 6.69 us: per_device(): jnp.concatenate([grads[:, :width], grads[:, width:] + state_part], axis=1)]
  transfers between devices with their start and end apart: 13 -> 1, of which waited for: 13 -> 1; matrix products, arithmetic and copies ran while one was open for 11% -> 6% of each run, Pallas kernels for 2% -> 5%
where the time goes in v2:
time: 515 us; the launch traced here: 506 us
  Pallas kernels  299 us (58%)
  matrix products  93.4 us (18%)
  local copies, waits for them, and re-layouts  50.1 us (10%)
  other arithmetic  29.9 us (6%)
  between operations  14.8 us (3%)
  waiting for transfers between devices  9.85 us (2%)
  blocking collectives  9.2 us (2%)
    pallas_call x1, Pallas kernels, scan_backward_scatter(): pl.pallas_call(functools.partial(scan_scatter_kernel, blocks, nseq * bloc...  82.3 us
    pallas_call x1, Pallas kernels, scan_forward_gather(): pl.pallas_call(functools.partial(scan_gather_kernel, blocks, nseq * block...  75.9 us
    pallas_call x1, Pallas kernels, scatter(): pl.pallas_call(functools.partial(scatter_kernel, chips, ranks, len(line),...  59.8 us
    pallas_call x1, Pallas kernels, gather(): pl.pallas_call(functools.partial(gather_kernel, chips, ranks, len(line),...  55 us
    dot_general x4, matrix products, mm_nt(): return lax.dot_general(a, b, COLS1, preferred_element_type=f32)  35.9 us
    dot_general x4, matrix products, mm(): return jnp.dot(a, b, preferred_element_type=f32)  35.4 us
    pallas_call x1, Pallas kernels, small_sums(): pl.pallas_call(functools.partial(sum_kernel, chips, ranks, shared), in_sp...  25.5 us
    dot_general x4, matrix products, mm_tn(): return lax.dot_general(a, b, ROWS0, preferred_element_type=f32)  22.1 us
  transfers between devices with their start and end apart: 1, of which 1 were waited for; matrix products, arithmetic and copies ran while one was open for 6% of the time, Pallas kernels for 5%

profile of v2, /device:TPU:0, one launch (start us, length us, event | category | flops | bytes accessed | tf_op | source)
XLA Modules:
  0.0 505.8 jit_solution(16375245923811273688)
XLA Ops:
  17.6 55.0 %gather.1 = (bf16[8,256,1152]{2,1,0:T(8,128)(2,1)}, bf16[4,256,2048]{2,1,0:T(8,128)(2,1)}) custom-call(bf16[256,1152]{1,0:T(8,128)(2,1)} %concatenate.27.refs_0_, bf16[256,2048]{1,0:T(8,128)(2,1)} %fusion.3.refs_1_), custom_call_target="tpu_custom_call" | custom-call | tf_op jit(solution)/shard_map/gather/pallas_call | solution.py:783
  72.6 8.7 %fusion.32 = f32[1024,1152]{1,0:T(8,128)S(1)} fusion(bf16[1024,2048]{1,0:T(8,128)(2,1)} %bitcast.92, bf16[2048,1152]{1,0:T(8,128)(2,1)} %bitcast.88), kind=kOutput, calls=%fused_computation.90 | convolution fusion | flops 4831838208 | bytes 13631488 | tf_op jit(solution)/shard_map/dot_general | solution.py:19
  86.6 4.4 fusion.33.refs_1_.refs_2_.refs_3_
  95.1 75.9 %scan_forward.1 = (f32[1024,1024]{1,0:T(8,128)}, bf16[1024,1024]{1,0:T(8,128)(2,1)}, bf16[8,256,1024]{2,1,0:T(8,128)(2,1)}, bf16[8,256,1024]{2,1,0:T(8,128)(2,1)}, bf16[4,256,2048]{2,1,0:T(8,128)(2,1)}) custom-call(f32[1024,1024]{1,0:T(8,128)} %slice.111.refs_0_.refs_1_, f32[1024,256]{1,0:T(8,128)} %fusion.33.refs_1_.refs_2_.refs_3_, ...), custom_call_target="tpu_custom_call" | custom-call | tf_op jit(solution)/shard_map/scan_forward/pallas_call | solution.py:946
  171.1 8.4 %fusion.34 = f32[1024,1024]{1,0:T(8,128)} fusion(bf16[1024,2048]{1,0:T(8,128)(2,1)S(1)} %bitcast.95, bf16[2048,1024]{1,0:T(8,128)(2,1)} %bitcast.98), kind=kOutput, calls=%fused_computation.92 | convolution fusion | flops 4294967296 | bytes 12582912 | tf_op jit(solution)/shard_map/dot_general | solution.py:19
  180.2 13.8 %multiply_reduce_fusion.2 = (f32[1024]{0:T(1024)S(1)}, f32[1024]{0:T(1024)S(1)}, f32[1024,1024]{1,0:T(8,128)}, f32[1024,1024]{1,0:T(8,128)}) fusion(f32[1024]{0:T(1024)S(1)} %dynamic_slice.26, f32[1024,1024]{1,0:T(8,128)} %get-tuple-element.33.refs_8_, f32[1024,1024]{1,0:T(8,128)} %fusion.34, bf16[1024,2048]{1,0:T(8,128)(2,1)} %bitcast.100, ...), kind=kOutput, calls=%fused_computation.14 | convolution fusion | flops 4305451008 | bytes 25178112 | tf_op jit(solution)/shard_map/dot_general | solution.py:19
  194.0 9.2 %psum.7 = f32[2,1024]{1,0:T(2,128)S(1)} all-reduce(f32[2,1024]{1,0:T(2,128)S(1)} %pad_maximum_fusion.6), channel_id=1, replica_groups=mesh['dp'=8,'tensor'=4] {'tensor'}, use_global_device_ids=true, to_apply=%region_3.4 | all-reduce | flops 2048 | bytes 16384 | tf_op jit(solution)/shard_map/psum | solution.py:1162
  203.3 10.1 %convolution_convert_fusion.1 = bf16[1024,2048]{1,0:T(8,128)(2,1)} fusion(bf16[2048,1024]{1,0:T(8,128)(2,1)} %bitcast.103, f32[1024,1024]{1,0:T(8,128)} %get-tuple-element.82, f32[1024]{0:T(1024)S(1)} %bitcast.77, f32[1024]{0:T(1024)S(1)} %dynamic_slice.26), kind=kOutput, calls=%fused_computation.17 | convolution fusion | flops 4300210176 | bytes 12591104 | tf_op jit(solution)/shard_map/dot_general | solution.py:27
  213.4 7.0 %convolution_convert_fusion.2 = bf16[2048,1024]{1,0:T(8,128)(2,1)} fusion(bf16[1024,2048]{1,0:T(8,128)(2,1)S(1)} %bitcast.101, f32[1024,1024]{1,0:T(8,128)S(1)} %copy-done.4, f32[1024]{0:T(1024)S(1)} %bitcast.78, f32[1024]{0:T(1024)S(1)} %dynamic_slice.26), kind=kOutput, calls=%fused_computation.18 | convolution fusion | flops 4300210176 | bytes 12591104 | tf_op jit(solution)/shard_map/dot_general | solution.py:23
  220.5 4.6 multiply_convert_fusion.1
  225.1 6.3 %convolution_convert_fusion.3 = bf16[2048,1024]{1,0:T(8,128)(2,1)} fusion(bf16[1024,2048]{1,0:T(8,128)(2,1)S(1)} %bitcast.96, bf16[1024,1024]{1,0:T(8,128)(2,1)S(1)} %get-tuple-element.83), kind=kOutput, calls=%fused_computation.19 | convolution fusion | flops 4297064448 | bytes 10485760 | tf_op jit(solution)/shard_map/dot_general | solution.py:23
  231.4 6.9 %fusion.35 = f32[1024,2048]{1,0:T(8,128)} fusion(bf16[1024,1024]{1,0:T(8,128)(2,1)S(1)} %get-tuple-element.83, bf16[2048,1024]{1,0:T(8,128)(2,1)S(1)} %bitcast.99), kind=kOutput, calls=%fused_computation.93 | convolution fusion | flops 4294967296 | bytes 14680064 | tf_op jit(solution)/shard_map/dot_general | solution.py:27
  238.3 82.3 %scan_backward.1 = (bf16[1024,1024]{1,0:T(8,128)(2,1)}, f32[1024,256]{1,0:T(8,128)}, bf16[1024,128]{1,0:T(8,128)(2,1)}, f32[40,1024]{1,0:T(8,128)}, f32[40,256]{...) custom-call(f32[1024,1024]{1,0:T(8,128)} %slice.111.refs_0_.refs_1_,, ...), custom_call_target="tpu_custom_call" | custom-call | tf_op jit(solution)/shard_map/scan_backward/pallas_call | solution.py:1056
  321.6 9.6 %fusion.9 = f32[1024,2048]{1,0:T(8,128)} fusion(bf16[2048,1152]{1,0:T(8,128)(2,1)S(1)} %bitcast.91, bf16[1024,128]{1,0:T(8,128)(2,1)S(1)} %broadcast_select_fusion, bf16[1024,1024]{1,0:T(8,128)(2,1)} %get-tuple-element.39), kind=kOutput, calls=%fused_computation.30 | convolution fusion | flops 4836556800 | bytes 15466496 | tf_op jit(solution)/shard_map/dot_general | solution.py:27
  331.3 7.1 %convolution_convert_fusion = bf16[2048,1152]{0,1:T(8,128)(2,1)} fusion(bf16[1024,2048]{1,0:T(8,128)(2,1)S(1)} %bitcast.97, bf16[1024,128]{1,0:T(8,128)(2,1)S(1)} %broadcast_select_fusion, bf16[1024,1024]{1,0:T(8,128)(2,1)S(1)} %copy-done.23), kind=kOutput, calls=%fused_computation.1 | convolution fusion | flops 4838916096 | bytes 11272192 | tf_op jit(solution)/shard_map/dot_general | solution.py:23
  338.4 4.8 slice.116
  348.7 5.1 %pad_maximum_fusion = bf16[2048,1152]{0,1:T(8,128)(2,1)} fusion(bf16[2048,128]{0,1:T(8,128)(2,1)S(1)} %slice_add_fusion, bf16[2048,1024]{0,1:T(8,128)(2,1)} %slice.116), kind=kLoop, calls=%fused_computation.2 | loop fusion | flops 9437184 | bytes 9437184 | tf_op jit(solution)/shard_map/concatenate | solution.py:1192
  353.8 6.7 %copy.47 = bf16[2048,1152]{1,0:T(8,128)(2,1)} copy(bf16[2048,1152]{0,1:T(8,128)(2,1)} %pad_maximum_fusion) | data formatting | bytes 9437184 | tf_op jit(solution)/shard_map/concatenate | solution.py:1192
  360.4 9.2 %add_convert_fusion = bf16[1024,2048]{1,0:T(8,128)(2,1)} fusion(f32[1024,2048]{1,0:T(8,128)} %fusion.35, f32[1024,2048]{1,0:T(8,128)} %fusion.9, bf16[2048,256]{1,0:T(8,128)(2,1)S(1)} %copy-done, bf16[4,1024,256]{2,1,0:T(8,128)(2,1)} %get-tuple-element.41, s32[]{:T(128)S(6)} %select_n.45), kind=kOutput, calls=%fused_computation | convolution fusion | flops 1080033280 | bytes 22544388 | tf_op jit(solution)/shard_map/dot_general | solution.py:27
  369.7 59.8 %scatter.1 = (f32[256,1152]{1,0:T(8,128)}, f32[256,2048]{1,0:T(8,128)}) custom-call(bf16[8,256,1152]{2,1,0:T(8,128)(2,1)} %bitcast.67, bf16[4,256,2048]{2,1,0:T(8,128)(2,1)} %bitcast.68), custom_call_target="tpu_custom_call" | custom-call | tf_op jit(solution)/shard_map/scatter/pallas_call | solution.py:816
  433.5 4.3 concatenate.34.own_ref
  437.8 25.5 %small_sums.1 = f32[4,88,128]{2,1,0:T(8,128)} custom-call(f32[88,128]{1,0:T(8,128)} %concatenate.34.own_ref), custom_call_target="tpu_custom_call" | custom-call | tf_op jit(solution)/shard_map/small_sums/pallas_call | solution.py:877
  481.2 5.0 fusion.5
  486.2 9.8 %all-gather.2.cloned.1.call-done = bf16[2048,256]{1,0:T(8,128)(2,1)} async-done(((bf16[64,256]{1,0:T(8,128)(2,1)}), bf16[2048,256]{1,0:T(8,128)(2,1)}) %all-gather.2.cloned.1.call-update) | async-done | bytes 1048592 | tf_op jit(solution)/shard_map/all_gather | solution.py:1199
  (130 shorter events, 51.3 us)
Async XLA Ops:
  7.2 79.4 %copy-start = (bf16[2048,256]{1,0:T(8,128)(2,1)S(1)}, bf16[2048,256]{1,0:T(8,128)(2,1)}, u32[]{:S(2)}) copy-start(bf16[2048,256]{1,0:T(8,128)(2,1)} %param.18) | copy-start | bytes 3145732
  7.2 4.2 copy-start.14
  7.2 4.3 copy-start.2
  7.2 488.8 %all-gather.2.cloned.1.call-start = ((), (), s32[]{:S(2)}) async-start(), calls=%async_computation | async-start | bytes 1081344 | tf_op jit(solution)/shard_map/all_gather | solution.py:1199
  7.3 9.0 %copy-start.9 = (f32[2048]{0:T(1024)S(1)}, f32[2048]{0:T(1024)}, u32[]{:S(2)}) copy-start(f32[2048]{0:T(1024)} %param.16) | copy-start | bytes 24580
  81.4 4.9 copy-start.24
  84.8 6.2 %copy-start.7 = (bf16[1024,256]{1,0:T(8,128)(2,1)S(1)}, bf16[1024,256]{1,0:T(8,128)(2,1)}, u32[]{:S(2)}) copy-start(bf16[1024,256]{1,0:T(8,128)(2,1)} %param.26) | copy-start | bytes 1572868
  86.6 7.6 %copy-start.15 = (s32[1,1024]{1,0:T(1,128)S(1)}, s32[1,1024]{1,0:T(1,128)}, u32[]{:S(2)}) copy-start(s32[1,1024]{1,0:T(1,128)} %param.15) | copy-start | bytes 12292
  95.1 75.9 %copy-start.18 = (bf16[4,256,2048]{2,1,0:T(8,128)(2,1)S(1)}, bf16[4,256,2048]{2,1,0:T(8,128)(2,1)}, u32[]{:S(2)}) copy-start(bf16[4,256,2048]{2,1,0:T(8,128)(2,1)} %get-tuple-element.31) | copy-start | bytes 12582916
  203.3 10.2 %copy-start.4 = (f32[1024,1024]{1,0:T(8,128)S(1)}, f32[1024,1024]{1,0:T(8,128)}, u32[]{:S(2)}) copy-start(f32[1024,1024]{1,0:T(8,128)} %get-tuple-element.82) | copy-start | bytes 12582916
  203.3 10.2 %copy-start.22 = (bf16[4,256,2048]{2,1,0:T(8,128)(2,1)S(1)}, bf16[4,256,2048]{2,1,0:T(8,128)(2,1)}, u32[]{:S(2)}) copy-start(bf16[4,256,2048]{2,1,0:T(8,128)(2,1)} %get-tuple-element.35) | copy-start | bytes 12582916
  213.4 7.1 %copy-start.1 = (f32[1024,1024]{1,0:T(8,128)S(1)}, f32[1024,1024]{1,0:T(8,128)}, u32[]{:S(2)}) copy-start(f32[1024,1024]{1,0:T(8,128)} %get-tuple-element.33.refs_8_) | copy-start | bytes 12582916
  213.4 7.1 %copy-start.3 = (f32[1024,1024]{1,0:T(8,128)S(1)}, f32[1024,1024]{1,0:T(8,128)}, u32[]{:S(2)}) copy-start(f32[1024,1024]{1,0:T(8,128)} %fusion.34) | copy-start | bytes 12582916
  213.4 7.1 %copy-start.5 = (f32[1024,1024]{1,0:T(8,128)S(1)}, f32[1024,1024]{1,0:T(8,128)}, u32[]{:S(2)}) copy-start(f32[1024,1024]{1,0:T(8,128)} %get-tuple-element.92) | copy-start | bytes 12582916
  220.5 4.6 copy-start.19
  225.1 6.3 %copy-start.21 = (bf16[8,256,1024]{2,1,0:T(8,128)(2,1)S(1)}, bf16[8,256,1024]{2,1,0:T(8,128)(2,1)}, u32[]{:S(2)}) copy-start(bf16[8,256,1024]{2,1,0:T(8,128)(2,1)} %get-tuple-element.34) | copy-start | bytes 12582916
  231.4 90.2 %slice-start = ((s8[4718592]{0:T(1024)(128)(4,1)}), s8[524288]{0:T(1024)(128)(4,1)S(1)}, s32[]{:S(2)}) async-start(s8[4718592]{0:T(1024)(128)(4,1)} %bitcast.89), calls=%async_computation.1 | async-start | bytes 1048576
  238.3 83.3 %slice-start.1 = ((s8[4718592]{0:T(1024)(128)(4,1)}), s8[4194304]{0:T(1024)(128)(4,1)S(1)}, s32[]{:S(2)}) async-start(s8[4718592]{0:T(1024)(128)(4,1)} %bitcast.89), calls=%async_computation.2 | async-start | bytes 8388608
  321.6 9.7 %copy-start.20 = (bf16[4,256,2048]{2,1,0:T(8,128)(2,1)S(1)}, bf16[4,256,2048]{2,1,0:T(8,128)(2,1)}, u32[]{:S(2)}) copy-start(bf16[4,256,2048]{2,1,0:T(8,128)(2,1)} %get-tuple-element.31) | copy-start | bytes 12582916
  321.6 9.7 %copy-start.23 = (bf16[1024,1024]{1,0:T(8,128)(2,1)S(1)}, bf16[1024,1024]{1,0:T(8,128)(2,1)}, u32[]{:S(2)}) copy-start(bf16[1024,1024]{1,0:T(8,128)(2,1)} %get-tuple-element.39) | copy-start | bytes 6291460
  369.7 63.7 %copy-start.8 = (f32[40,1024]{1,0:T(8,128)S(1)}, f32[40,1024]{1,0:T(8,128)}, u32[]{:S(2)}) copy-start(f32[40,1024]{1,0:T(8,128)} %get-tuple-element.44) | copy-start | bytes 491524
  369.7 63.7 %copy-start.11 = (f32[40,256]{1,0:T(8,128)S(1)}, f32[40,256]{1,0:T(8,128)}, u32[]{:S(2)}) copy-start(f32[40,256]{1,0:T(8,128)} %get-tuple-element.43) | copy-start | bytes 122884
  369.7 63.8 %copy-start.13 = (f32[24,128]{1,0:T(8,128)S(1)}, f32[24,128]{1,0:T(8,128)}, u32[]{:S(2)}) copy-start(f32[24,128]{1,0:T(8,128)} %get-tuple-element.45) | copy-start | bytes 36868
  469.2 11.9 %copy-start.6 = (bf16[256,2048]{1,0:T(8,128)(2,1)S(1)}, bf16[256,2048]{1,0:T(8,128)(2,1)}, u32[]{:S(2)}) copy-start(bf16[256,2048]{1,0:T(8,128)(2,1)} %refs_11_.1) | copy-start | bytes 3145732
  (4 other events, 14.1 us)
Sparse Core Ops, SparseCore 0:
  431.3 64.6 all-gather.1

commit v3 on v1

--- a/solution.py
+++ b/solution.py
@@ -135,46 +135,6 @@
     tail_x[...] = x_ref[n - 8 :, :]
     tail_bc[...] = bc_ref[n - 8 :, :]
     tail_seg[...] = seg_ref[n - 8 :, :]
-
-
-def scan_forward(x, bc, st, seg, tapx, tapbc, par, spread, skip, nseq):
-    tokens, width = x.shape
-    n = BLOCK
-    blocks = tokens // nseq // n
-    at = lambda s, i: (s * blocks + i, 0)
-    whole = lambda s, i: (0, 0)
-    states = LANES
-    return pl.pallas_call(
-        functools.partial(scan_fwd_kernel, blocks),
-        grid=(nseq, blocks),
-        in_specs=[
-            pl.BlockSpec((n, width), at),
-            pl.BlockSpec((n, 2 * states), at),
-            pl.BlockSpec((n, LANES), at),
-            pl.BlockSpec((n, LANES), at),
-            pl.BlockSpec(tapx.shape, whole),
-            pl.BlockSpec(tapbc.shape, whole),
-            pl.BlockSpec(par.shape, whole),
-            pl.BlockSpec(spread.shape, whole),
-            pl.BlockSpec(skip.shape, whole),
-        ],
-        out_specs=[pl.BlockSpec((n, width), at), pl.BlockSpec((states, width), at)],
-        out_shape=[
-            jax.ShapeDtypeStruct((tokens, width), f32),
-            jax.ShapeDtypeStruct((tokens // n * states, width), bf16),
-        ],
-        scratch_shapes=[
-            pltpu.VMEM((states, width), f32),
-            pltpu.VMEM((8, width), f32),
-            pltpu.VMEM((8, 2 * states), f32),
-            pltpu.VMEM((8, LANES), jnp.int32),
-        ],
-        compiler_params=pltpu.CompilerParams(vmem_limit_bytes=VMEM_BYTES),
-        cost_estimate=pl.CostEstimate(
-            flops=tokens * width * 1000, bytes_accessed=tokens * width * 12, transcendentals=0
-        ),
-        name="scan_forward",
-    )(x, bc, st, seg, tapx, tapbc, par, spread, skip)
 
 
 def fold(v):
@@ -305,7 +265,7 @@
     gu = taps[3:4] * gconv
     for k in (1, 2, 3):
         gu = gu + taps[3 - k : 4 - k] * jnp.where(wide(ahead[k]), ext[k : k + n], 0.0)
-    gbc_ref[...] = gu
+    gbc_ref[...] = gu.astype(gbc_ref.dtype)
     for k in range(4):
         row = 8 * (3 - k)
         gtapbc_ref[row : row + 8, :] += fold(gconv * shifts_bc[k])
@@ -321,22 +281,932 @@
     glog = after + edge
     gdt = sum_dt + a * glog
     gst = gdt * sigmoid(v)
-    gst_ref[...] = gst.astype(bf16)
+    gst_ref[...] = jnp.where(low_lanes, 0.0, gst).astype(bf16)
     gpar_ref[0:8] += fold(gst)
     gpar_ref[8:16] += fold(a * dt * glog)
     gpar_ref[16:24] += sum_skip
 
 
-def scan_backward(x, bc, st, seg, gy, y, h, tapx, tapbc, par, spread, skip, nseq):
+def spread_matrix(heads):
+    row = lax.broadcasted_iota(jnp.int32, (LANES, heads * WIDTH), 0)
+    col = lax.broadcasted_iota(jnp.int32, (LANES, heads * WIDTH), 1)
+    return (row % (LANES // 2) == col // WIDTH).astype(bf16)
+
+
+def on_lanes(v):
+    half = jnp.pad(v, [(0, 0)] * (v.ndim - 1) + [(0, LANES // 2 - v.shape[-1])])
+    return jnp.concatenate([half, half], axis=-1)
+
+
+MESH = pl.DeviceIdType.MESH
+
+
+def place():
+    dp, rank = lax.axis_index("dp"), lax.axis_index("tensor")
+    return dp // 2, dp % 2, rank
+
+
+def remote(src, dst, send, recv, dp, rank):
+    return pltpu.make_async_remote_copy(
+        src_ref=src, dst_ref=dst, send_sem=send, recv_sem=recv, device_id=(dp, rank),
+        device_id_type=MESH,
+    )
+
+
+def greet(chips, ranks):
+    chip, core, rank = place()
+    sem = pltpu.get_barrier_semaphore()
+    me = chip * 2 + core
+
+    def signal(dp, r):
+        pl.semaphore_signal(sem, inc=1, device_id=(dp, r), device_id_type=MESH)
+
+    signal(chip * 2 + 1 - core, rank)
+    for step in (1, -1):
+        @pl.when((chip + step >= 0) & (chip + step < chips))
+        def _():
+            signal(me + 2 * step, rank)
+    for k in range(1, ranks):
+        signal(me, lax.rem(rank + k, ranks))
+    pl.semaphore_wait(sem, ranks + (chip + chips - 1) // chips + (2 * chips - 2 - chip) // chips)
+
+
+def greet_all(chips, ranks):
+    chip, core, rank = place()
+    sem = pltpu.get_barrier_semaphore()
+    me, devices = chip * 2 + core, 2 * chips
+    for k in range(1, devices):
+        pl.semaphore_signal(
+            sem, inc=1, device_id=(lax.rem(me + k, devices), rank), device_id_type=MESH
+        )
+    for k in range(1, ranks):
+        pl.semaphore_signal(
+            sem, inc=1, device_id=(me, lax.rem(rank + k, ranks)), device_id_type=MESH
+        )
+    pl.semaphore_wait(sem, devices + ranks - 2)
+
+
+def slab(ref, index, rows):
+    return ref.at[pl.ds(pl.multiple_of(index * rows, rows), rows)]
+
+
+class LineGather:
+    def __init__(self, own, slots, send, recv, local, chips):
+        self.own, self.slots, self.send, self.recv, self.local = own, slots, send, recv, local
+        self.chips, self.rows = chips, own.shape[0]
+        self.chip, self.core, self.rank = place()
+        self.me = self.chip * 2 + self.core
+        self.partner = self.chip * 2 + 1 - self.core
+        self.steps = chips
+
+    @staticmethod
+    def scratch(chips):
+        n = 2 * chips
+        return [
+            pltpu.SemaphoreType.DMA((3, n)), pltpu.SemaphoreType.DMA((n,)), pltpu.SemaphoreType.DMA,
+        ]
+
+    def copy(self, way, origin, src=None):
+        target = (self.me + 2, self.me - 2, self.partner)[way]
+        slot = slab(self.slots, origin, self.rows)
+        return remote(
+            slot if src is None else src, slot, self.send.at[way, origin], self.recv.at[origin],
+            target, self.rank,
+        )
+
+    def pass_on(self, way, origin, src=None, wait=False):
+        def go():
+            copy = self.copy(way, origin, src)
+            copy.wait_send() if wait else copy.start()
+
+        if way == 0:
+            pl.when(self.chip + 1 < self.chips)(go)
+        elif way == 1:
+            pl.when(self.chip > 0)(go)
+        else:
+            go()
+
+    def keep(self):
+        return pltpu.make_async_copy(self.own, slab(self.slots, self.me, self.rows), self.local)
+
+    def sides(self, k):
+        return ((0, self.chip - k >= 0, -k), (1, self.chip + k < self.chips, k))
+
+    def step(self, k):
+        if k == 0:
+            for way in (0, 1, 2):
+                self.pass_on(way, self.me, self.own)
+            self.keep().start()
+            return
+        for way, there, shift in self.sides(k):
+            @pl.when(there)
+            def _():
+                origin = self.me + 2 * shift
+                self.copy(2, origin).wait_recv()
+                self.pass_on(way, origin)
+                self.pass_on(2, origin)
+
+    def arrive(self, k, use=None):
+        if k == 0:
+            self.keep().wait()
+            self.copy(2, self.partner).wait_recv()
+            if use is not None:
+                use(self.chip)
+            return
+        for way, there, shift in self.sides(k):
+            @pl.when(there)
+            def _():
+                self.copy(2, self.partner + 2 * shift).wait_recv()
+                if use is not None:
+                    use(self.chip + shift)
+
+    def sent(self):
+        for way in (0, 1, 2):
+            self.pass_on(way, self.me, self.own, wait=True)
+        for k in range(1, self.chips):
+            for way, there, shift in self.sides(k):
+                @pl.when(there)
+                def _():
+                    origin = self.me + 2 * shift
+                    self.pass_on(way, origin, wait=True)
+                    self.pass_on(2, origin, wait=True)
+
+    def finish(self):
+        for k in range(self.chips):
+            self.arrive(k)
+        self.sent()
+
+
+class TensorGather:
+    def __init__(self, own, slots, send, recv, local, ranks):
+        self.own, self.slots, self.send, self.recv, self.local = own, slots, send, recv, local
+        self.ranks, self.rows = ranks, own.shape[0]
+        chip, core, self.rank = place()
+        self.me = chip * 2 + core
+        self.steps = 2
+
+    @staticmethod
+    def scratch(ranks):
+        return [
+            pltpu.SemaphoreType.DMA((ranks,)), pltpu.SemaphoreType.DMA((ranks,)), pltpu.SemaphoreType.DMA,
+        ]
+
+    def near(self, k):
+        x = self.rank % 2
+        y = self.rank // 2
+        across = (y * 2 + 1 - x, (1 - y) * 2 + x)
+        if k < 2:
+            return remote(
+                self.own, slab(self.slots, self.rank, self.rows), self.send.at[k], self.recv.at[k],
+                self.me, across[k],
+            )
+        half = slab(self.slots, across[k - 2] * 2 + (k - 2), self.rows // 2)
+        return remote(half, half, self.send.at[k], self.recv.at[k], self.me, across[3 - k])
+
+    def direct(self, k):
+        return remote(
+            self.own, slab(self.slots, self.rank, self.rows), self.send.at[k], self.recv.at[k],
+            self.me, lax.rem(self.rank + k, self.ranks),
+        )
+
+    def keep(self):
+        return pltpu.make_async_copy(self.own, slab(self.slots, self.rank, self.rows), self.local)
+
+    def step(self, k):
+        if k == 0:
+            if self.ranks == 4:
+                self.near(0).start()
+                self.near(1).start()
+            else:
+                for j in range(1, self.ranks):
+                    self.direct(j).start()
+            self.keep().start()
+        elif self.ranks == 4:
+            for j in (0, 1):
+                self.near(j).wait_recv()
+                self.near(2 + j).start()
+
+    def finish(self):
+        self.keep().wait()
+        if self.ranks == 4:
+            for j in (0, 1):
+                self.near(j).wait_send()
+                self.near(2 + j).wait()
+        else:
+            for j in range(1, self.ranks):
+                self.direct(j).wait()
+
+
+def add_rows(target, others, out=None):
+    out = target if out is None else out
+    rows = target.shape[0]
+    some = 32 if rows % 32 == 0 else 16 if rows % 16 == 0 else 8
+
+    @pl.loop(0, rows // some)
+    def _(i):
+        at = pl.ds(pl.multiple_of(i * some, some), some)
+        total = target[at].astype(f32)
+        for other in others:
+            total = total + other[at].astype(f32)
+        out[at] = total.astype(out.dtype)
+
+
+class LineScatter:
+    def __init__(self, parts, out, mine, swap, up, down, send, recv, local, chips):
+        self.parts, self.out, self.mine, self.swap, self.up, self.down = parts, out, mine, swap, up, down
+        self.send, self.recv, self.local, self.chips = send, recv, local, chips
+        self.rows = parts.shape[0] // (2 * chips)
+        self.chip, self.core, self.rank = place()
+        self.me = self.chip * 2 + self.core
+        self.partner = self.chip * 2 + 1 - self.core
+        self.steps = chips
+
+    @staticmethod
+    def scratch(chips, shape, dtype=bf16):
+        block = (chips, shape[0] // (2 * chips)) + tuple(shape[1:])
+        return [pltpu.VMEM(block, dtype)] * 4 + [
+            pltpu.SemaphoreType.DMA((3, chips)), pltpu.SemaphoreType.DMA((3, chips)),
+            pltpu.SemaphoreType.DMA((chips,)),
+        ]
+
+    def order(self):
+        n = self.chips
+        return [c for k in range(n // 2) for c in (n - 1 - k, k)]
+
+    def over(self, c):
+        return remote(
+            slab(self.parts, 2 * c + 1 - self.core, self.rows), self.swap.at[c], self.send.at[2, c],
+            self.recv.at[2, c], self.partner, self.rank,
+        )
+
+    def load(self, c):
+        return pltpu.make_async_copy(
+            slab(self.parts, 2 * c + self.core, self.rows), self.mine.at[c], self.local.at[c]
+        )
+
+    def along(self, way, c, first=False):
+        buffer = (self.up, self.down)[way]
+        src = self.mine.at[c] if first else buffer.at[c]
+        return remote(
+            src, buffer.at[c], self.send.at[way, c], self.recv.at[way, c],
+            self.me + (2, -2)[way], self.rank,
+        )
+
+    def step(self, k):
+        n, chip = self.chips, self.chip
+        if k == 0:
+            for c in self.order():
+                self.over(c).start()
+                self.load(c).start()
+            return
+        if k == 1:
+            for c in self.order():
+                self.over(c).wait()
+                self.load(c).wait()
+                add_rows(self.mine.at[c], [self.swap.at[c]])
+
+                @pl.when((chip == 0) & (c > 0))
+                def _():
+                    self.along(0, c, True).start()
+
+                @pl.when((chip == n - 1) & (c < n - 1))
+                def _():
+                    self.along(1, c, True).start()
+            return
+        t = k - 1
+        c = n - 1 - (t - chip)
+
+        @pl.when((chip > 0) & (t >= chip) & (c > chip))
+        def _():
+            self.along(0, c).wait_recv()
+            add_rows(self.up.at[c], [self.mine.at[c]])
+            self.along(0, c).start()
+
+        d = t - (n - 1 - chip)
+
+        @pl.when((chip < n - 1) & (d >= 0) & (d < chip))
+        def _():
+            self.along(1, d).wait_recv()
+            add_rows(self.down.at[d], [self.mine.at[d]])
+            self.along(1, d).start()
+
+    def finish(self):
+        n, chip = self.chips, self.chip
+        out, mine, up, down = self.out, self.mine.at[chip], self.up.at[chip], self.down.at[chip]
+
+        @pl.when(chip == 0)
+        def _():
+            self.along(1, chip).wait_recv()
+            add_rows(mine, [down], out)
+
+        @pl.when(chip == n - 1)
+        def _():
+            self.along(0, chip).wait_recv()
+            add_rows(mine, [up], out)
+
+        @pl.when((chip > 0) & (chip < n - 1))
+        def _():
+            self.along(0, chip).wait_recv()
+            self.along(1, chip).wait_recv()
+            add_rows(mine, [up, down], out)
+
+        for c in range(n):
+            @pl.when((chip < n - 1) & (c > chip))
+            def _():
+                self.along(0, c).wait_send()
+
+            @pl.when((chip > 0) & (c < chip))
+            def _():
+                self.along(1, c).wait_send()
+
+
+class TensorScatter:
+    def __init__(self, parts, land, send, recv, local, ranks):
+        self.parts, self.land = parts, land
+        self.send, self.recv, self.local, self.ranks = send, recv, local, ranks
+        self.rows = parts.shape[0] // ranks
+        chip, core, self.rank = place()
+        self.me = chip * 2 + core
+        self.steps = 1
+
+    @staticmethod
+    def scratch(ranks, shape):
+        return [
+            pltpu.VMEM((ranks, shape[0] // ranks, shape[1]), bf16),
+            pltpu.SemaphoreType.DMA((ranks,)), pltpu.SemaphoreType.DMA((ranks,)),
+            pltpu.SemaphoreType.DMA,
+        ]
+
+    def load(self):
+        return pltpu.make_async_copy(
+            slab(self.parts, self.rank, self.rows), self.land.at[0], self.local
+        )
+
+    def copy(self, k):
+        to = lax.rem(self.rank + k, self.ranks)
+        return remote(
+            slab(self.parts, to, self.rows), self.land.at[k], self.send.at[k], self.recv.at[k],
+            self.me, to,
+        )
+
+    def step(self, k):
+        for j in range(1, self.ranks):
+            self.copy(j).start()
+        self.load().start()
+
+    def arrive(self):
+        self.load().wait()
+        for j in range(1, self.ranks):
+            self.copy(j).wait()
+
+    def total(self, at):
+        total = self.land[0, at].astype(f32)
+        for j in range(1, self.ranks):
+            total = total + self.land[j, at].astype(f32)
+        return total
+
+
+def row_loop(rows, some, body):
+    @pl.loop(0, rows // some)
+    def _(i):
+        body(pl.ds(pl.multiple_of(i * some, some), some))
+
+
+def params(number):
+    return pltpu.CompilerParams(
+        collective_id=number, has_side_effects=True, vmem_limit_bytes=VMEM_BYTES
+    )
+
+
+ANY = pl.BlockSpec(memory_space=pl.ANY)
+ONCHIP = pl.BlockSpec(memory_space=pltpu.VMEM)
+
+
+epsilon = 1e-05
+CHUNK = 256
+
+
+def shaped(shape, dtype):
+    return jax.ShapeDtypeStruct(shape, dtype)
+
+
+def dma(count=None):
+    return pltpu.SemaphoreType.DMA if count is None else pltpu.SemaphoreType.DMA((count,))
+
+
+def project_kernel(
+    chips, ranks, res_ref, gain_ref, ws_ref, wx_own, x_ref, st_ref, bc_ref, normed_out, wx_out,
+    own, normed, wx, *sems
+):
+    greet(chips, ranks)
+    line = LineGather(wx_own, wx, *sems[:3], chips)
+    tensor = TensorGather(own, normed, *sems[3:6], ranks)
+    line.step(0)
+    gain = gain_ref[...]
+
+    def norm(at):
+        v = res_ref[at].astype(f32)
+        scaling = lax.rsqrt(jnp.mean(v * v, axis=1, keepdims=True) + epsilon)
+        own[at] = (v * scaling * gain).astype(bf16)
+
+    row_loop(own.shape[0], 32, norm)
+    tensor.step(0)
+    line.step(1)
+    tensor.step(1)
+    if chips > 2:
+        line.step(2)
+    tensor.finish()
+    keep_normed = pltpu.make_async_copy(normed, normed_out, sems[6])
+    keep_normed.start()
+    tokens, width = x_ref.shape
+    deep = 2 * line.rows
+
+    def states(at):
+        bc_ref[at] = mm(normed[at], ws_ref[...])
+
+    row_loop(tokens, CHUNK, states)
+
+    def use(first, chip):
+        ks = pl.ds(pl.multiple_of(chip * deep, deep), deep)
+
+        def rows(at):
+            left = normed[at, ks]
+            x, st = mm(left, wx[ks, :width]), mm(left, wx[ks, width:])
+            if first:
+                x_ref[at], st_ref[at] = x, st
+            else:
+                x_ref[at] += x
+                st_ref[at] += st
+
+        row_loop(tokens, CHUNK, rows)
+
+    line.arrive(0, functools.partial(use, True))
+    line.arrive(1, functools.partial(use, False))
+    for k in range(2, chips):
+        if k + 1 < chips:
+            line.step(k + 1)
+        line.arrive(k, functools.partial(use, False))
+    keep_wx = pltpu.make_async_copy(wx, wx_out, sems[7])
+    keep_wx.start()
+    line.sent()
+    keep_normed.wait()
+    keep_wx.wait()
+
+
+def project(number, chips, ranks, residual, norm_gain, ws, wx_own):
+    rows, model = residual.shape
+    tokens, width = rows * ranks, wx_own.shape[1]
+    return pl.pallas_call(
+        functools.partial(project_kernel, chips, ranks),
+        in_specs=[ONCHIP, ONCHIP, ONCHIP, ANY],
+        out_specs=[ONCHIP, ONCHIP, ONCHIP, ANY, ANY],
+        out_shape=[
+            shaped((tokens, width - LANES), f32), shaped((tokens, LANES), f32),
+            shaped((tokens, ws.shape[1]), f32), shaped((tokens, model), bf16),
+            shaped((model, width), bf16),
+        ],
+        scratch_shapes=[
+            pltpu.VMEM((rows, model), bf16), pltpu.VMEM((tokens, model), bf16),
+            pltpu.VMEM((model, width), bf16),
+            *LineGather.scratch(chips), *TensorGather.scratch(ranks), dma(), dma(),
+        ],
+        compiler_params=params(number),
+        name="project",
+    )(residual, norm_gain, ws, wx_own)
+
+
+def scan_gather_kernel(blocks, total, chips, ranks, *refs):
+    own, (wz_own, cot_own) = refs[:9], refs[9:11]
+    outs, (wz_out, cot_out) = refs[11:13], refs[13:15]
+    scratch, sems = refs[15:19], refs[19:]
+    now = pl.program_id(0) * blocks + pl.program_id(1)
+    line = LineGather(wz_own, wz_out, *sems[:3], chips)
+    tensor = TensorGather(cot_own, cot_out, *sems[3:], ranks)
+
+    @pl.when(now == 0)
+    def _():
+        greet(chips, ranks)
+        line.step(0)
+        tensor.step(0)
+
+    @pl.when(now == total - 2)
+    def _():
+        line.step(1)
+
+    scan_fwd_kernel(blocks, *own, *outs, *scratch)
+
+    @pl.when(now == total - 1)
+    def _():
+        tensor.step(1)
+        for k in range(2, chips):
+            line.step(k)
+        line.finish()
+        tensor.finish()
+
+
+def scan_forward_gather(
+    number, chips, ranks, wz_own, cot_own, x, bc, st, seg, tapx, tapbc, par, spread, skip, nseq
+):
     tokens, width = x.shape
+    n = BLOCK
+    blocks = tokens // nseq // n
+    at = lambda s, i: (s * blocks + i, 0)
+    whole = lambda s, i: (0, 0)
+    states = LANES
+    return pl.pallas_call(
+        functools.partial(scan_gather_kernel, blocks, nseq * blocks, chips, ranks),
+        grid=(nseq, blocks),
+        in_specs=[
+            pl.BlockSpec((n, width), at),
+            pl.BlockSpec((n, 2 * states), at),
+            pl.BlockSpec((n, LANES), at),
+            pl.BlockSpec((n, LANES), at),
+            pl.BlockSpec(tapx.shape, whole),
+            pl.BlockSpec(tapbc.shape, whole),
+            pl.BlockSpec(par.shape, whole),
+            pl.BlockSpec(spread.shape, whole),
+            pl.BlockSpec(skip.shape, whole),
+            ANY,
+            ANY,
+        ],
+        out_specs=[
+            pl.BlockSpec((n, width), at), pl.BlockSpec((states, width), at), ANY, ANY,
+        ],
+        out_shape=[
+            shaped((tokens, width), f32),
+            shaped((tokens // n * states, width), bf16),
+            shaped((wz_own.shape[0] * 2 * chips, width), bf16),
+            shaped((tokens, cot_own.shape[1]), bf16),
+        ],
+        scratch_shapes=[
+            pltpu.VMEM((states, width), f32),
+            pltpu.VMEM((8, width), f32),
+            pltpu.VMEM((8, 2 * states), f32),
+            pltpu.VMEM((8, LANES), jnp.int32),
+            *LineGather.scratch(chips), *TensorGather.scratch(ranks),
+        ],
+        compiler_params=params(number),
+        name="scan_forward",
+    )(x, bc, st, seg, tapx, tapbc, par, spread, skip, wz_own, cot_own)
+
+
+def lane_sums(v):
+    total = v[:, :LANES]
+    for i in range(LANES, v.shape[1], LANES):
+        total = total + v[:, i : i + LANES]
+    return total
+
+
+def row_sums(picks, v):
+    high = v.astype(bf16)
+    low = (v - high.astype(f32)).astype(bf16)
+    return mm_nt(picks, high) + mm_nt(picks, low)
+
+
+def gate_kernel(
+    chips, ranks, gain_ref, wo_own, normed_in, wz_in, y_in, cot_in,
+    gz_ref, gy_ref, ng_ref, ggain_ref, wo_out,
+    wo, normed, wz, y, cot, z, gng, squares, dots, columns, land, send, recv, loads, *sems
+):
+    line = LineGather(wo_own, wo, *sems[:3], chips)
+    tokens, width = y.shape
+    inner = width * ranks
+    rank = line.rank
+    load = [
+        pltpu.make_async_copy(src, dst, loads.at[i])
+        for i, (src, dst) in enumerate(((normed_in, normed), (wz_in, wz), (y_in, y), (cot_in, cot)))
+    ]
+    greet(chips, ranks)
+    line.step(0)
+    for copy in load:
+        copy.start()
+    load[0].wait()
+    load[1].wait()
+
+    def gate(at):
+        z[at] = mm(normed[at], wz[...])
+
+    row_loop(tokens, CHUNK, gate)
+    load[2].wait()
+    load[3].wait()
+    deep = 2 * line.rows
+
+    def use(first, chip):
+        ks = pl.ds(pl.multiple_of(chip * deep, deep), deep)
+
+        def rows(at):
+            v = mm(cot[at, ks], wo[ks])
+            if first:
+                gng[at] = v
+            else:
+                gng[at] += v
+
+        row_loop(tokens, CHUNK, rows)
+
+    line.arrive(0, functools.partial(use, True))
+    for k in range(1, chips):
+        line.step(k)
+        line.arrive(k, functools.partial(use, False))
+    keep = pltpu.make_async_copy(wo, wo_out, loads.at[4])
+    keep.start()
+    gain = gain_ref[0:1]
+
+    def sums(at):
+        zz = z[at]
+        gated = y[at] * (zz * sigmoid(zz))
+        squares[at] = lane_sums(gated * gated)
+        dots[at] = lane_sums(gng[at] * gain * gated)
+
+    row_loop(tokens, 16, sums)
+    half = lax.broadcasted_iota(jnp.int32, (8, LANES), 0) < 4
+    one, other = half.astype(bf16), jnp.logical_not(half).astype(bf16)
+    for r in range(0, tokens, CHUNK):
+        at = slice(r, r + CHUNK)
+        land[rank, :, at] = row_sums(one, squares[at]) + row_sums(other, dots[at])
+    copies = [
+        remote(
+            land.at[rank], land.at[rank], send.at[k], recv.at[k], line.me, lax.rem(rank + k, ranks)
+        )
+        for k in range(1, ranks)
+    ]
+    for copy in copies:
+        copy.start()
+    line.sent()
+    for copy in copies:
+        copy.wait()
+    for r in range(0, tokens, LANES):
+        at = slice(r, r + LANES)
+        total = land[0, :, at]
+        for k in range(1, ranks):
+            total = total + land[k, :, at]
+        columns[at] = jnp.transpose(jnp.concatenate([total] * (LANES // 8), axis=0))
+    ggain_ref[...] = jnp.zeros_like(ggain_ref)
+
+    def grads(at):
+        zz, yy, gg = z[at], y[at], gng[at]
+        sig = sigmoid(zz)
+        silu = zz * sig
+        gated = yy * silu
+        scale = lax.rsqrt(columns[at, 0:1] / inner + epsilon)
+        ng_ref[at] = (gated * scale * gain).astype(bf16)
+        weight = scale * scale * scale * columns[at, 4:5] / inner
+        ggain_ref[...] += fold(gg * gated * scale)
+        grad = scale * gain * gg - gated * weight
+        gz_ref[at] = (grad * yy * (sig * (1.0 + zz * (1.0 - sig)))).astype(bf16)
+        gy_ref[at] = grad * silu
+
+    row_loop(tokens, 16, grads)
+    keep.wait()
+
+
+def gate(number, chips, ranks, gain, wo_own, normed, wz, y, cot):
+    tokens, width = y.shape
+    model = normed.shape[1]
+    return pl.pallas_call(
+        functools.partial(gate_kernel, chips, ranks),
+        in_specs=[ONCHIP] + [ANY] * 5,
+        out_specs=[ONCHIP] * 4 + [ANY],
+        out_shape=[
+            shaped((tokens, width), bf16), shaped((tokens, width), f32), shaped((tokens, width), bf16),
+            shaped((8, width), f32), shaped((model, width), bf16),
+        ],
+        scratch_shapes=[
+            pltpu.VMEM((model, width), bf16), pltpu.VMEM((tokens, model), bf16),
+            pltpu.VMEM((model, width), bf16), pltpu.VMEM((tokens, width), f32),
+            pltpu.VMEM((tokens, model), bf16), pltpu.VMEM((tokens, width), f32),
+            pltpu.VMEM((tokens, width), f32), pltpu.VMEM((tokens, LANES), f32),
+            pltpu.VMEM((tokens, LANES), f32), pltpu.VMEM((tokens, LANES), f32),
+            pltpu.VMEM((ranks, 8, tokens), f32), dma(ranks), dma(ranks), dma(5),
+            *LineGather.scratch(chips),
+        ],
+        compiler_params=params(number),
+        name="gate",
+    )(gain, wo_own, normed, wz, y, cot)
+
+
+def stream_grads(src, grad, parts, wide, cbuf, stage, csem, ssem):
+    count = src.shape[1] // CHUNK
+
+    def load(j):
+        slot = lax.rem(j, 2)
+        columns = pl.ds(pl.multiple_of(j * CHUNK, CHUNK), CHUNK)
+        return pltpu.make_async_copy(src.at[:, columns], cbuf.at[slot], csem.at[slot])
+
+    def store(j):
+        slot = lax.rem(j, 2)
+        return pltpu.make_async_copy(
+            stage.at[slot, :, pl.ds(0, wide)], slab(parts, j, CHUNK), ssem.at[slot]
+        )
+
+    load(0).start()
+
+    @pl.loop(0, count)
+    def _(j):
+        slot = lax.rem(j, 2)
+
+        @pl.when(j + 1 < count)
+        def _():
+            load(j + 1).start()
+
+        load(j).wait()
+
+        @pl.when(j >= 2)
+        def _():
+            store(j - 2).wait()
+
+        stage[slot, :, :wide] = mm_tn(cbuf[slot], grad[...]).astype(bf16)
+        store(j).start()
+
+    for j in (count - 2, count - 1):
+        store(j).wait()
+
+
+def stream_back(terms, kept, parts, stage, ssem):
+    tokens, model = parts.shape
+    count = model // CHUNK
+
+    def loads(j):
+        slot = lax.rem(j, 2)
+        return [
+            pltpu.make_async_copy(slab(right, j, CHUNK), buffer.at[slot], sem.at[slot])
+            for _, right, buffer, sem in terms
+        ]
+
+    def store(j):
+        slot = lax.rem(j, 2)
+        columns = pl.ds(pl.multiple_of(j * CHUNK, CHUNK), CHUNK)
+        return pltpu.make_async_copy(stage.at[slot], parts.at[:, columns], ssem.at[slot])
+
+    for copy in loads(0):
+        copy.start()
+
+    @pl.loop(0, count)
+    def _(j):
+        slot = lax.rem(j, 2)
+
+        @pl.when(j + 1 < count)
+        def _():
+            for copy in loads(j + 1):
+                copy.start()
+
+        for copy in loads(j):
+            copy.wait()
+
+        @pl.when(j >= 2)
+        def _():
+            store(j - 2).wait()
+
+        for r in range(0, tokens, CHUNK):
+            at = slice(r, r + CHUNK)
+            total = jnp.zeros((CHUNK, CHUNK), f32)
+            for left, _, buffer, _ in terms:
+                total = total + mm_nt(left[at], buffer[slot])
+            for left, right in kept:
+                total = total + mm_nt(left[at], right[pl.ds(pl.multiple_of(j * CHUNK, CHUNK), CHUNK)])
+            stage[slot, at] = total.astype(bf16)
+        store(j).start()
+
+    for j in (count - 2, count - 1):
+        store(j).wait()
+
+
+def backward_kernel(blocks, total, chips, ranks, *refs):
+    ins, refs = refs[:15], refs[15:]
+    (res_ref, ws_ref, ggain_ref, gz_in, ng_in, normed_in, cot_in, wo_in, wz_in, wx_in), refs = refs[:10], refs[10:]
+    (z_sum, o_sum, block_out, pack_ref, xparts, tparts, sparts, zparts, oparts, pparts, gbc_slots), refs = refs[:11], refs[11:]
+    scratch, refs = refs[:4], refs[4:]
+    (gxs, gbc_own, gtapx, gtapbc, gpar, gz, ng, cbuf, stage, back, wbuf, xbuf, gbc_sum, state_stage), refs = refs[:14], refs[14:]
+    (loads, csem, ssem, bsem, wsem, xsem), refs = refs[:6], refs[6:]
+    job0 = LineScatter(zparts, z_sum, *refs[:7], chips)
+    job1 = LineScatter(oparts, o_sum, *refs[7:14], chips)
+    across = TensorScatter(pparts, *refs[14:18], ranks)
+    around = TensorGather(gbc_own, gbc_slots, *refs[18:], ranks)
+    now = pl.program_id(0) * blocks + pl.program_id(1)
+    tokens, width = gz.shape
+    rank = across.rank
+
+    @pl.when(now == 0)
+    def _():
+        fetch = [
+            pltpu.make_async_copy(gz_in, gz, loads.at[0]),
+            pltpu.make_async_copy(ng_in, ng, loads.at[1]),
+        ]
+        for copy in fetch:
+            copy.start()
+        greet(chips, ranks)
+        fetch[0].wait()
+        stream_grads(normed_in, gz, zparts, width, cbuf, stage, csem, ssem)
+        job0.step(0)
+        fetch[1].wait()
+        stream_back([(ng, wo_in, wbuf, wsem)], [], pparts, back, bsem)
+        across.step(0)
+        job0.step(1)
+        stream_grads(cot_in, ng, oparts, width, cbuf, stage, csem, ssem)
+        job1.step(0)
+
+    early = [k for k in range(2, chips) if 2 * k - 3 < total - 1]
+
+    @pl.when(now == 1)
+    def _():
+        job1.step(1)
+
+    for k in early:
+        @pl.when(now == 2 * k - 3)
+        def _():
+            job0.step(k)
+
+    @pl.when(now == total - 1)
+    def _():
+        if chips > 2:
+            job1.step(2)
+
+    row = pl.multiple_of(
+        (pl.program_id(0) * blocks + blocks - 1 - pl.program_id(1)) * BLOCK, BLOCK
+    )
+    here = pl.ds(row, BLOCK)
+    outs = (
+        gxs.at[here, pl.ds(0, width)], gbc_own.at[here], gxs.at[here, pl.ds(width, LANES)],
+        gtapx, gtapbc, gpar,
+    )
+    scan_bwd_kernel(blocks, *ins, *outs, *scratch)
+
+    @pl.when(now == total - 1)
+    def _():
+        around.step(0)
+        stream_grads(normed_in, gxs, xparts, width + LANES, cbuf, stage, csem, ssem)
+        around.step(1)
+        for k in range(2, chips):
+            if k not in early:
+                job0.step(k)
+        for k in range(3, chips):
+            job1.step(k)
+        stream_back(
+            [(gz, wz_in, wbuf, wsem), (gxs, wx_in, xbuf, xsem)], [(gbc_own, ws_ref)], tparts, back, bsem
+        )
+        around.finish()
+        for r in range(ranks):
+            copy = pltpu.make_async_copy(slab(gbc_slots, r, tokens), cbuf.at[r % 2], csem.at[r % 2])
+            copy.start()
+            copy.wait()
+
+            def add(at):
+                v = cbuf[r % 2, at].astype(f32)
+                gbc_sum[at] = v if r == 0 else gbc_sum[at] + v
+
+            row_loop(tokens, 64, add)
+
+        def rounded(at):
+            gbc_own[at] = gbc_sum[at].astype(bf16)
+
+        row_loop(tokens, 64, rounded)
+        depth = sparts.shape[0]
+        for i in range(depth // CHUNK):
+            columns = pl.ds(pl.multiple_of(rank * depth + i * CHUNK, CHUNK), CHUNK)
+            copy = pltpu.make_async_copy(normed_in.at[:, columns], cbuf.at[0], csem.at[0])
+            copy.start()
+            copy.wait()
+            state_stage[...] = mm_tn(cbuf[0], gbc_own[...])
+            copy = pltpu.make_async_copy(state_stage, sparts.at[pl.ds(i * CHUNK, CHUNK)], csem.at[1])
+            copy.start()
+            copy.wait()
+        pack_ref[...] = jnp.zeros_like(pack_ref)
+        for k in range(5):
+            rows = slice(8 * k, 8 * k + 8)
+            pack_ref[k : k + 1, :width] = jnp.sum(gtapx[rows], axis=0, keepdims=True)
+            pack_ref[k : k + 1, width:] = jnp.sum(gtapbc[rows], axis=0, keepdims=True)
+        pack_ref[5:6, :width] = jnp.sum(ggain_ref[...], axis=0, keepdims=True)
+        for k in range(3):
+            pack_ref[6:7, k * LANES : (k + 1) * LANES] = jnp.sum(
+                gpar[8 * k : 8 * k + 8], axis=0, keepdims=True
+            )
+        across.arrive()
+
+        def residual(at):
+            block_out[at] = res_ref[at].astype(f32) + across.total(at)
+
+        row_loop(across.rows, 16, residual)
+        job0.finish()
+        job1.finish()
+
+
+def backward(
+    number, chips, ranks, residual, ws, ggain, gz, ng, normed, cot, wo, wz, wx,
+    x, bc, st, seg, gy, y, h, tapx, tapbc, par, spread, skip, nseq,
+):
+    tokens, width = x.shape
+    model = normed.shape[1]
     n = BLOCK
     blocks = tokens // nseq // n
     at = lambda s, i: (s * blocks + blocks - 1 - i, 0)
     tail = lambda s, i: (jnp.maximum((s * blocks + blocks - 1 - i) * (n // 8) - 1, 0), 0)
     whole = lambda s, i: (0, 0)
     states = LANES
+    full = lambda v: pl.BlockSpec(v.shape, whole)
+    once = lambda shape: pl.BlockSpec(shape, whole)
+    own = model // (2 * chips)
+    depth = model // ranks
     return pl.pallas_call(
-        functools.partial(scan_bwd_kernel, blocks),
+        functools.partial(backward_kernel, blocks, nseq * blocks, chips, ranks),
         grid=(nseq, blocks),
         in_specs=[
             pl.BlockSpec((n, width), at),
@@ -349,59 +1219,194 @@
             pl.BlockSpec((n, width), at),
             pl.BlockSpec((n, width), at),
             pl.BlockSpec((states, width), at),
-            pl.BlockSpec(tapx.shape, whole),
-            pl.BlockSpec(tapbc.shape, whole),
-            pl.BlockSpec(par.shape, whole),
-            pl.BlockSpec(spread.shape, whole),
-            pl.BlockSpec(skip.shape, whole),
-        ],
+            full(tapx), full(tapbc), full(par), full(spread), full(skip),
+            full(residual), full(ws), full(ggain),
+        ]
+        + [ANY] * 7,
         out_specs=[
-            pl.BlockSpec((n, width), at),
-            pl.BlockSpec((n, 2 * states), at),
-            pl.BlockSpec((n, LANES), at),
-            pl.BlockSpec((40, width), whole),
-            pl.BlockSpec((40, 2 * states), whole),
-            pl.BlockSpec((24, LANES), whole),
-        ],
+            once((own, width)), once((own, width)), once(residual.shape), once((8, width + 2 * states)),
+        ]
+        + [ANY] * 7,
         out_shape=[
-            jax.ShapeDtypeStruct((tokens, width), bf16),
-            jax.ShapeDtypeStruct((tokens, 2 * states), f32),
-            jax.ShapeDtypeStruct((tokens, LANES), bf16),
-            jax.ShapeDtypeStruct((40, width), f32),
-            jax.ShapeDtypeStruct((40, 2 * states), f32),
-            jax.ShapeDtypeStruct((24, LANES), f32),
+            shaped((own, width), f32), shaped((own, width), f32), shaped(residual.shape, f32),
+            shaped((8, width + 2 * states), f32),
+            shaped((model, width + LANES), bf16), shaped((tokens, model), bf16),
+            shaped((depth, 2 * states), f32),
+            shaped((model, width), bf16), shaped((model, width), bf16), shaped((tokens, model), bf16),
+            shaped((ranks * tokens, 2 * states), bf16),
         ],
         scratch_shapes=[
             pltpu.VMEM((states, width), f32),
             pltpu.VMEM((8, width), f32),
             pltpu.VMEM((8, 2 * states), f32),
             pltpu.VMEM((8, LANES), jnp.int32),
+            pltpu.VMEM((tokens, width + LANES), bf16),
+            pltpu.VMEM((tokens, 2 * states), bf16),
+            pltpu.VMEM((40, width), f32),
+            pltpu.VMEM((40, 2 * states), f32),
+            pltpu.VMEM((24, LANES), f32),
+            pltpu.VMEM((tokens, width), bf16),
+            pltpu.VMEM((tokens, width), bf16),
+            pltpu.VMEM((2, tokens, CHUNK), bf16),
+            pltpu.VMEM((2, CHUNK, width + LANES), bf16),
+            pltpu.VMEM((2, tokens, CHUNK), bf16),
+            pltpu.VMEM((2, CHUNK, width), bf16),
+            pltpu.VMEM((2, CHUNK, width + LANES), bf16),
+            pltpu.VMEM((tokens, 2 * states), f32),
+            pltpu.VMEM((CHUNK, 2 * states), f32),
+            *[dma(2)] * 6,
+            *LineScatter.scratch(chips, (model, width)),
+            *LineScatter.scratch(chips, (model, width)),
+            *TensorScatter.scratch(ranks, (tokens, model)),
+            *TensorGather.scratch(ranks),
         ],
-        compiler_params=pltpu.CompilerParams(vmem_limit_bytes=VMEM_BYTES),
-        cost_estimate=pl.CostEstimate(
-            flops=tokens * width * 3000, bytes_accessed=tokens * width * 20, transcendentals=0
-        ),
-        name="scan_backward",
-    )(x, x, bc, bc, st, seg, seg, gy, y, h, tapx, tapbc, par, spread, skip)
-
-
-def spread_matrix(heads):
-    row = lax.broadcasted_iota(jnp.int32, (LANES, heads * WIDTH), 0)
-    col = lax.broadcasted_iota(jnp.int32, (LANES, heads * WIDTH), 1)
-    return (row % (LANES // 2) == col // WIDTH).astype(bf16)
-
-
-def on_lanes(v):
-    half = jnp.pad(v, [(0, 0)] * (v.ndim - 1) + [(0, LANES // 2 - v.shape[-1])])
-    return jnp.concatenate([half, half], axis=-1)
-
-
-epsilon = 1e-05
-
-
-def placed_at(whole, piece, offset):
-    start = (0,) * (len(whole) - 1) + (offset,)
-    return lax.dynamic_update_slice(jnp.zeros(whole, piece.dtype), piece, start)
+        compiler_params=params(number),
+        name="backward",
+    )(
+        x, x, bc, bc, st, seg, seg, gy, y, h, tapx, tapbc, par, spread, skip,
+        residual, ws, ggain, gz, ng, normed, cot, wo, wz, wx,
+    )
+
+
+def everyone(buffer, mine, count, send, recv, device):
+    row = buffer.at[mine]
+    return [
+        remote(row, row, send.at[k], recv.at[k], *device(lax.rem(mine + k, count)))
+        for k in range(1, count)
+    ]
+
+
+def added(buffer, count):
+    total = buffer[0]
+    for k in range(1, count):
+        total = total + buffer[k]
+    return total
+
+
+def finish_kernel(chips, ranks, *refs):
+    (pack_ref, res_ref, cot_ref, gain_ref, xparts, tparts, sparts), refs = refs[:7], refs[7:]
+    (x_ref, out_ref, state_ref, sums_ref, norm_ref), refs = refs[:5], refs[5:]
+    (state_own, state_line, state_low, state_all, land_dp, land_rank, norm_rank, norm_dp, norm_acc), refs = refs[:9], refs[9:]
+    (psend, precv, qsend, qrecv, nsend, nrecv, msend, mrecv), refs = refs[:8], refs[8:]
+    x_job = LineScatter(xparts, x_ref, *refs[:7], chips)
+    s_job = LineScatter(sparts, state_own, *refs[7:14], chips)
+    across = TensorScatter(tparts, *refs[14:18], ranks)
+    s_line = LineGather(state_own, state_line, *refs[18:21], chips)
+    s_rank = TensorGather(state_low, state_all, *refs[21:24], ranks)
+    me, rank, devices = x_job.me, x_job.rank, 2 * chips
+    over_dp = lambda d: (d, rank)
+    over_rank = lambda r: (me, r)
+    width = x_ref.shape[1] - LANES
+    greet_all(chips, ranks)
+    s_job.step(0)
+    x_job.step(0)
+    across.step(0)
+    land_dp[me] = pack_ref[...]
+    first = everyone(land_dp, me, devices, psend, precv, over_dp)
+    for copy in first:
+        copy.start()
+    s_job.step(1)
+    x_job.step(1)
+    for copy in first:
+        copy.wait()
+    land_rank[rank] = added(land_dp, devices)
+    second = everyone(land_rank, rank, ranks, qsend, qrecv, over_rank)
+    for copy in second:
+        copy.start()
+    for k in range(2, chips):
+        s_job.step(k)
+        x_job.step(k)
+    s_job.finish()
+    for k in range(chips):
+        s_line.step(k)
+    s_line.finish()
+
+    def lower(at):
+        state_low[at] = state_line[at].astype(bf16)
+
+    row_loop(state_low.shape[0], 64, lower)
+    s_rank.step(0)
+    for copy in second:
+        copy.wait()
+    shared = land_rank[0, :, width:]
+    for r in range(1, ranks):
+        shared = shared + land_rank[r, :, width:]
+    for r in range(ranks):
+        sums_ref[:, r * width : (r + 1) * width] = land_rank[r, :, :width]
+    sums_ref[:, ranks * width :] = shared
+    across.arrive()
+    norm_acc[...] = jnp.zeros_like(norm_acc)
+    gain = gain_ref[...]
+    model = gain.shape[1]
+
+    def last(at):
+        grad = across.total(at)
+        v = res_ref[at].astype(f32)
+        scaling = lax.rsqrt(jnp.mean(v * v, axis=1, keepdims=True) + epsilon)
+        norm_acc[...] += fold(grad * v * scaling)
+        grad = grad * gain
+        along = jnp.sum(grad * v, axis=1, keepdims=True)
+        weight = scaling * scaling * scaling * along / model
+        out_ref[at] = cot_ref[at].astype(f32) + scaling * grad - v * weight
+
+    row_loop(across.rows, 16, last)
+    row = jnp.sum(norm_acc[...], axis=0, keepdims=True)
+    eighth = model // 8
+    for i in range(8):
+        norm_rank[rank, i : i + 1, :] = row[:, i * eighth : (i + 1) * eighth]
+    third = everyone(norm_rank, rank, ranks, nsend, nrecv, over_rank)
+    for copy in third:
+        copy.start()
+    s_rank.step(1)
+    for copy in third:
+        copy.wait()
+    norm_dp[me] = added(norm_rank, ranks)
+    fourth = everyone(norm_dp, me, devices, msend, mrecv, over_dp)
+    for copy in fourth:
+        copy.start()
+    x_job.finish()
+    s_rank.finish()
+
+    def state(at):
+        state_ref[at] = state_all[at].astype(f32)
+
+    row_loop(state_ref.shape[0], 64, state)
+    for copy in fourth:
+        copy.wait()
+    norm_ref[...] = added(norm_dp, devices)
+
+
+def finish(number, chips, ranks, pack, residual, cot, norm_gain, xparts, tparts, sparts):
+    rows, model = residual.shape
+    devices = 2 * chips
+    own = model // devices
+    depth, states = sparts.shape
+    wide = pack.shape[1]
+    width = wide - states
+    return pl.pallas_call(
+        functools.partial(finish_kernel, chips, ranks),
+        in_specs=[ONCHIP] * 4 + [ANY] * 3,
+        out_specs=[ONCHIP] * 5,
+        out_shape=[
+            shaped((own, xparts.shape[1]), f32), shaped((rows, model), f32), shaped((model, states), f32),
+            shaped((8, width * ranks + states), f32), shaped((8, model // 8), f32),
+        ],
+        scratch_shapes=[
+            pltpu.VMEM((depth // devices, states), f32), pltpu.VMEM((depth, states), f32),
+            pltpu.VMEM((depth, states), bf16), pltpu.VMEM((model, states), bf16),
+            pltpu.VMEM((devices, 8, wide), f32), pltpu.VMEM((ranks, 8, wide), f32),
+            pltpu.VMEM((ranks, 8, model // 8), f32), pltpu.VMEM((devices, 8, model // 8), f32),
+            pltpu.VMEM((8, model), f32),
+            dma(devices), dma(devices), dma(ranks), dma(ranks),
+            dma(ranks), dma(ranks), dma(devices), dma(devices),
+            *LineScatter.scratch(chips, xparts.shape),
+            *LineScatter.scratch(chips, sparts.shape, f32),
+            *TensorScatter.scratch(ranks, tparts.shape),
+            *LineGather.scratch(chips), *TensorGather.scratch(ranks),
+        ],
+        compiler_params=params(number),
+        name="finish",
+    )(pack, residual, cot, norm_gain, xparts, tparts, sparts)
 
 
 def per_device(
@@ -409,23 +1414,13 @@
     conv_bias, step_bias, decay_log, skip_gain, gated_gain, out_weight, cotangent,
 ):
     rank = lax.axis_index("tensor")
-    model_width = residual.shape[1]
+    chips, ranks = lax.axis_size("dp") // 2, lax.axis_size("tensor")
     width = inner_weight.shape[2]
     heads = step_weight.shape[1]
     inner_width = gated_gain.shape[0]
     nseq, length = segment_ids.shape
     tokens = nseq * length
     inner_start, head_start = rank * width, rank * heads
-    stream = residual.astype(f32)
-    scaling = lax.rsqrt(jnp.mean(stream * stream, axis=1, keepdims=True) + epsilon)
-    normed = (stream * scaling * norm_gain).astype(bf16)
-    normed_all = lax.all_gather(normed, "tensor", axis=0, tiled=True)
-    wx = lax.all_gather(
-        jnp.concatenate([inner_weight[:, 1], on_lanes(step_weight)], axis=1), "dp", axis=0, tiled=True
-    )
-    wz = lax.all_gather(inner_weight[:, 0], "dp", axis=0, tiled=True)
-    wo = lax.all_gather(out_weight, "dp", axis=1, tiled=True)
-    cot_all = lax.all_gather(cotangent, "tensor", axis=0, tiled=True)
     taps = jnp.concatenate([conv_weight, conv_bias[None], jnp.zeros((3, conv_bias.shape[0]), f32)], axis=0)
     tapx = lax.dynamic_slice_in_dim(taps, inner_start, width, 1)
     tapbc = taps[:, inner_width:]
@@ -435,65 +1430,35 @@
         [on_lanes(local(step_bias)[None]), on_lanes(rates[None]), jnp.zeros((6, LANES), f32)], axis=0
     )
     skip = jnp.broadcast_to(jnp.repeat(local(skip_gain), WIDTH)[None], (8, width))
-    gain = lax.dynamic_slice_in_dim(gated_gain, inner_start, width, 0)
+    gain = jnp.broadcast_to(
+        lax.dynamic_slice_in_dim(gated_gain, inner_start, width, 0)[None], (8, width)
+    )
     spread = spread_matrix(heads)
     seg = jnp.broadcast_to(segment_ids.reshape(tokens, 1), (tokens, LANES))
 
-    xst = mm(normed_all, wx)
-    bc = mm(normed_all, state_weight)
-    x, st = xst[:, :width], xst[:, width:]
-    y, h = scan_forward(x, bc, st, seg, tapx, tapbc, par, spread, skip, nseq)
-    z = mm(normed_all, wz)
-    sig = jax.nn.sigmoid(z)
-    silu = z * sig
-    gated = y * silu
-    gng = mm_nt(cot_all, wo)
-    sums = lax.psum(
-        jnp.stack([jnp.sum(gated * gated, axis=1), jnp.sum(gng * gain * gated, axis=1)]), "tensor"
-    )
-    scale_g = lax.rsqrt(sums[0] / inner_width + epsilon)[:, None]
-    normed_g = (gated * scale_g * gain).astype(bf16)
-    grad_gated = scale_g * gain * gng - gated * (scale_g**3 * sums[1][:, None] / inner_width)
-    gain_grad = jnp.sum(gng * gated * scale_g, axis=0)
-    gz = (grad_gated * y * (sig * (1.0 + z * (1.0 - sig)))).astype(bf16)
-    gy = grad_gated * silu
-    scatter = lambda v, axis, dim: lax.psum_scatter(
-        v.astype(bf16), axis, scatter_dimension=dim, tiled=True
-    ).astype(f32)
-    block_out = stream + scatter(mm(normed_g, wo), "tensor", 0)
-    out_grad = scatter(mm_tn(normed_g, cot_all), "dp", 1)
-    z_grad = scatter(mm_tn(normed_all, gz), "dp", 0)
-    gx, gbc, gst, gtapx, gtapbc, gpar = scan_backward(
-        x, bc, st, seg, gy, y, h, tapx, tapbc, par, spread, skip, nseq
-    )
-    gbc = gbc.astype(bf16)
-    gxs = jnp.concatenate([gx, gst * (lax.broadcasted_iota(jnp.int32, (1, LANES), 1) < LANES // 2)], axis=1)
-    total = mm_nt(gz, wz) + mm_nt(gxs, wx) + mm_nt(gbc, state_weight)
-    grad_normed = scatter(total, "tensor", 0)
-    x_grad = scatter(mm_tn(normed_all, gxs), "dp", 0)
-    state_grad = scatter(mm_tn(normed_all, gbc), ("dp", "tensor"), 0)
-    state_grad = lax.all_gather(state_grad, ("dp", "tensor"), axis=0, tiled=True)
-    gtapx = gtapx.reshape(5, 8, -1).sum(1)
-    gtapbc = gtapbc.reshape(5, 8, -1).sum(1)
-    gpar = gpar.reshape(3, 8, -1).sum(1)[:, :heads]
-    gtaps = jnp.concatenate(
-        [placed_at((5, inner_width), gtapx, inner_start), gtapbc], axis=1
-    )
-    gpars = placed_at((3, step_bias.shape[0]), gpar, head_start)
-    ggain = placed_at((1, inner_width), gain_grad[None], inner_start)
-    gtaps, gpars, ggain = lax.psum((gtaps, gpars, ggain), ("dp", "tensor"))
-    norm_grad = lax.psum(jnp.sum(grad_normed * stream * scaling, axis=0), ("dp", "tensor"))
-    along = jnp.sum(grad_normed * norm_gain * stream, axis=1, keepdims=True)
-    residual_grad = (
-        cotangent.astype(f32)
-        + scaling * norm_gain * grad_normed
-        - stream * (scaling**3 * along / model_width)
+    wx_own = jnp.concatenate([inner_weight[:, 1], on_lanes(step_weight)], axis=1)
+    x, st, bc, normed, wx = project(
+        1, chips, ranks, residual, norm_gain[None], state_weight, wx_own
+    )
+    y, h, wz, cot = scan_forward_gather(
+        2, chips, ranks, inner_weight[:, 0], cotangent,
+        x, bc, st, seg, tapx, tapbc, par, spread, skip, nseq,
+    )
+    gz, gy, ng, ggain, wo = gate(3, chips, ranks, gain, out_weight.T, normed, wz, y, cot)
+    z_grad, out_grad, block_out, pack, xparts, tparts, sparts, *_ = backward(
+        4, chips, ranks, residual, state_weight, ggain, gz, ng, normed, cot, wo, wz, wx,
+        x, bc, st, seg, gy, y, h, tapx, tapbc, par, spread, skip, nseq,
+    )
+    x_grad, residual_grad, state_grad, sums, norm_grad = finish(
+        5, chips, ranks, pack, residual, cotangent, norm_gain[None], xparts, tparts, sparts
     )
     inner_grad = jnp.stack([z_grad, x_grad[:, :width]], axis=1)
+    by_head = sums[6, :inner_width].reshape(ranks, width)
+    by_head = [by_head[:, k * LANES : k * LANES + heads].reshape(-1) for k in range(3)]
     return (
-        block_out, residual_grad, norm_grad, inner_grad, state_grad,
-        x_grad[:, width : width + heads], gtaps[:4], gtaps[4], gpars[0], gpars[1], gpars[2],
-        ggain[0], out_grad,
+        block_out, residual_grad, norm_grad.reshape(-1), inner_grad, state_grad,
+        x_grad[:, width : width + heads], sums[:4], sums[4], *by_head,
+        sums[5, :inner_width], out_grad.T,
     )
 
 

time: 960 us -> 431 us (0.45)
  waiting for transfers between devices: 677 us -> 0 us
  Pallas kernels: 58.8 us -> 389 us
  matrix products: 97.8 us -> 0 us
  blocking collectives: 51.7 us -> 0 us
  other arithmetic: 28.3 us -> 3.47 us
  between operations: 14.5 us -> 0.79 us
  local copies, waits for them, and re-layouts: 24.4 us -> 35.4 us
    reduce_scatter x6 -> x0, waiting for transfers between devices: 348 us -> none  [per_device(): lax.psum_scatter(v.astype(bf16), axis, scatter_dimension=dim, tiled=True)]
    pallas_call x2 -> x5, Pallas kernels: 58.8 us -> 389 us  [the longest x1 119 us: backward(): pl.pallas_call(functools.partial(backward_kernel, blocks, nseq * blocks,...]
    all_gather x6 -> x0, waiting for transfers between devices: 267 us -> none  [the longest x1 59.5 us: per_device(): lax.all_gather(state_grad, ('dp', 'tensor'), axis=0, tiled=True)]
    dot_general x12 -> x0, matrix products: 97.8 us -> none  [the longest x4 33.4 us: mm(): return jnp.dot(a, b, preferred_element_type=f32)]
    psum x1 -> x0, waiting for transfers between devices: 60.2 us -> none  [per_device(): gtaps, gpars, ggain = lax.psum((gtaps, gpars, ggain), ('dp', 'tensor'))]
    psum x2 -> x0, blocking collectives: 51.7 us -> none  [the longest x1 41.7 us: per_device(): lax.psum(jnp.sum(grad_normed * stream * scaling, axis=0), ('dp', 'tensor'))]
  transfers between devices with their start and end apart: 13 -> 0, of which waited for: 13 -> 0; matrix products, arithmetic and copies ran while one was open for 11% -> 0% of each run, Pallas kernels for 2% -> 0%
where the time goes in v3:
time: 431 us; the launch traced here: 429 us
  Pallas kernels  389 us (90%)
  local copies, waits for them, and re-layouts  35.4 us (8%)
    pallas_call x1, Pallas kernels, backward(): pl.pallas_call(functools.partial(backward_kernel, blocks, nseq * blocks,...  119 us
    pallas_call x1, Pallas kernels, finish(): pl.pallas_call(functools.partial(finish_kernel, chips, ranks), in_specs=[...  99.3 us
    pallas_call x1, Pallas kernels, gate(): pl.pallas_call(functools.partial(gate_kernel, chips, ranks), in_specs=[ON...  61 us
    pallas_call x1, Pallas kernels, project(): pl.pallas_call(functools.partial(project_kernel, chips, ranks), in_specs=...  57.6 us
    pallas_call x1, Pallas kernels, scan_forward_gather(): pl.pallas_call(functools.partial(scan_gather_kernel, blocks, nseq * block...  52.9 us
    unnamed x19, local copies, waits for them, and re-layouts  16.4 us

profile of v3, /device:TPU:0, one launch (start us, length us, event | category | flops | bytes accessed | tf_op | source)
XLA Modules:
  0.0 429.1 jit_solution(7894022492149473377)
XLA Ops:
  6.8 1.0 maximum_maximum_fusion
  9.8 1.7 broadcast_in_dim.44.refs_3_.refs_5_.refs_6_
  11.5 2.0 copy.29
  13.5 1.5 fusion.4
  15.0 1.2 copy_bitcast_fusion
  16.2 1.0 concatenate.15.wx_own
  17.1 57.6 %project.1 = (f32[1024,1024]{1,0:T(8,128)}, f32[1024,128]{1,0:T(8,128)}, f32[1024,256]{1,0:T(8,128)}, bf16[1024,2048]{1,0:T(8,128)(2,1)}, bf16[2048,1152]{1,0:T(8,128)(2,1)}) custom-call(bf16[256,2048]{1,0:T(8,128)(2,1)} %refs_1_.1, f32[1,2048]{1,0:T(1,128)} %bitcast.21, bf16[2048,256]{1,0:T(8,128)(2,1)} %refs_16_.1, bf16[256,1152]{1,0:T(8,128)(2,1)} %concatenate.15.wx_own), custom_call_target="tpu_custom_call" | custom-call | tf_op jit(solution)/shard_map/project/pallas_call | solution.py:759
  74.8 52.9 %scan_forward.1 = (f32[1024,1024]{1,0:T(8,128)}, bf16[1024,1024]{1,0:T(8,128)(2,1)}, bf16[2048,1024]{1,0:T(8,128)(2,1)}, bf16[1024,2048]{1,0:T(8,128)(2,1)}) custom-call(f32[1024,1024]{1,0:T(8,128)} %get-tuple-element.39.refs_0_.refs_1_, f32[1024,256]{1,0:T(8,128)} %get-tuple-element.40.refs_1_.refs_2_.refs_3_, ...), custom_call_target="tpu_custom_call" | custom-call | tf_op jit(solution)/shard_map/scan_forward/pallas_call | solution.py:816
  127.7 61.0 %gate.1 = (bf16[1024,1024]{1,0:T(8,128)(2,1)}, f32[1024,1024]{1,0:T(8,128)}, bf16[1024,1024]{1,0:T(8,128)(2,1)}, f32[8,1024]{1,0:T(8,128)}, bf16[2048,1024]{1,0:T(8,128)(2,1)}) custom-call(f32[8,1024]{1,0:T(8,128)} %broadcast_in_dim.45.gain_ref, bf16[256,1024]{1,0:T(8,128)(2,1)} %bitcast.18, bf16[1024,2048]{1,0:T(8,128)(2,1)} %get-tuple-element.42.normed_in.refs_20_, ...), custom_call_target="tpu_custom_call" | custom-call | tf_op jit(solution)/shard_map/gate/pallas_call | solution.py:965
  188.7 118.6 %backward.1 = (f32[256,1024]{1,0:T(8,128)}, f32[256,1024]{1,0:T(8,128)}, f32[256,2048]{1,0:T(8,128)}, f32[8,1280]{1,0:T(8,128)}, bf16[2048,1152]{1,0:T(8,128)(2,...) custom-call(f32[1024,1024]{1,0:T(8,128)} %get-tuple-element.39.refs_, ...), custom_call_target="tpu_custom_call" | custom-call | tf_op jit(solution)/shard_map/backward/pallas_call | solution.py:1208
  307.2 2.5 copy.33
  309.8 99.3 %finish.1 = (f32[256,1152]{1,0:T(8,128)}, f32[256,2048]{1,0:T(8,128)}, f32[2048,256]{1,0:T(8,128)}, f32[8,4352]{1,0:T(8,128)}, f32[8,256]{1,0:T(8,128)}) custom-call(f32[8,1280]{1,0:T(8,128)} %get-tuple-element.54.refs_0_, bf16[256,2048]{1,0:T(8,128)(2,1)} %refs_1_.1, bf16[256,2048]{1,0:T(8,128)(2,1)} %refs_2_.1, f32[1,2048]{1,0:T(1,128)} %bitcast.22, ...), custom_call_target="tpu_custom_call" | custom-call | tf_op jit(solution)/shard_map/finish/pallas_call | solution.py:1386
  409.1 1.4 copy.36
  410.5 1.6 slice_reduce_fusion
  412.1 1.6 fusion.5
  413.7 1.5 slice.41
  417.0 0.9 slice.40
  417.9 1.3 slice_bitcast_fusion
  420.2 2.9 copy.31
  423.1 1.3 copy.42
  424.4 1.0 copy-done.3
  425.5 1.3 copy.43
  426.8 1.0 copy-done.2
  427.8 1.3 copy.44
  (39 shorter events, 10.8 us)
Async XLA Ops:
  0.6 12.9 %copy-start = (bf16[256,2,1024]{2,1,0:T(2,128)(2,1)S(1)}, bf16[256,2,1024]{2,1,0:T(2,128)(2,1)}, u32[]{:S(2)}) copy-start(bf16[256,2,1024]{2,1,0:T(2,128)(2,1)} %param.17) | copy-start | bytes 3145732
  409.1 10.8 %copy-start.4 = (f32[256,1024]{1,0:T(8,128)S(1)}, f32[256,1024]{1,0:T(8,128)}, u32[]{:S(2)}) copy-start(f32[256,1024]{1,0:T(8,128)} %get-tuple-element.60) | copy-start | bytes 3145732
  420.2 3.0 copy-start.1
  423.1 2.3 copy-start.3
  425.5 2.3 copy-start.2

commit v4 on v3

--- a/solution.py
+++ b/solution.py
@@ -9,7 +9,7 @@
 LANES = 128
 BLOCK = 128
 WIDTH = 64
-VMEM_BYTES = 56 * 1024 * 1024
+VMEM_BYTES = 60 * 1024 * 1024
 f32, bf16 = jnp.float32, jnp.bfloat16
 ROWS0 = (((0,), (0,)), ((), ()))
 COLS1 = (((1,), (1,)), ((), ()))
@@ -50,13 +50,10 @@
 def convolve(tail, part, masks, taps):
     n = part.shape[0]
     ext = jnp.concatenate([tail, part], axis=0)
-    shifts = [part] + [
-        jnp.where(masks[k], ext[8 - k : 8 - k + n], 0.0) for k in (1, 2, 3)
-    ]
     total = taps[4:5] + taps[3:4] * part
     for k in (1, 2, 3):
-        total = total + taps[3 - k : 4 - k] * shifts[k]
-    return total, shifts
+        total = total + taps[3 - k : 4 - k] * jnp.where(masks[k], ext[8 - k : 8 - k + n], 0.0)
+    return total
 
 
 def wide(v):
@@ -82,7 +79,7 @@
 
 def scan_fwd_kernel(
     blocks, x_ref, bc_ref, st_ref, seg_ref, tapx_ref, tapbc_ref, par_ref, spread_ref, skip_ref,
-    y_ref, h_ref, state, tail_x, tail_bc, tail_seg,
+    y_ref, h_ref, conv_ref, convbc_ref, state, tail_x, tail_bc, tail_seg,
 ):
     n = BLOCK
     block = pl.program_id(1)
@@ -108,7 +105,8 @@
     onto_w = mm(two_parts(onto, low_lanes), spread)
     through_w = mm(two_parts(jnp.broadcast_to(through, (8, LANES)), low_lanes[:8]), spread)[0:1]
     bc_masks = [None] + [wide(m) for m in masks[1:]]
-    conv_bc, _ = convolve(tail_bc[...], bc_ref[...], bc_masks, tapbc_ref[...])
+    conv_bc = convolve(tail_bc[...], bc_ref[...], bc_masks, tapbc_ref[...])
+    convbc_ref[...] = conv_bc
     act_bc = conv_bc * sigmoid(conv_bc)
     b, c = act_bc[:, :LANES].astype(bf16), act_bc[:, LANES:].astype(bf16)
     cross = mm_nt(c, b)
@@ -117,7 +115,8 @@
     first_half = lax.broadcasted_iota(jnp.int32, (n, LANES), 1) < WIDTH
     for pair in range(x_ref.shape[1] // LANES):
         sl = slice(pair * LANES, (pair + 1) * LANES)
-        conv, _ = convolve(tail_x[:, sl], x_ref[:, sl], masks, tapx_ref[:, sl])
+        conv = convolve(tail_x[:, sl], x_ref[:, sl], masks, tapx_ref[:, sl])
+        conv_ref[:, sl] = conv
         xs = conv * sigmoid(conv)
         xd = xs * dt_w[:, sl]
         outside = mm(c, entering[:, sl]) * into_w[:, sl]
@@ -145,10 +144,10 @@
 
 
 def scan_bwd_kernel(
-    blocks, x_ref, xt_ref, bc_ref, bct_ref, st_ref, seg_ref, segt_ref, gy_ref, y_ref, h_ref,
+    blocks, x_ref, conv_ref, bc_ref, convbc_ref, st_ref, seg_ref, segt_ref, gy_ref, y_ref, h_ref,
     tapx_ref, tapbc_ref, par_ref, spread_ref, skip_ref,
     gx_ref, gbc_ref, gst_ref, gtapx_ref, gtapbc_ref, gpar_ref,
-    gstate, head_x, head_bc, head_seg,
+    gstate, head_x, head_bc, head_seg, xs_s, slope_s, back_s, dt_s, onto_s, xd_s, into_s, onto_low, sums_s,
 ):
     n = BLOCK
     step = pl.program_id(1)
@@ -169,24 +168,21 @@
 
     seg = seg_ref[...]
     first = block == 0
-    seg_tail = jnp.where(first, -1, segt_ref[...])
-    masks = shifted_masks(jnp.concatenate([seg_tail, seg], axis=0), seg)
     seg_next = jnp.concatenate([seg, head_seg[...]], axis=0)
     ahead = [None] + [seg_next[k : k + n] == seg for k in (1, 2, 3)]
-    prev_seg, end_seg = seg_tail[7:8], seg[n - 1 : n]
+    prev_seg = jnp.where(first, -1, segt_ref[7:8])
+    end_seg = seg[n - 1 : n]
     v, dt, a, cum, into, onto, through, bias = step_state(
         st_ref[...], par_ref[...], seg, prev_seg, end_seg, n
     )
     cum_t = jnp.transpose(cum)
     low_lanes = lax.broadcasted_iota(jnp.int32, (n, LANES), 1) >= LANES // 2
     spread = spread_ref[...]
-    dt_w = mm(two_parts(dt, low_lanes), spread)
+    dt_s[...] = mm(two_parts(dt, low_lanes), spread)
     into_w = mm(two_parts(into, low_lanes), spread)
-    onto_w = mm(two_parts(onto, low_lanes), spread)
+    onto_s[...] = mm(two_parts(onto, low_lanes), spread)
     through_w = mm(two_parts(jnp.broadcast_to(through, (8, LANES)), low_lanes[:8]), spread)[0:1]
-    bc_masks = [None] + [wide(m) for m in masks[1:]]
-    tail_bc = jnp.where(first, 0.0, bct_ref[...])
-    conv_bc, shifts_bc = convolve(tail_bc, bc_ref[...], bc_masks, tapbc_ref[...])
+    conv_bc = convbc_ref[...]
     sig_bc = sigmoid(conv_bc)
     act_bc = conv_bc * sig_bc
     b, c = act_bc[:, :LANES].astype(bf16), act_bc[:, LANES:].astype(bf16)
@@ -195,41 +191,42 @@
     halves = lambda t: jnp.concatenate(
         [jnp.where(first_half, t, 0.0), jnp.where(first_half, 0.0, t)], axis=0
     ).astype(bf16)
-
-    gcross = jnp.zeros((n, n), f32)
-    gb = jnp.zeros((n, LANES), f32)
-    gc = jnp.zeros((n, LANES), f32)
-    sum_q = jnp.zeros((n, LANES), f32)
-    sum_state = jnp.zeros((n, LANES), f32)
-    sum_dt = jnp.zeros((n, LANES), f32)
-    sum_skip = jnp.zeros((8, LANES), f32)
-    sum_last = jnp.zeros((8, LANES), f32)
-    for pair in range(x_ref.shape[1] // LANES):
-        sl = slice(pair * LANES, (pair + 1) * LANES)
-        tail_x = jnp.where(first, 0.0, xt_ref[:, sl])
-        part = x_ref[:, sl]
-        taps = tapx_ref[:, sl]
-        conv, shifts = convolve(tail_x, part, masks, taps)
+    pairs = [slice(i, i + LANES) for i in range(0, x_ref.shape[1], LANES)]
+
+    for sl in pairs:
+        conv = conv_ref[:, sl]
         sig = sigmoid(conv)
         xs = conv * sig
-        xd = xs * dt_w[:, sl]
-        xd_low = xd.astype(bf16)
+        xs_s[:, sl] = xs
+        slope_s[:, sl] = sig + xs * (1.0 - sig)
+        xd = xs * dt_s[:, sl]
+        xd_s[:, sl] = xd.astype(bf16)
+        onto_low[:, sl] = (xd * onto_s[:, sl]).astype(bf16)
+        into_s[:, sl] = (gy_ref[:, sl] * into_w[:, sl]).astype(bf16)
+    before = h_ref[...]
+    gstate_low = gstate[...].astype(bf16)
+    gy_into = into_s[...]
+    gc = mm_nt(gy_into, before)
+    gb = mm_nt(onto_low[...], gstate_low)
+    back_s[...] = mm(b, gstate_low)
+    edges = 5 * n
+    for sl in pairs:
+        old = through_w[:, sl] * gstate[:, sl]
+        last = fold(old * before[:, sl].astype(f32))
+        skips = fold(gy_ref[:, sl] * xs_s[:, sl])
+        both = jnp.concatenate([last, skips], axis=0)
+        high = both.astype(bf16)
+        sums_s[edges : edges + 16, sl] = high
+        sums_s[edges + 16 : edges + 32, sl] = (both - high.astype(f32)).astype(bf16)
+        gstate[:, sl] = old + mm_tn(c, gy_into[:, sl])
+    gcross = jnp.zeros((n, n), f32)
+    for pair, sl in enumerate(pairs):
+        xs = xs_s[:, sl]
+        xd_low = xd_s[:, sl]
         gy = gy_ref[:, sl]
-        gy_low = gy.astype(bf16)
         skip = skip_ref[0:1, sl]
         inner = y_ref[:, sl] - skip * xs
-        spread_p = spread[:, sl]
-        gstate_low = gstate[:, sl].astype(bf16)
-        before = h_ref[:, sl]
-        gy_into = (gy * into_w[:, sl]).astype(bf16)
-        xd_onto = (xd * onto_w[:, sl]).astype(bf16)
-        gc = gc + mm_nt(gy_into, before)
-        gb = gb + mm_nt(xd_onto, gstate_low)
-        g_state = onto_w[:, sl] * mm(b, gstate_low)
-        sum_last = sum_last + head_sums(
-            fold(gstate[:, sl] * (through_w[:, sl] * before.astype(f32))), spread_p
-        )
-        gstate[:, sl] = through_w[:, sl] * gstate[:, sl] + mm_tn(c, gy_into)
+        g_state = onto_s[:, sl] * back_s[:, sl]
         gy_halves = halves(gy)
         gmix = mm_nt(gy_halves, xd_low)
         mixes = []
@@ -237,38 +234,50 @@
             decay = jnp.exp(cum[:, h : h + 1] - cum_t[h : h + 1, :] + bias)
             mixes.append((decay * cross).astype(bf16))
             gcross = gcross + decay * gmix[i * n : (i + 1) * n]
-        g_inside = mm_tn(jnp.concatenate(mixes, axis=0), gy_halves)
-        gxd = g_inside + g_state
-        xd_r, gy_r = xd_low.astype(f32), gy_low.astype(f32)
-        sum_q = sum_q + head_sums(gy_r * inner - xd_r * gxd, spread_p)
-        sum_state = sum_state + head_sums(xd_r * g_state, spread_p)
-        sum_dt = sum_dt + head_sums(xs * gxd, spread_p)
-        sum_skip = sum_skip + head_sums(fold(gy * xs), spread_p)
-        gxs = dt_w[:, sl] * gxd + skip * gy
-        gconv = gxs * (sig * (1.0 + conv * (1.0 - sig)))
+        gxd = mm_tn(jnp.concatenate(mixes, axis=0), gy_halves) + g_state
+        xd_r, gy_r = xd_low.astype(f32), gy.astype(bf16).astype(f32)
+        q = gy_r * inner - xd_r * gxd
+        high = q.astype(bf16)
+        sums_s[0:n, sl] = high
+        sums_s[n : 2 * n, sl] = (q - high.astype(f32)).astype(bf16)
+        q = xd_r * g_state
+        high = q.astype(bf16)
+        sums_s[2 * n : 3 * n, sl] = high
+        sums_s[3 * n : 4 * n, sl] = (q - high.astype(f32)).astype(bf16)
+        sums_s[4 * n : 5 * n, sl] = (xs * gxd).astype(bf16)
+        gconv = (dt_s[:, sl] * gxd + skip * gy) * slope_s[:, sl]
+        taps = tapx_ref[:, sl]
+        part = x_ref[:, sl]
         ext = jnp.concatenate([gconv, head_x[:, sl]], axis=0)
         gu = taps[3:4] * gconv
+        gtapx_ref[24:32, sl] += fold(gconv * part)
         for k in (1, 2, 3):
-            gu = gu + taps[3 - k : 4 - k] * jnp.where(ahead[k], ext[k : k + n], 0.0)
+            later = jnp.where(ahead[k], ext[k : k + n], 0.0)
+            gu = gu + taps[3 - k : 4 - k] * later
+            gtapx_ref[8 * (3 - k) : 8 * (4 - k), sl] += fold(later * part)
         gx_ref[:, sl] = gu.astype(bf16)
-        for k in range(4):
-            row = 8 * (3 - k)
-            gtapx_ref[row : row + 8, sl] += fold(gconv * shifts[k])
         gtapx_ref[32:40, sl] += fold(gconv)
         head_x[:, sl] = gconv[0:8]
+    sums = mm_nt(sums_s[...], spread)
+    sum_q = sums[0:n] + sums[n : 2 * n]
+    sum_state = sums[2 * n : 3 * n] + sums[3 * n : 4 * n]
+    sum_dt = sums[4 * n : 5 * n]
+    sum_last = sums[edges : edges + 8] + sums[edges + 16 : edges + 24]
+    sum_skip = sums[edges + 8 : edges + 16] + sums[edges + 24 : edges + 32]
     gcross_low = gcross.astype(bf16)
     gc = gc + mm(gcross_low, b)
     gb = gb + mm_tn(gcross_low, c)
-    gconv = jnp.concatenate([gb, gc], axis=1) * (sig_bc * (1.0 + conv_bc * (1.0 - sig_bc)))
+    gconv = jnp.concatenate([gb, gc], axis=1) * (sig_bc + act_bc * (1.0 - sig_bc))
     ext = jnp.concatenate([gconv, head_bc[...]], axis=0)
     taps = tapbc_ref[...]
+    part = bc_ref[...]
     gu = taps[3:4] * gconv
+    gtapbc_ref[24:32, :] += fold(gconv * part)
     for k in (1, 2, 3):
-        gu = gu + taps[3 - k : 4 - k] * jnp.where(wide(ahead[k]), ext[k : k + n], 0.0)
+        later = jnp.where(wide(ahead[k]), ext[k : k + n], 0.0)
+        gu = gu + taps[3 - k : 4 - k] * later
+        gtapbc_ref[8 * (3 - k) : 8 * (4 - k), :] += fold(later * part)
     gbc_ref[...] = gu.astype(gbc_ref.dtype)
-    for k in range(4):
-        row = 8 * (3 - k)
-        gtapbc_ref[row : row + 8, :] += fold(gconv * shifts_bc[k])
     gtapbc_ref[32:40, :] += fold(gconv)
     head_bc[...] = gconv[0:8]
     head_seg[...] = seg[0:8]
@@ -287,6 +296,19 @@
     gpar_ref[16:24] += sum_skip
 
 
+def scan_bwd_scratch(width, states):
+    n = BLOCK
+    return [
+        pltpu.VMEM((states, width), f32),
+        pltpu.VMEM((8, width), f32),
+        pltpu.VMEM((8, 2 * states), f32),
+        pltpu.VMEM((8, LANES), jnp.int32),
+        *[pltpu.VMEM((n, width), f32)] * 5,
+        *[pltpu.VMEM((n, width), bf16)] * 3,
+        pltpu.VMEM((5 * n + 32, width), bf16),
+    ]
+
+
 def spread_matrix(heads):
     row = lax.broadcasted_iota(jnp.int32, (LANES, heads * WIDTH), 0)
     col = lax.broadcasted_iota(jnp.int32, (LANES, heads * WIDTH), 1)
@@ -512,21 +534,20 @@
 
 
 class LineScatter:
-    def __init__(self, parts, out, mine, swap, up, down, send, recv, local, chips):
-        self.parts, self.out, self.mine, self.swap, self.up, self.down = parts, out, mine, swap, up, down
-        self.send, self.recv, self.local, self.chips = send, recv, local, chips
-        self.rows = parts.shape[0] // (2 * chips)
+    def __init__(self, parts, swap, flow, send, recv, temp, tsem, chips):
+        self.parts, self.swap, self.flow = parts, swap, flow
+        self.send, self.recv, self.temp, self.tsem, self.chips = send, recv, temp, tsem, chips
+        self.rows, self.wide = parts.shape[0] // (2 * chips), parts.shape[1]
         self.chip, self.core, self.rank = place()
         self.me = self.chip * 2 + self.core
         self.partner = self.chip * 2 + 1 - self.core
-        self.steps = chips
 
     @staticmethod
     def scratch(chips, shape, dtype=bf16):
-        block = (chips, shape[0] // (2 * chips)) + tuple(shape[1:])
-        return [pltpu.VMEM(block, dtype)] * 4 + [
+        block = (shape[0] // (2 * chips),) + tuple(shape[1:])
+        return [
+            pltpu.VMEM((chips,) + block, dtype), pltpu.VMEM((chips + 1,) + block, dtype),
             pltpu.SemaphoreType.DMA((3, chips)), pltpu.SemaphoreType.DMA((3, chips)),
-            pltpu.SemaphoreType.DMA((chips,)),
         ]
 
     def order(self):
@@ -539,16 +560,23 @@
             self.recv.at[2, c], self.partner, self.rank,
         )
 
-    def load(self, c):
+    def load(self, i):
+        c = self.order()[i]
         return pltpu.make_async_copy(
-            slab(self.parts, 2 * c + self.core, self.rows), self.mine.at[c], self.local.at[c]
+            slab(self.parts, 2 * c + self.core, self.rows), self.held(i), self.tsem.at[i % 2]
         )
 
+    def held(self, i):
+        return self.temp.at[i % 2, pl.ds(0, self.rows), pl.ds(0, self.wide)]
+
     def along(self, way, c, first=False):
-        buffer = (self.up, self.down)[way]
-        src = self.mine.at[c] if first else buffer.at[c]
+        if way == 0:
+            here = there = c
+        else:
+            here, there = c, jnp.where(c == self.chip - 1, self.chips, c)
+        src = self.swap.at[c] if first else self.flow.at[here]
         return remote(
-            src, buffer.at[c], self.send.at[way, c], self.recv.at[way, c],
+            src, self.flow.at[there], self.send.at[way, c], self.recv.at[way, c],
             self.me + (2, -2)[way], self.rank,
         )
 
@@ -557,13 +585,16 @@
         if k == 0:
             for c in self.order():
                 self.over(c).start()
-                self.load(c).start()
             return
         if k == 1:
-            for c in self.order():
+            self.load(0).start()
+            self.load(1).start()
+            for i, c in enumerate(self.order()):
                 self.over(c).wait()
-                self.load(c).wait()
-                add_rows(self.mine.at[c], [self.swap.at[c]])
+                self.load(i).wait()
+                add_rows(self.swap.at[c], [self.held(i)])
+                if i + 2 < n:
+                    self.load(i + 2).start()
 
                 @pl.when((chip == 0) & (c > 0))
                 def _():
@@ -579,7 +610,7 @@
         @pl.when((chip > 0) & (t >= chip) & (c > chip))
         def _():
             self.along(0, c).wait_recv()
-            add_rows(self.up.at[c], [self.mine.at[c]])
+            add_rows(self.flow.at[c], [self.swap.at[c]])
             self.along(0, c).start()
 
         d = t - (n - 1 - chip)
@@ -587,12 +618,12 @@
         @pl.when((chip < n - 1) & (d >= 0) & (d < chip))
         def _():
             self.along(1, d).wait_recv()
-            add_rows(self.down.at[d], [self.mine.at[d]])
+            add_rows(self.flow.at[d], [self.swap.at[d]])
             self.along(1, d).start()
 
-    def finish(self):
+    def finish(self, out):
         n, chip = self.chips, self.chip
-        out, mine, up, down = self.out, self.mine.at[chip], self.up.at[chip], self.down.at[chip]
+        mine, up, down = self.swap.at[chip], self.flow.at[chip], self.flow.at[n]
 
         @pl.when(chip == 0)
         def _():
@@ -630,9 +661,8 @@
         self.steps = 1
 
     @staticmethod
-    def scratch(ranks, shape):
+    def scratch(ranks):
         return [
-            pltpu.VMEM((ranks, shape[0] // ranks, shape[1]), bf16),
             pltpu.SemaphoreType.DMA((ranks,)), pltpu.SemaphoreType.DMA((ranks,)),
             pltpu.SemaphoreType.DMA,
         ]
@@ -652,10 +682,8 @@
     def step(self, k):
         for j in range(1, self.ranks):
             self.copy(j).start()
-        self.load().start()
 
     def arrive(self):
-        self.load().wait()
         for j in range(1, self.ranks):
             self.copy(j).wait()
 
@@ -777,8 +805,8 @@
 
 def scan_gather_kernel(blocks, total, chips, ranks, *refs):
     own, (wz_own, cot_own) = refs[:9], refs[9:11]
-    outs, (wz_out, cot_out) = refs[11:13], refs[13:15]
-    scratch, sems = refs[15:19], refs[19:]
+    outs, (wz_out, cot_out) = refs[11:15], refs[15:17]
+    scratch, sems = refs[17:21], refs[21:]
     now = pl.program_id(0) * blocks + pl.program_id(1)
     line = LineGather(wz_own, wz_out, *sems[:3], chips)
     tensor = TensorGather(cot_own, cot_out, *sems[3:], ranks)
@@ -826,15 +854,18 @@
             pl.BlockSpec(par.shape, whole),
             pl.BlockSpec(spread.shape, whole),
             pl.BlockSpec(skip.shape, whole),
-            ANY,
-            ANY,
+            pl.BlockSpec(wz_own.shape, whole),
+            pl.BlockSpec(cot_own.shape, whole),
         ],
         out_specs=[
-            pl.BlockSpec((n, width), at), pl.BlockSpec((states, width), at), ANY, ANY,
+            pl.BlockSpec((n, width), at), pl.BlockSpec((states, width), at),
+            pl.BlockSpec((n, width), at), pl.BlockSpec((n, 2 * states), at), ANY, ANY,
         ],
         out_shape=[
             shaped((tokens, width), f32),
             shaped((tokens // n * states, width), bf16),
+            shaped((tokens, width), f32),
+            shaped((tokens, 2 * states), f32),
             shaped((wz_own.shape[0] * 2 * chips, width), bf16),
             shaped((tokens, cot_own.shape[1]), bf16),
         ],
@@ -1021,20 +1052,20 @@
         store(j).wait()
 
 
-def stream_back(terms, kept, parts, stage, ssem):
+def stream_back(terms, kept, parts, stage, ssem, begin=0, end=1):
     tokens, model = parts.shape
-    count = model // CHUNK
+    base, count = int(model // CHUNK * begin), int(model // CHUNK * (end - begin))
 
     def loads(j):
         slot = lax.rem(j, 2)
         return [
-            pltpu.make_async_copy(slab(right, j, CHUNK), buffer.at[slot], sem.at[slot])
+            pltpu.make_async_copy(slab(right, base + j, CHUNK), buffer.at[slot], sem.at[slot])
             for _, right, buffer, sem in terms
         ]
 
     def store(j):
         slot = lax.rem(j, 2)
-        columns = pl.ds(pl.multiple_of(j * CHUNK, CHUNK), CHUNK)
+        columns = pl.ds(pl.multiple_of((base + j) * CHUNK, CHUNK), CHUNK)
         return pltpu.make_async_copy(stage.at[slot], parts.at[:, columns], ssem.at[slot])
 
     for copy in loads(0):
@@ -1062,7 +1093,9 @@
             for left, _, buffer, _ in terms:
                 total = total + mm_nt(left[at], buffer[slot])
             for left, right in kept:
-                total = total + mm_nt(left[at], right[pl.ds(pl.multiple_of(j * CHUNK, CHUNK), CHUNK)])
+                total = total + mm_nt(
+                    left[at], right[pl.ds(pl.multiple_of((base + j) * CHUNK, CHUNK), CHUNK)]
+                )
             stage[slot, at] = total.astype(bf16)
         store(j).start()
 
@@ -1070,55 +1103,87 @@
         store(j).wait()
 
 
+def everyone(buffer, mine, count, send, recv, device):
+    row = buffer.at[mine]
+    return [
+        remote(row, row, send.at[k], recv.at[k], *device(lax.rem(mine + k, count)))
+        for k in range(1, count)
+    ]
+
+
+def added(buffer, count):
+    total = buffer[0]
+    for k in range(1, count):
+        total = total + buffer[k]
+    return total
+
+
 def backward_kernel(blocks, total, chips, ranks, *refs):
     ins, refs = refs[:15], refs[15:]
-    (res_ref, ws_ref, ggain_ref, gz_in, ng_in, normed_in, cot_in, wo_in, wz_in, wx_in), refs = refs[:10], refs[10:]
-    (z_sum, o_sum, block_out, pack_ref, xparts, tparts, sparts, zparts, oparts, pparts, gbc_slots), refs = refs[:11], refs[11:]
-    scratch, refs = refs[:4], refs[4:]
-    (gxs, gbc_own, gtapx, gtapbc, gpar, gz, ng, cbuf, stage, back, wbuf, xbuf, gbc_sum, state_stage), refs = refs[:14], refs[14:]
-    (loads, csem, ssem, bsem, wsem, xsem), refs = refs[:6], refs[6:]
-    job0 = LineScatter(zparts, z_sum, *refs[:7], chips)
-    job1 = LineScatter(oparts, o_sum, *refs[7:14], chips)
-    across = TensorScatter(pparts, *refs[14:18], ranks)
-    around = TensorGather(gbc_own, gbc_slots, *refs[18:], ranks)
+    (ggain_ref, gain_ref), refs = refs[:2], refs[2:]
+    (res_in, cot_own_in, ws_in, gz_in, ng_in, normed_in, cot_in, wo_in, wz_in, wx_in), refs = refs[:10], refs[10:]
+    (sums_ref, norm_ref, state_ref), refs = refs[:3], refs[3:]
+    (z_sum, o_sum, x_sum, block_out, res_grad), refs = refs[:5], refs[5:]
+    (xparts, tparts, sparts, zparts, oparts, pparts, gbc_slots, pland), refs = refs[:8], refs[8:]
+    scratch, refs = refs[:13], refs[13:]
+    (gxs, gbc_own, gtapx, gtapbc, gpar, gz, ng, cbuf, stage, back, wbuf, xbuf), refs = refs[:12], refs[12:]
+    (gbc_sum, ws, res, other, wide_out, line_out, tland, state_stage), refs = refs[:8], refs[8:]
+    (state_own, state_line, state_low, state_all, pack, packs, land_rank), refs = refs[:7], refs[7:]
+    (norm_rank, norm_dp, norm_acc), refs = refs[:3], refs[3:]
+    (loads, csem, ssem, bsem, wsem, xsem, osem), refs = refs[:7], refs[7:]
+    (qsend, qrecv, nsend, nrecv, msend, mrecv), refs = refs[:6], refs[6:]
+    z_job = LineScatter(zparts, *refs[:4], stage, ssem, chips)
+    o_job = LineScatter(oparts, *refs[4:8], stage, ssem, chips)
+    x_job = LineScatter(xparts, *refs[8:12], stage, ssem, chips)
+    s_job = LineScatter(sparts, *refs[12:16], state_stage, csem, chips)
+    refs = refs[16:]
+    first = TensorScatter(pparts, pland, *refs[:3], ranks)
+    second = TensorScatter(tparts, tland, *refs[3:6], ranks)
+    around = TensorGather(gbc_own, gbc_slots, *refs[6:9], ranks)
+    s_line = LineGather(state_own, state_line, *refs[9:12], chips)
+    s_rank = TensorGather(state_low, state_all, *refs[12:15], ranks)
+    p_line = LineGather(pack, packs, *refs[15:18], chips)
     now = pl.program_id(0) * blocks + pl.program_id(1)
     tokens, width = gz.shape
-    rank = across.rank
+    model = normed_in.shape[1]
+    rank, me, devices = first.rank, first.me, 2 * chips
+    over_dp = lambda d: (d, rank)
+    over_rank = lambda r: (me, r)
+    fetch = [
+        pltpu.make_async_copy(src, dst, loads.at[i])
+        for i, (src, dst) in enumerate(((gz_in, gz), (ng_in, ng), (ws_in, ws), (res_in, res)))
+    ]
+
+    def once(src, dst, sem):
+        copy = pltpu.make_async_copy(src, dst, sem)
+        copy.start()
+        copy.wait()
 
     @pl.when(now == 0)
     def _():
-        fetch = [
-            pltpu.make_async_copy(gz_in, gz, loads.at[0]),
-            pltpu.make_async_copy(ng_in, ng, loads.at[1]),
-        ]
         for copy in fetch:
             copy.start()
-        greet(chips, ranks)
+        greet_all(chips, ranks)
         fetch[0].wait()
         stream_grads(normed_in, gz, zparts, width, cbuf, stage, csem, ssem)
-        job0.step(0)
+        z_job.step(0)
         fetch[1].wait()
         stream_back([(ng, wo_in, wbuf, wsem)], [], pparts, back, bsem)
-        across.step(0)
-        job0.step(1)
+        first.step(0)
+        z_job.step(1)
         stream_grads(cot_in, ng, oparts, width, cbuf, stage, csem, ssem)
-        job1.step(0)
-
-    early = [k for k in range(2, chips) if 2 * k - 3 < total - 1]
-
-    @pl.when(now == 1)
+        o_job.step(0)
+
+    early = [k for k in range(2, chips) if 3 * k - 4 < total - 1]
+
+    @pl.when(now == 2)
     def _():
-        job1.step(1)
+        o_job.step(1)
 
     for k in early:
-        @pl.when(now == 2 * k - 3)
+        @pl.when(now == 3 * k - 4)
         def _():
-            job0.step(k)
-
-    @pl.when(now == total - 1)
-    def _():
-        if chips > 2:
-            job1.step(2)
+            z_job.step(k)
 
     row = pl.multiple_of(
         (pl.program_id(0) * blocks + blocks - 1 - pl.program_id(1)) * BLOCK, BLOCK
@@ -1133,21 +1198,39 @@
     @pl.when(now == total - 1)
     def _():
         around.step(0)
+        fetch[2].wait()
+        fetch[3].wait()
         stream_grads(normed_in, gxs, xparts, width + LANES, cbuf, stage, csem, ssem)
-        around.step(1)
+        x_job.step(0)
+        pack[...] = jnp.zeros_like(pack)
+        for k in range(5):
+            rows = slice(8 * k, 8 * k + 8)
+            pack[k : k + 1, :width] = jnp.sum(gtapx[rows], axis=0, keepdims=True)
+            pack[k : k + 1, width:] = jnp.sum(gtapbc[rows], axis=0, keepdims=True)
+        pack[5:6, :width] = jnp.sum(ggain_ref[...], axis=0, keepdims=True)
+        for k in range(3):
+            pack[6:7, k * LANES : (k + 1) * LANES] = jnp.sum(
+                gpar[8 * k : 8 * k + 8], axis=0, keepdims=True
+            )
+        p_line.step(0)
         for k in range(2, chips):
             if k not in early:
-                job0.step(k)
+                z_job.step(k)
+        around.step(1)
+        if chips > 2:
+            o_job.step(2)
+        terms = [(gz, wz_in, wbuf, wsem), (gxs, wx_in, xbuf, xsem)]
+        stream_back(terms, [(gbc_own, ws)], tparts, back, bsem, 0, 0.5)
+        x_job.step(1)
         for k in range(3, chips):
-            job1.step(k)
-        stream_back(
-            [(gz, wz_in, wbuf, wsem), (gxs, wx_in, xbuf, xsem)], [(gbc_own, ws_ref)], tparts, back, bsem
-        )
+            o_job.step(k)
+        stream_back(terms, [(gbc_own, ws)], tparts, back, bsem, 0.5, 1)
+        second.step(0)
+        for k in range(1, chips):
+            p_line.step(k)
         around.finish()
         for r in range(ranks):
-            copy = pltpu.make_async_copy(slab(gbc_slots, r, tokens), cbuf.at[r % 2], csem.at[r % 2])
-            copy.start()
-            copy.wait()
+            once(slab(gbc_slots, r, tokens), cbuf.at[r % 2], csem.at[r % 2])
 
             def add(at):
                 v = cbuf[r % 2, at].astype(f32)
@@ -1162,39 +1245,111 @@
         depth = sparts.shape[0]
         for i in range(depth // CHUNK):
             columns = pl.ds(pl.multiple_of(rank * depth + i * CHUNK, CHUNK), CHUNK)
-            copy = pltpu.make_async_copy(normed_in.at[:, columns], cbuf.at[0], csem.at[0])
+            once(normed_in.at[:, columns], cbuf.at[0], csem.at[0])
+            state_stage[0] = mm_tn(cbuf[0], gbc_own[...])
+            once(state_stage.at[0], sparts.at[pl.ds(i * CHUNK, CHUNK)], csem.at[1])
+        s_job.step(0)
+        z_job.finish(line_out.at[:, pl.ds(0, width)])
+        once(line_out.at[:, pl.ds(0, width)], z_sum, osem.at[0])
+        s_job.step(1)
+        p_line.finish()
+        total_pack = packs[0:8]
+        for k in range(1, devices):
+            total_pack = total_pack + packs[8 * k : 8 * k + 8]
+        land_rank[rank] = total_pack
+        packed = everyone(land_rank, rank, ranks, qsend, qrecv, over_rank)
+        for copy in packed:
             copy.start()
+        first.arrive()
+        for r in range(ranks):
+            if r == 0:
+                once(slab(pparts, rank, first.rows), other, osem.at[1])
+            else:
+                once(pland.at[r], other, osem.at[1])
+
+            def add(at):
+                wide_out[at] = (res[at] if r == 0 else wide_out[at]).astype(f32) + other[at].astype(f32)
+
+            row_loop(first.rows, 16, add)
+        keep = pltpu.make_async_copy(wide_out, block_out, osem.at[2])
+        keep.start()
+        o_job.finish(line_out.at[:, pl.ds(0, width)])
+        once(line_out.at[:, pl.ds(0, width)], o_sum, osem.at[0])
+        for k in range(2, chips):
+            s_job.step(k)
+            x_job.step(k)
+        for copy in packed:
             copy.wait()
-            state_stage[...] = mm_tn(cbuf[0], gbc_own[...])
-            copy = pltpu.make_async_copy(state_stage, sparts.at[pl.ds(i * CHUNK, CHUNK)], csem.at[1])
+        shared = land_rank[0, :, width:]
+        for r in range(1, ranks):
+            shared = shared + land_rank[r, :, width:]
+        for r in range(ranks):
+            sums_ref[:, r * width : (r + 1) * width] = land_rank[r, :, :width]
+        sums_ref[:, ranks * width :] = shared
+        s_job.finish(state_own)
+        for k in range(chips):
+            s_line.step(k)
+        keep.wait()
+        once(cot_own_in, other, osem.at[1])
+        once(slab(tparts, rank, second.rows), tland.at[0], osem.at[2])
+        second.arrive()
+        norm_acc[...] = jnp.zeros_like(norm_acc)
+        gain = gain_ref[...]
+
+        def last(at):
+            grad = second.total(at)
+            v = res[at].astype(f32)
+            scaling = lax.rsqrt(jnp.mean(v * v, axis=1, keepdims=True) + epsilon)
+            norm_acc[...] += fold(grad * v * scaling)
+            grad = grad * gain
+            along = jnp.sum(grad * v, axis=1, keepdims=True)
+            weight = scaling * scaling * scaling * along / model
+            wide_out[at] = other[at].astype(f32) + scaling * grad - v * weight
+
+        row_loop(second.rows, 16, last)
+        keep_grad = pltpu.make_async_copy(wide_out, res_grad, osem.at[2])
+        keep_grad.start()
+        line = jnp.sum(norm_acc[...], axis=0, keepdims=True)
+        eighth = model // 8
+        for i in range(8):
+            norm_rank[rank, i : i + 1, :] = line[:, i * eighth : (i + 1) * eighth]
+        across = everyone(norm_rank, rank, ranks, nsend, nrecv, over_rank)
+        for copy in across:
             copy.start()
+        s_line.finish()
+
+        def lower(at):
+            state_low[at] = state_line[at].astype(bf16)
+
+        row_loop(state_low.shape[0], 64, lower)
+        s_rank.step(0)
+        for copy in across:
             copy.wait()
-        pack_ref[...] = jnp.zeros_like(pack_ref)
-        for k in range(5):
-            rows = slice(8 * k, 8 * k + 8)
-            pack_ref[k : k + 1, :width] = jnp.sum(gtapx[rows], axis=0, keepdims=True)
-            pack_ref[k : k + 1, width:] = jnp.sum(gtapbc[rows], axis=0, keepdims=True)
-        pack_ref[5:6, :width] = jnp.sum(ggain_ref[...], axis=0, keepdims=True)
-        for k in range(3):
-            pack_ref[6:7, k * LANES : (k + 1) * LANES] = jnp.sum(
-                gpar[8 * k : 8 * k + 8], axis=0, keepdims=True
-            )
-        across.arrive()
-
-        def residual(at):
-            block_out[at] = res_ref[at].astype(f32) + across.total(at)
-
-        row_loop(across.rows, 16, residual)
-        job0.finish()
-        job1.finish()
+        norm_dp[me] = added(norm_rank, ranks)
+        along_dp = everyone(norm_dp, me, devices, msend, mrecv, over_dp)
+        for copy in along_dp:
+            copy.start()
+        s_rank.step(1)
+        x_job.finish(line_out)
+        once(line_out, x_sum, osem.at[0])
+        s_rank.finish()
+
+        def state(at):
+            state_ref[at] = state_all[at].astype(f32)
+
+        row_loop(state_ref.shape[0], 64, state)
+        for copy in along_dp:
+            copy.wait()
+        norm_ref[...] = added(norm_dp, devices)
+        keep_grad.wait()
 
 
 def backward(
-    number, chips, ranks, residual, ws, ggain, gz, ng, normed, cot, wo, wz, wx,
-    x, bc, st, seg, gy, y, h, tapx, tapbc, par, spread, skip, nseq,
+    number, chips, ranks, ggain, norm_gain, residual, cot_own, ws, gz, ng, normed, cot, wo, wz, wx,
+    x, conv, bc, convbc, st, seg, gy, y, h, tapx, tapbc, par, spread, skip, nseq,
 ):
     tokens, width = x.shape
-    model = normed.shape[1]
+    rows, model = residual.shape
     n = BLOCK
     blocks = tokens // nseq // n
     at = lambda s, i: (s * blocks + blocks - 1 - i, 0)
@@ -1203,43 +1358,41 @@
     states = LANES
     full = lambda v: pl.BlockSpec(v.shape, whole)
     once = lambda shape: pl.BlockSpec(shape, whole)
-    own = model // (2 * chips)
-    depth = model // ranks
+    devices = 2 * chips
+    own, depth, wide = model // devices, model // ranks, width + 2 * states
     return pl.pallas_call(
         functools.partial(backward_kernel, blocks, nseq * blocks, chips, ranks),
         grid=(nseq, blocks),
         in_specs=[
             pl.BlockSpec((n, width), at),
-            pl.BlockSpec((8, width), tail),
+            pl.BlockSpec((n, width), at),
             pl.BlockSpec((n, 2 * states), at),
-            pl.BlockSpec((8, 2 * states), tail),
+            pl.BlockSpec((n, 2 * states), at),
             pl.BlockSpec((n, LANES), at),
             pl.BlockSpec((n, LANES), at),
             pl.BlockSpec((8, LANES), tail),
             pl.BlockSpec((n, width), at),
             pl.BlockSpec((n, width), at),
             pl.BlockSpec((states, width), at),
-            full(tapx), full(tapbc), full(par), full(spread), full(skip),
-            full(residual), full(ws), full(ggain),
+            full(tapx), full(tapbc), full(par), full(spread), full(skip), full(ggain), full(norm_gain),
         ]
-        + [ANY] * 7,
+        + [ANY] * 10,
         out_specs=[
-            once((own, width)), once((own, width)), once(residual.shape), once((8, width + 2 * states)),
+            once((8, width * ranks + 2 * states)), once((8, model // 8)), once((model, 2 * states)),
         ]
-        + [ANY] * 7,
+        + [ANY] * 13,
         out_shape=[
-            shaped((own, width), f32), shaped((own, width), f32), shaped(residual.shape, f32),
-            shaped((8, width + 2 * states), f32),
+            shaped((8, width * ranks + 2 * states), f32), shaped((8, model // 8), f32),
+            shaped((model, 2 * states), f32),
+            shaped((own, width), f32), shaped((own, width), f32), shaped((own, width + LANES), f32),
+            shaped((rows, model), f32), shaped((rows, model), f32),
             shaped((model, width + LANES), bf16), shaped((tokens, model), bf16),
             shaped((depth, 2 * states), f32),
             shaped((model, width), bf16), shaped((model, width), bf16), shaped((tokens, model), bf16),
-            shaped((ranks * tokens, 2 * states), bf16),
+            shaped((ranks * tokens, 2 * states), bf16), shaped((ranks, rows, model), bf16),
         ],
         scratch_shapes=[
-            pltpu.VMEM((states, width), f32),
-            pltpu.VMEM((8, width), f32),
-            pltpu.VMEM((8, 2 * states), f32),
-            pltpu.VMEM((8, LANES), jnp.int32),
+            *scan_bwd_scratch(width, states),
             pltpu.VMEM((tokens, width + LANES), bf16),
             pltpu.VMEM((tokens, 2 * states), bf16),
             pltpu.VMEM((40, width), f32),
@@ -1253,160 +1406,39 @@
             pltpu.VMEM((2, CHUNK, width), bf16),
             pltpu.VMEM((2, CHUNK, width + LANES), bf16),
             pltpu.VMEM((tokens, 2 * states), f32),
-            pltpu.VMEM((CHUNK, 2 * states), f32),
-            *[dma(2)] * 6,
+            pltpu.VMEM((model, 2 * states), bf16),
+            pltpu.VMEM((rows, model), bf16),
+            pltpu.VMEM((rows, model), bf16),
+            pltpu.VMEM((rows, model), f32),
+            pltpu.VMEM((own, width + LANES), f32),
+            pltpu.VMEM((ranks, rows, model), bf16),
+            pltpu.VMEM((2, CHUNK, 2 * states), f32),
+            pltpu.VMEM((depth // devices, 2 * states), f32),
+            pltpu.VMEM((depth, 2 * states), f32),
+            pltpu.VMEM((depth, 2 * states), bf16),
+            pltpu.VMEM((model, 2 * states), bf16),
+            pltpu.VMEM((8, wide), f32),
+            pltpu.VMEM((8 * devices, wide), f32),
+            pltpu.VMEM((ranks, 8, wide), f32),
+            pltpu.VMEM((ranks, 8, model // 8), f32),
+            pltpu.VMEM((devices, 8, model // 8), f32),
+            pltpu.VMEM((8, model), f32),
+            dma(4), *[dma(2)] * 5, dma(3),
+            *[dma(ranks)] * 4, *[dma(devices)] * 2,
             *LineScatter.scratch(chips, (model, width)),
             *LineScatter.scratch(chips, (model, width)),
-            *TensorScatter.scratch(ranks, (tokens, model)),
-            *TensorGather.scratch(ranks),
+            *LineScatter.scratch(chips, (model, width + LANES)),
+            *LineScatter.scratch(chips, (depth, 2 * states), f32),
+            *TensorScatter.scratch(ranks), *TensorScatter.scratch(ranks),
+            *TensorGather.scratch(ranks), *LineGather.scratch(chips),
+            *TensorGather.scratch(ranks), *LineGather.scratch(chips),
         ],
         compiler_params=params(number),
         name="backward",
     )(
-        x, x, bc, bc, st, seg, seg, gy, y, h, tapx, tapbc, par, spread, skip,
-        residual, ws, ggain, gz, ng, normed, cot, wo, wz, wx,
+        x, conv, bc, convbc, st, seg, seg, gy, y, h, tapx, tapbc, par, spread, skip, ggain, norm_gain,
+        residual, cot_own, ws, gz, ng, normed, cot, wo, wz, wx,
     )
-
-
-def everyone(buffer, mine, count, send, recv, device):
-    row = buffer.at[mine]
-    return [
-        remote(row, row, send.at[k], recv.at[k], *device(lax.rem(mine + k, count)))
-        for k in range(1, count)
-    ]
-
-
-def added(buffer, count):
-    total = buffer[0]
-    for k in range(1, count):
-        total = total + buffer[k]
-    return total
-
-
-def finish_kernel(chips, ranks, *refs):
-    (pack_ref, res_ref, cot_ref, gain_ref, xparts, tparts, sparts), refs = refs[:7], refs[7:]
-    (x_ref, out_ref, state_ref, sums_ref, norm_ref), refs = refs[:5], refs[5:]
-    (state_own, state_line, state_low, state_all, land_dp, land_rank, norm_rank, norm_dp, norm_acc), refs = refs[:9], refs[9:]
-    (psend, precv, qsend, qrecv, nsend, nrecv, msend, mrecv), refs = refs[:8], refs[8:]
-    x_job = LineScatter(xparts, x_ref, *refs[:7], chips)
-    s_job = LineScatter(sparts, state_own, *refs[7:14], chips)
-    across = TensorScatter(tparts, *refs[14:18], ranks)
-    s_line = LineGather(state_own, state_line, *refs[18:21], chips)
-    s_rank = TensorGather(state_low, state_all, *refs[21:24], ranks)
-    me, rank, devices = x_job.me, x_job.rank, 2 * chips
-    over_dp = lambda d: (d, rank)
-    over_rank = lambda r: (me, r)
-    width = x_ref.shape[1] - LANES
-    greet_all(chips, ranks)
-    s_job.step(0)
-    x_job.step(0)
-    across.step(0)
-    land_dp[me] = pack_ref[...]
-    first = everyone(land_dp, me, devices, psend, precv, over_dp)
-    for copy in first:
-        copy.start()
-    s_job.step(1)
-    x_job.step(1)
-    for copy in first:
-        copy.wait()
-    land_rank[rank] = added(land_dp, devices)
-    second = everyone(land_rank, rank, ranks, qsend, qrecv, over_rank)
-    for copy in second:
-        copy.start()
-    for k in range(2, chips):
-        s_job.step(k)
-        x_job.step(k)
-    s_job.finish()
-    for k in range(chips):
-        s_line.step(k)
-    s_line.finish()
-
-    def lower(at):
-        state_low[at] = state_line[at].astype(bf16)
-
-    row_loop(state_low.shape[0], 64, lower)
-    s_rank.step(0)
-    for copy in second:
-        copy.wait()
-    shared = land_rank[0, :, width:]
-    for r in range(1, ranks):
-        shared = shared + land_rank[r, :, width:]
-    for r in range(ranks):
-        sums_ref[:, r * width : (r + 1) * width] = land_rank[r, :, :width]
-    sums_ref[:, ranks * width :] = shared
-    across.arrive()
-    norm_acc[...] = jnp.zeros_like(norm_acc)
-    gain = gain_ref[...]
-    model = gain.shape[1]
-
-    def last(at):
-        grad = across.total(at)
-        v = res_ref[at].astype(f32)
-        scaling = lax.rsqrt(jnp.mean(v * v, axis=1, keepdims=True) + epsilon)
-        norm_acc[...] += fold(grad * v * scaling)
-        grad = grad * gain
-        along = jnp.sum(grad * v, axis=1, keepdims=True)
-        weight = scaling * scaling * scaling * along / model
-        out_ref[at] = cot_ref[at].astype(f32) + scaling * grad - v * weight
-
-    row_loop(across.rows, 16, last)
-    row = jnp.sum(norm_acc[...], axis=0, keepdims=True)
-    eighth = model // 8
-    for i in range(8):
-        norm_rank[rank, i : i + 1, :] = row[:, i * eighth : (i + 1) * eighth]
-    third = everyone(norm_rank, rank, ranks, nsend, nrecv, over_rank)
-    for copy in third:
-        copy.start()
-    s_rank.step(1)
-    for copy in third:
-        copy.wait()
-    norm_dp[me] = added(norm_rank, ranks)
-    fourth = everyone(norm_dp, me, devices, msend, mrecv, over_dp)
-    for copy in fourth:
-        copy.start()
-    x_job.finish()
-    s_rank.finish()
-
-    def state(at):
-        state_ref[at] = state_all[at].astype(f32)
-
-    row_loop(state_ref.shape[0], 64, state)
-    for copy in fourth:
-        copy.wait()
-    norm_ref[...] = added(norm_dp, devices)
-
-
-def finish(number, chips, ranks, pack, residual, cot, norm_gain, xparts, tparts, sparts):
-    rows, model = residual.shape
-    devices = 2 * chips
-    own = model // devices
-    depth, states = sparts.shape
-    wide = pack.shape[1]
-    width = wide - states
-    return pl.pallas_call(
-        functools.partial(finish_kernel, chips, ranks),
-        in_specs=[ONCHIP] * 4 + [ANY] * 3,
-        out_specs=[ONCHIP] * 5,
-        out_shape=[
-            shaped((own, xparts.shape[1]), f32), shaped((rows, model), f32), shaped((model, states), f32),
-            shaped((8, width * ranks + states), f32), shaped((8, model // 8), f32),
-        ],
-        scratch_shapes=[
-            pltpu.VMEM((depth // devices, states), f32), pltpu.VMEM((depth, states), f32),
-            pltpu.VMEM((depth, states), bf16), pltpu.VMEM((model, states), bf16),
-            pltpu.VMEM((devices, 8, wide), f32), pltpu.VMEM((ranks, 8, wide), f32),
-            pltpu.VMEM((ranks, 8, model // 8), f32), pltpu.VMEM((devices, 8, model // 8), f32),
-            pltpu.VMEM((8, model), f32),
-            dma(devices), dma(devices), dma(ranks), dma(ranks),
-            dma(ranks), dma(ranks), dma(devices), dma(devices),
-            *LineScatter.scratch(chips, xparts.shape),
-            *LineScatter.scratch(chips, sparts.shape, f32),
-            *TensorScatter.scratch(ranks, tparts.shape),
-            *LineGather.scratch(chips), *TensorGather.scratch(ranks),
-        ],
-        compiler_params=params(number),
-        name="finish",
-    )(pack, residual, cot, norm_gain, xparts, tparts, sparts)
 
 
 def per_device(
@@ -1440,17 +1472,15 @@
     x, st, bc, normed, wx = project(
         1, chips, ranks, residual, norm_gain[None], state_weight, wx_own
     )
-    y, h, wz, cot = scan_forward_gather(
+    y, h, conv, convbc, wz, cot = scan_forward_gather(
         2, chips, ranks, inner_weight[:, 0], cotangent,
         x, bc, st, seg, tapx, tapbc, par, spread, skip, nseq,
     )
     gz, gy, ng, ggain, wo = gate(3, chips, ranks, gain, out_weight.T, normed, wz, y, cot)
-    z_grad, out_grad, block_out, pack, xparts, tparts, sparts, *_ = backward(
-        4, chips, ranks, residual, state_weight, ggain, gz, ng, normed, cot, wo, wz, wx,
-        x, bc, st, seg, gy, y, h, tapx, tapbc, par, spread, skip, nseq,
-    )
-    x_grad, residual_grad, state_grad, sums, norm_grad = finish(
-        5, chips, ranks, pack, residual, cotangent, norm_gain[None], xparts, tparts, sparts
+    sums, norm_grad, state_grad, z_grad, out_grad, x_grad, block_out, residual_grad, *_ = backward(
+        4, chips, ranks, ggain, norm_gain[None], residual, cotangent, state_weight,
+        gz, ng, normed, cot, wo, wz, wx,
+        x, conv, bc, convbc, st, seg, gy, y, h, tapx, tapbc, par, spread, skip, nseq,
     )
     inner_grad = jnp.stack([z_grad, x_grad[:, :width]], axis=1)
     by_head = sums[6, :inner_width].reshape(ranks, width)

time: 431 us -> 400 us (0.928)
  Pallas kernels: 389 us -> 358 us
    pallas_call x1 -> x0, Pallas kernels: 99.3 us -> none  [finish(): pl.pallas_call(functools.partial(finish_kernel, chips, ranks), in_specs=[...]
    pallas_call x1, Pallas kernels: 119 us -> 194 us  [backward(): pl.pallas_call(functools.partial(backward_kernel, blocks, nseq * blocks,...]
    pallas_call x1, Pallas kernels: 52.9 us -> 45.4 us  [scan_forward_gather(): pl.pallas_call(functools.partial(scan_gather_kernel, blocks, nseq * block...]
    unnamed x19 -> x21, local copies, waits for them, and re-layouts: 16.4 us -> 15.9 us
where the time goes in v4:
time: 400 us; the launch traced here: 397 us
  Pallas kernels  358 us (90%)
  local copies, waits for them, and re-layouts  34.9 us (9%)
    pallas_call x1, Pallas kernels, backward(): pl.pallas_call(functools.partial(backward_kernel, blocks, nseq * blocks,...  194 us
    pallas_call x1, Pallas kernels, gate(): pl.pallas_call(functools.partial(gate_kernel, chips, ranks), in_specs=[ON...  61.7 us
    pallas_call x1, Pallas kernels, project(): pl.pallas_call(functools.partial(project_kernel, chips, ranks), in_specs=...  57.7 us
    pallas_call x1, Pallas kernels, scan_forward_gather(): pl.pallas_call(functools.partial(scan_gather_kernel, blocks, nseq * block...  45.4 us
    unnamed x21, local copies, waits for them, and re-layouts  15.9 us

profile of v4, /device:TPU:0, one launch (start us, length us, event | category | flops | bytes accessed | tf_op | source)
XLA Modules:
  0.0 397.4 jit_solution(16657889576783421456)
XLA Ops:
  6.7 1.0 maximum_maximum_fusion
  8.9 0.8 fusion.refs_7_.refs_13_
  9.8 1.7 broadcast_in_dim.44.refs_3_.refs_5_.refs_6_
  11.4 2.0 copy.30
  13.5 1.5 fusion.4
  15.0 1.2 copy_bitcast_fusion
  16.1 1.0 concatenate.15.wx_own
  17.1 57.7 %project.1 = (f32[1024,1024]{1,0:T(8,128)}, f32[1024,128]{1,0:T(8,128)}, f32[1024,256]{1,0:T(8,128)}, bf16[1024,2048]{1,0:T(8,128)(2,1)}, bf16[2048,1152]{1,0:T(8,128)(2,1)}) custom-call(bf16[256,2048]{1,0:T(8,128)(2,1)} %refs_17_.1, f32[1,2048]{1,0:T(1,128)} %bitcast.21, bf16[2048,256]{1,0:T(8,128)(2,1)} %refs_19_.1, bf16[256,1152]{1,0:T(8,128)(2,1)} %concatenate.15.wx_own), custom_call_target="tpu_custom_call" | custom-call | tf_op jit(solution)/shard_map/project/pallas_call | solution.py:787
  74.8 45.4 %scan_forward.1 = (f32[1024,1024]{1,0:T(8,128)}, bf16[1024,1024]{1,0:T(8,128)(2,1)}, f32[1024,1024]{1,0:T(8,128)}, f32[1024,256]{1,0:T(8,128)}, bf16[2048,1024]{1,0:T(8,128)(2,1)}, /*index=5*/bf16[1024,2048]{1,0:T(8,128)(2,1)}) custom-call(f32[1024,1024]{1,0:T(8,128)} %get-tuple-element.37.refs_0_, f32[1024,256]{1,0:T(8,128)} %get-tuple-element.38.refs_1_.refs_2_, ...), custom_call_target="tpu_custom_call" | custom-call | tf_op jit(solution)/shard_map/scan_forward/pallas_call | solution.py:844
  120.2 61.7 %gate.1 = (bf16[1024,1024]{1,0:T(8,128)(2,1)}, f32[1024,1024]{1,0:T(8,128)}, bf16[1024,1024]{1,0:T(8,128)(2,1)}, f32[8,1024]{1,0:T(8,128)}, bf16[2048,1024]{1,0:T(8,128)(2,1)}) custom-call(f32[8,1024]{1,0:T(8,128)} %broadcast_in_dim.53.gain_ref, bf16[256,1024]{1,0:T(8,128)(2,1)} %bitcast.18, bf16[1024,2048]{1,0:T(8,128)(2,1)} %get-tuple-element.42.normed_in.refs_22_, ...), custom_call_target="tpu_custom_call" | custom-call | tf_op jit(solution)/shard_map/gate/pallas_call | solution.py:996
  181.9 193.6 %backward.1 = (f32[8,4352]{1,0:T(8,128)}, f32[8,256]{1,0:T(8,128)}, f32[2048,256]{1,0:T(8,128)}, f32[256,1024]{1,0:T(8,128)}, f32[256,1024]{1,0:T(8,128)}, /*ind...) custom-call(f32[1024,1024]{1,0:T(8,128)} %get-tuple-element.37.refs_, ...), custom_call_target="tpu_custom_call" | custom-call | tf_op jit(solution)/shard_map/backward/pallas_call | solution.py:1363
  375.4 1.4 copy.36
  376.8 1.6 slice_reduce_fusion
  378.4 1.6 fusion.5
  380.0 1.5 slice.41
  383.4 0.9 slice.40
  384.3 1.3 slice_bitcast_fusion
  386.5 2.9 copy.31
  389.4 1.3 copy.33
  391.4 1.3 copy.42
  392.7 1.0 copy-done.2
  393.8 1.3 copy.43
  395.1 1.0 copy-done.1
  396.1 1.3 copy.44
  (40 shorter events, 10.7 us)
Async XLA Ops:
  0.6 12.8 %copy-start = (bf16[256,2,1024]{2,1,0:T(2,128)(2,1)S(1)}, bf16[256,2,1024]{2,1,0:T(2,128)(2,1)}, u32[]{:S(2)}) copy-start(bf16[256,2,1024]{2,1,0:T(2,128)(2,1)} %param.17) | copy-start | bytes 3145732
  375.4 10.8 %copy-start.5 = (f32[256,1024]{1,0:T(8,128)S(1)}, f32[256,1024]{1,0:T(8,128)}, u32[]{:S(2)}) copy-start(f32[256,1024]{1,0:T(8,128)} %get-tuple-element.56) | copy-start | bytes 3145732
  386.5 3.0 copy-start.4
  389.4 2.0 copy-start.3
  391.4 2.3 copy-start.2
  393.8 2.3 copy-start.1

commit v5 on v4

--- a/solution.py
+++ b/solution.py
@@ -147,7 +147,7 @@
     blocks, x_ref, conv_ref, bc_ref, convbc_ref, st_ref, seg_ref, segt_ref, gy_ref, y_ref, h_ref,
     tapx_ref, tapbc_ref, par_ref, spread_ref, skip_ref,
     gx_ref, gbc_ref, gst_ref, gtapx_ref, gtapbc_ref, gpar_ref,
-    gstate, head_x, head_bc, head_seg, xs_s, slope_s, back_s, dt_s, onto_s, xd_s, into_s, onto_low, sums_s,
+    gstate, head_x, head_bc, head_seg, xs_s, slope_s, back_s, dt_s, onto_s, xd_s, sums_s,
 ):
     n = BLOCK
     step = pl.program_id(1)
@@ -191,6 +191,7 @@
     halves = lambda t: jnp.concatenate(
         [jnp.where(first_half, t, 0.0), jnp.where(first_half, 0.0, t)], axis=0
     ).astype(bf16)
+    into_s, onto_low = sums_s.at[0:n], sums_s.at[n : 2 * n]
     pairs = [slice(i, i + LANES) for i in range(0, x_ref.shape[1], LANES)]
 
     for sl in pairs:
@@ -304,7 +305,7 @@
         pltpu.VMEM((8, 2 * states), f32),
         pltpu.VMEM((8, LANES), jnp.int32),
         *[pltpu.VMEM((n, width), f32)] * 5,
-        *[pltpu.VMEM((n, width), bf16)] * 3,
+        pltpu.VMEM((n, width), bf16),
         pltpu.VMEM((5 * n + 32, width), bf16),
     ]
 
@@ -522,22 +523,23 @@
 def add_rows(target, others, out=None):
     out = target if out is None else out
     rows = target.shape[0]
-    some = 32 if rows % 32 == 0 else 16 if rows % 16 == 0 else 8
-
-    @pl.loop(0, rows // some)
-    def _(i):
-        at = pl.ds(pl.multiple_of(i * some, some), some)
-        total = target[at].astype(f32)
+    some = 64 if rows % 64 == 0 else rows
+    kind = out.dtype if len(others) == 1 else f32
+
+    def add(at):
+        total = target[at].astype(kind)
         for other in others:
-            total = total + other[at].astype(f32)
+            total = total + other[at].astype(kind)
         out[at] = total.astype(out.dtype)
 
+    row_loop(rows, some, add)
+
 
 class LineScatter:
-    def __init__(self, parts, swap, flow, send, recv, temp, tsem, chips):
+    def __init__(self, parts, swap, flow, send, recv, chips):
         self.parts, self.swap, self.flow = parts, swap, flow
-        self.send, self.recv, self.temp, self.tsem, self.chips = send, recv, temp, tsem, chips
-        self.rows, self.wide = parts.shape[0] // (2 * chips), parts.shape[1]
+        self.send, self.recv, self.chips = send, recv, chips
+        self.rows = parts.shape[0] // (2 * chips)
         self.chip, self.core, self.rank = place()
         self.me = self.chip * 2 + self.core
         self.partner = self.chip * 2 + 1 - self.core
@@ -559,15 +561,6 @@
             slab(self.parts, 2 * c + 1 - self.core, self.rows), self.swap.at[c], self.send.at[2, c],
             self.recv.at[2, c], self.partner, self.rank,
         )
-
-    def load(self, i):
-        c = self.order()[i]
-        return pltpu.make_async_copy(
-            slab(self.parts, 2 * c + self.core, self.rows), self.held(i), self.tsem.at[i % 2]
-        )
-
-    def held(self, i):
-        return self.temp.at[i % 2, pl.ds(0, self.rows), pl.ds(0, self.wide)]
 
     def along(self, way, c, first=False):
         if way == 0:
@@ -580,29 +573,33 @@
             self.me + (2, -2)[way], self.rank,
         )
 
-    def step(self, k):
+    def send_off(self, c):
+        n, chip = self.chips, self.chip
+
+        @pl.when((chip == 0) & (c > 0))
+        def _():
+            self.along(0, c, True).start()
+
+        @pl.when((chip == n - 1) & (c < n - 1))
+        def _():
+            self.along(1, c, True).start()
+
+    def send_rest(self):
+        for c in self.order()[2:]:
+            self.send_off(c)
+
+    def step(self, k, hold=False):
         n, chip = self.chips, self.chip
         if k == 0:
             for c in self.order():
                 self.over(c).start()
             return
         if k == 1:
-            self.load(0).start()
-            self.load(1).start()
             for i, c in enumerate(self.order()):
                 self.over(c).wait()
-                self.load(i).wait()
-                add_rows(self.swap.at[c], [self.held(i)])
-                if i + 2 < n:
-                    self.load(i + 2).start()
-
-                @pl.when((chip == 0) & (c > 0))
-                def _():
-                    self.along(0, c, True).start()
-
-                @pl.when((chip == n - 1) & (c < n - 1))
-                def _():
-                    self.along(1, c, True).start()
+                add_rows(self.swap.at[c], [slab(self.parts, 2 * c + self.core, self.rows)])
+                if i < 2 or not hold:
+                    self.send_off(c)
             return
         t = k - 1
         c = n - 1 - (t - chip)
@@ -651,26 +648,17 @@
                 self.along(1, c).wait_send()
 
 
-class TensorScatter:
-    def __init__(self, parts, land, send, recv, local, ranks):
-        self.parts, self.land = parts, land
-        self.send, self.recv, self.local, self.ranks = send, recv, local, ranks
+class DirectScatter:
+    def __init__(self, parts, land, temp, send, recv, tsem, ranks):
+        self.parts, self.land, self.temp = parts, land, temp
+        self.send, self.recv, self.tsem, self.ranks = send, recv, tsem, ranks
         self.rows = parts.shape[0] // ranks
         chip, core, self.rank = place()
         self.me = chip * 2 + core
-        self.steps = 1
 
     @staticmethod
     def scratch(ranks):
-        return [
-            pltpu.SemaphoreType.DMA((ranks,)), pltpu.SemaphoreType.DMA((ranks,)),
-            pltpu.SemaphoreType.DMA,
-        ]
-
-    def load(self):
-        return pltpu.make_async_copy(
-            slab(self.parts, self.rank, self.rows), self.land.at[0], self.local
-        )
+        return [dma(ranks), dma(ranks), dma(2)]
 
     def copy(self, k):
         to = lax.rem(self.rank + k, self.ranks)
@@ -679,19 +667,202 @@
             self.me, to,
         )
 
-    def step(self, k):
-        for j in range(1, self.ranks):
-            self.copy(j).start()
+    def step(self, k, g):
+        if k == 0 and g == 1:
+            for j in range(1, self.ranks):
+                self.copy(j).start()
 
     def arrive(self):
         for j in range(1, self.ranks):
             self.copy(j).wait()
 
-    def total(self, at):
-        total = self.land[0, at].astype(f32)
-        for j in range(1, self.ranks):
-            total = total + self.land[j, at].astype(f32)
-        return total
+    def totals(self, some, body):
+        @pl.loop(0, self.rows // some)
+        def _(i):
+            at = pl.ds(pl.multiple_of(i * some, some), some)
+            total = None
+            for j in range(self.ranks):
+                src = slab(self.parts, self.rank * (self.rows // some) + i, some) if j == 0 else self.land.at[j, at]
+                copy = pltpu.make_async_copy(src, self.temp.at[j % 2, pl.ds(0, some)], self.tsem.at[j % 2])
+                copy.start()
+                copy.wait()
+                v = self.temp[j % 2, pl.ds(0, some)].astype(f32)
+                total = v if total is None else total + v
+            body(at, total)
+
+
+class SmallScatter:
+    def __init__(self, parts, swap, land, send, recv, chips):
+        self.parts, self.swap, self.land, self.send, self.recv = parts, swap, land, send, recv
+        self.chips, self.rows = chips, parts.shape[0] // (2 * chips)
+        self.chip, self.core, self.rank = place()
+
+    @staticmethod
+    def scratch(chips, shape, dtype):
+        block = pltpu.VMEM((chips, shape[0] // (2 * chips), shape[1]), dtype)
+        return [
+            block, block, pltpu.SemaphoreType.DMA((2, chips)), pltpu.SemaphoreType.DMA((2, chips)),
+        ]
+
+    def over(self, c):
+        return remote(
+            slab(self.parts, 2 * c + 1 - self.core, self.rows), self.swap.at[c], self.send.at[0, c],
+            self.recv.at[0, c], self.chip * 2 + 1 - self.core, self.rank,
+        )
+
+    def straight(self, k):
+        to = lax.rem(self.chip + k, self.chips)
+        return remote(
+            self.swap.at[to], self.land.at[self.chip], self.send.at[1, k], self.recv.at[1, k],
+            2 * to + self.core, self.rank,
+        )
+
+    def step(self, k):
+        if k == 0:
+            for c in range(self.chips):
+                self.over(c).start()
+            return
+        for c in range(self.chips):
+            self.over(c).wait()
+            add_rows(self.swap.at[c], [slab(self.parts, 2 * c + self.core, self.rows)])
+        for j in range(1, self.chips):
+            self.straight(j).start()
+
+    def finish(self, out):
+        for j in range(1, self.chips):
+            self.straight(j).wait()
+        total = self.swap[self.chip].astype(f32)
+        for j in range(1, self.chips):
+            total = total + self.land[lax.rem(self.chip + j, self.chips)].astype(f32)
+        out[...] = total.astype(out.dtype)
+
+
+class SmallGather:
+    def __init__(self, own, slots, send, recv, chips):
+        self.own, self.slots, self.send, self.recv = own, slots, send, recv
+        self.chips, self.rows = chips, own.shape[0]
+        self.chip, self.core, self.rank = place()
+        self.me = self.chip * 2 + self.core
+
+    @staticmethod
+    def scratch(chips):
+        return [pltpu.SemaphoreType.DMA((2, chips)), pltpu.SemaphoreType.DMA((2, chips))]
+
+    def straight(self, k):
+        slot = slab(self.slots, self.me, self.rows)
+        return remote(
+            self.own, slot, self.send.at[0, k], self.recv.at[0, k],
+            2 * lax.rem(self.chip + k, self.chips) + self.core, self.rank,
+        )
+
+    def over(self, k):
+        slot = slab(
+            self.slots, 2 * lax.rem(self.chip + self.chips - k, self.chips) + self.core, self.rows
+        )
+        return remote(
+            self.own if k == 0 else slot, slot, self.send.at[1, k], self.recv.at[1, k],
+            self.chip * 2 + 1 - self.core, self.rank,
+        )
+
+    def step(self, k):
+        if k == 0:
+            for j in range(1, self.chips):
+                self.straight(j).start()
+            self.over(0).start()
+            self.slots[pl.ds(pl.multiple_of(self.me * self.rows, self.rows), self.rows)] = self.own[...]
+            return
+        for j in range(1, self.chips):
+            self.straight(j).wait_recv()
+            self.over(j).start()
+
+    def finish(self):
+        for j in range(1, self.chips):
+            self.straight(j).wait_send()
+        for j in range(self.chips):
+            self.over(j).wait()
+
+
+class HalvesScatter:
+    def __init__(self, parts, land, temp, send, recv, tsem):
+        self.parts, self.land, self.temp, self.send, self.recv, self.tsem = parts, land, temp, send, recv, tsem
+        chip, core, self.rank = place()
+        self.me = chip * 2 + core
+        self.rows = parts.shape[0] // 4
+        self.half, self.wide = self.rows // 2, parts.shape[1] // 2
+        x, y = self.rank % 2, self.rank // 2
+        self.across = (y * 2 + 1 - x, (1 - y) * 2 + x)
+        self.far = (1 - y) * 2 + 1 - x
+
+    @staticmethod
+    def scratch(shape):
+        return [
+            pltpu.VMEM((2, 6, shape[0] // 8, shape[1] // 2), bf16),
+            *[pltpu.SemaphoreType.DMA((2, n)) for n in (6, 6, 2)],
+        ]
+
+    @staticmethod
+    def temp(shape):
+        return pltpu.VMEM((2, 2, shape[0] // 8, shape[1] // 2), bf16)
+
+    def part(self, g, owner, way):
+        return slab(self.parts.at[:, pl.ds(g * self.wide, self.wide)], owner * 2 + way, self.half)
+
+    def copy(self, g, i):
+        if i < 4:
+            way = i // 2
+            src = self.part(g, self.across[way] if i % 2 == 0 else self.far, way)
+            to = self.across[way]
+        else:
+            way = i - 4
+            src, to = self.land.at[g, 2 * way + 1], self.across[1 - way]
+        return remote(
+            src, self.land.at[g, i], self.send.at[g, i], self.recv.at[g, i], self.me, to
+        )
+
+    def fetch(self, g, owner, way):
+        return pltpu.make_async_copy(
+            self.part(g, owner, way), self.temp.at[g, way], self.tsem.at[g, way]
+        )
+
+    def step(self, k, g):
+        if k == 0:
+            for i in (1, 3, 0, 2):
+                self.copy(g, i).start()
+            return
+        for way in (0, 1):
+            self.fetch(g, self.across[1 - way], way).start()
+        for way in (0, 1):
+            self.copy(g, 2 * way + 1).wait_recv()
+            self.fetch(g, self.across[1 - way], way).wait()
+            add_rows(self.land.at[g, 2 * way + 1], [self.temp.at[g, way]])
+            self.copy(g, 4 + way).start()
+        for way in (0, 1):
+            self.fetch(g, self.rank, way).start()
+
+    def arrive(self):
+        for g in (0, 1):
+            for way in (0, 1):
+                self.copy(g, 2 * way + 1).wait_send()
+                self.copy(g, 2 * way).wait()
+                self.copy(g, 4 + way).wait()
+                self.fetch(g, self.rank, way).wait()
+
+    def totals(self, some, body):
+        for way in (0, 1):
+            def add(i):
+                at = pl.ds(pl.multiple_of(i * some, some), some)
+                total = jnp.concatenate(
+                    [
+                        self.temp[g, way, at].astype(f32)
+                        + self.land[g, 2 * way, at].astype(f32)
+                        + self.land[g, 4 + way, at].astype(f32)
+                        for g in (0, 1)
+                    ],
+                    axis=1,
+                )
+                body(pl.ds(pl.multiple_of(way * self.half + i * some, some), some), total)
+
+            pl.loop(0, self.half // some)(add)
 
 
 def row_loop(rows, some, body):
@@ -1015,92 +1186,88 @@
     )(gain, wo_own, normed, wz, y, cot)
 
 
-def stream_grads(src, grad, parts, wide, cbuf, stage, csem, ssem):
-    count = src.shape[1] // CHUNK
-
-    def load(j):
+class Grads:
+    def __init__(self, src, grad, parts, cbuf, csem):
+        self.src, self.grad, self.parts, self.cbuf, self.csem = src, grad, parts, cbuf, csem
+        self.count = src.shape[1] // CHUNK
+
+    def load(self, j):
         slot = lax.rem(j, 2)
         columns = pl.ds(pl.multiple_of(j * CHUNK, CHUNK), CHUNK)
-        return pltpu.make_async_copy(src.at[:, columns], cbuf.at[slot], csem.at[slot])
-
-    def store(j):
-        slot = lax.rem(j, 2)
         return pltpu.make_async_copy(
-            stage.at[slot, :, pl.ds(0, wide)], slab(parts, j, CHUNK), ssem.at[slot]
+            self.src.at[:, columns], self.cbuf.at[slot], self.csem.at[slot]
         )
 
-    load(0).start()
-
-    @pl.loop(0, count)
-    def _(j):
-        slot = lax.rem(j, 2)
-
-        @pl.when(j + 1 < count)
-        def _():
-            load(j + 1).start()
-
-        load(j).wait()
-
-        @pl.when(j >= 2)
-        def _():
-            store(j - 2).wait()
-
-        stage[slot, :, :wide] = mm_tn(cbuf[slot], grad[...]).astype(bf16)
-        store(j).start()
-
-    for j in (count - 2, count - 1):
-        store(j).wait()
-
-
-def stream_back(terms, kept, parts, stage, ssem, begin=0, end=1):
-    tokens, model = parts.shape
-    base, count = int(model // CHUNK * begin), int(model // CHUNK * (end - begin))
-
-    def loads(j):
+    def begin(self):
+        self.load(0).start()
+
+    def run(self):
+        @pl.loop(0, self.count)
+        def _(j):
+            @pl.when(j + 1 < self.count)
+            def _():
+                self.load(j + 1).start()
+
+            self.load(j).wait()
+            at = pl.ds(pl.multiple_of(j * CHUNK, CHUNK), CHUNK)
+            self.parts[at] = mm_tn(self.cbuf[lax.rem(j, 2)], self.grad[...]).astype(bf16)
+
+
+class Back:
+    def __init__(self, terms, parts, stage, ssem):
+        self.terms, self.parts, self.stage, self.ssem = terms, parts, stage, ssem
+        self.count = parts.shape[1] // CHUNK
+
+    def loads(self, j):
         slot = lax.rem(j, 2)
         return [
-            pltpu.make_async_copy(slab(right, base + j, CHUNK), buffer.at[slot], sem.at[slot])
-            for _, right, buffer, sem in terms
+            pltpu.make_async_copy(slab(right, j, CHUNK), buffer.at[slot], sem.at[slot])
+            for _, right, buffer, sem in self.terms
         ]
 
-    def store(j):
+    def store(self, j):
         slot = lax.rem(j, 2)
-        columns = pl.ds(pl.multiple_of((base + j) * CHUNK, CHUNK), CHUNK)
-        return pltpu.make_async_copy(stage.at[slot], parts.at[:, columns], ssem.at[slot])
-
-    for copy in loads(0):
-        copy.start()
-
-    @pl.loop(0, count)
-    def _(j):
-        slot = lax.rem(j, 2)
-
-        @pl.when(j + 1 < count)
-        def _():
-            for copy in loads(j + 1):
-                copy.start()
-
-        for copy in loads(j):
-            copy.wait()
-
-        @pl.when(j >= 2)
-        def _():
-            store(j - 2).wait()
-
-        for r in range(0, tokens, CHUNK):
-            at = slice(r, r + CHUNK)
-            total = jnp.zeros((CHUNK, CHUNK), f32)
-            for left, _, buffer, _ in terms:
-                total = total + mm_nt(left[at], buffer[slot])
-            for left, right in kept:
-                total = total + mm_nt(
-                    left[at], right[pl.ds(pl.multiple_of((base + j) * CHUNK, CHUNK), CHUNK)]
-                )
-            stage[slot, at] = total.astype(bf16)
-        store(j).start()
-
-    for j in (count - 2, count - 1):
-        store(j).wait()
+        columns = pl.ds(pl.multiple_of(j * CHUNK, CHUNK), CHUNK)
+        return pltpu.make_async_copy(
+            self.stage.at[slot], self.parts.at[:, columns], self.ssem.at[slot]
+        )
+
+    def begin(self):
+        for copy in self.loads(0):
+            copy.start()
+
+    def run(self, between=None):
+        count = self.count
+
+        @pl.loop(0, count)
+        def _(j):
+            slot = lax.rem(j, 2)
+
+            @pl.when(j + 1 < count)
+            def _():
+                for copy in self.loads(j + 1):
+                    copy.start()
+
+            for copy in self.loads(j):
+                copy.wait()
+
+            @pl.when(j >= 2)
+            def _():
+                self.store(j - 2).wait()
+
+            if between is not None:
+                pl.when(j == count // 2 + 1)(between)
+
+            for r in range(0, self.parts.shape[0], CHUNK):
+                at = slice(r, r + CHUNK)
+                total = jnp.zeros((CHUNK, CHUNK), f32)
+                for left, _, buffer, _ in self.terms:
+                    total = total + mm_nt(left[at], buffer[slot])
+                self.stage[slot, at] = total.astype(bf16)
+            self.store(j).start()
+
+        for j in (count - 2, count - 1):
+            self.store(j).wait()
 
 
 def everyone(buffer, mine, count, send, recv, device):
@@ -1122,68 +1289,133 @@
     ins, refs = refs[:15], refs[15:]
     (ggain_ref, gain_ref), refs = refs[:2], refs[2:]
     (res_in, cot_own_in, ws_in, gz_in, ng_in, normed_in, cot_in, wo_in, wz_in, wx_in), refs = refs[:10], refs[10:]
-    (sums_ref, norm_ref, state_ref), refs = refs[:3], refs[3:]
-    (z_sum, o_sum, x_sum, block_out, res_grad), refs = refs[:5], refs[5:]
-    (xparts, tparts, sparts, zparts, oparts, pparts, gbc_slots, pland), refs = refs[:8], refs[8:]
-    scratch, refs = refs[:13], refs[13:]
-    (gxs, gbc_own, gtapx, gtapbc, gpar, gz, ng, cbuf, stage, back, wbuf, xbuf), refs = refs[:12], refs[12:]
-    (gbc_sum, ws, res, other, wide_out, line_out, tland, state_stage), refs = refs[:8], refs[8:]
-    (state_own, state_line, state_low, state_all, pack, packs, land_rank), refs = refs[:7], refs[7:]
+    (sums_ref, norm_ref), refs = refs[:2], refs[2:]
+    (z_sum, o_sum, x_sum, block_out, res_grad, state_out), refs = refs[:6], refs[6:]
+    (tparts, pparts, pland, tland), refs = refs[:4], refs[4:]
+    scratch, refs = refs[:11], refs[11:]
+    (gxs, gbc_own, gtapx, gtapbc, gpar, gz, ng, cbuf, parts, back, wbuf, xbuf), refs = refs[:12], refs[12:]
+    (gbc_slots, sbuf, wide_out, line_out, sparts, state_f, state_g), refs = refs[:7], refs[7:]
+    (state_own, state_line, state_low, land_core, land_chip, land_rank), refs = refs[:6], refs[6:]
     (norm_rank, norm_dp, norm_acc), refs = refs[:3], refs[3:]
-    (loads, csem, ssem, bsem, wsem, xsem, osem), refs = refs[:7], refs[7:]
-    (qsend, qrecv, nsend, nrecv, msend, mrecv), refs = refs[:6], refs[6:]
-    z_job = LineScatter(zparts, *refs[:4], stage, ssem, chips)
-    o_job = LineScatter(oparts, *refs[4:8], stage, ssem, chips)
-    x_job = LineScatter(xparts, *refs[8:12], stage, ssem, chips)
-    s_job = LineScatter(sparts, *refs[12:16], state_stage, csem, chips)
+    (loads, csem, bsem, wsem, xsem, ysem, osem, fsem), refs = refs[:8], refs[8:]
+    (psem, qsem, rsem, nsem, msem), refs = refs[:5], refs[5:]
+    half_parts = parts.at[:, pl.ds(0, gz.shape[1])]
+    z_job = LineScatter(half_parts, *refs[:4], chips)
+    o_job = LineScatter(half_parts, *refs[4:8], chips)
+    x_job = LineScatter(parts, *refs[8:12], chips)
+    s_job = SmallScatter(sparts, *refs[12:16], chips)
     refs = refs[16:]
-    first = TensorScatter(pparts, pland, *refs[:3], ranks)
-    second = TensorScatter(tparts, tland, *refs[3:6], ranks)
-    around = TensorGather(gbc_own, gbc_slots, *refs[6:9], ranks)
-    s_line = LineGather(state_own, state_line, *refs[9:12], chips)
-    s_rank = TensorGather(state_low, state_all, *refs[12:15], ranks)
-    p_line = LineGather(pack, packs, *refs[15:18], chips)
+    around = TensorGather(gbc_own, gbc_slots, *refs[:3], ranks)
+    s_line = SmallGather(state_own, state_line, *refs[3:5], chips)
+    state_all = gbc_slots.at[pl.ds(gz.shape[0], normed_in.shape[1])]
+    s_rank = TensorGather(state_low, state_all, *refs[5:8], ranks)
+    temp, refs = refs[8], refs[9:]
+    if ranks == 4:
+        first = HalvesScatter(pparts, refs[0], temp, *refs[1:4])
+        second = HalvesScatter(tparts, refs[4], temp, *refs[5:8])
+    else:
+        first = DirectScatter(pparts, pland, temp, *refs[:3], ranks)
+        second = DirectScatter(tparts, tland, temp, *refs[3:6], ranks)
     now = pl.program_id(0) * blocks + pl.program_id(1)
     tokens, width = gz.shape
     model = normed_in.shape[1]
     rank, me, devices = first.rank, first.me, 2 * chips
+    chip, core = z_job.chip, z_job.core
     over_dp = lambda d: (d, rank)
     over_rank = lambda r: (me, r)
+    by_core = everyone(land_core, core, 2, psem.at[0], psem.at[1], lambda c: (chip * 2 + c, rank))
+    by_chip = everyone(land_chip, chip, chips, qsem.at[0], qsem.at[1], lambda c: (c * 2 + core, rank))
+    by_rank = everyone(land_rank, rank, ranks, rsem.at[0], rsem.at[1], over_rank)
+    norm_by_rank = everyone(norm_rank, rank, ranks, nsem.at[0], nsem.at[1], over_rank)
+    norm_by_dp = everyone(norm_dp, me, devices, msem.at[0], msem.at[1], over_dp)
+
+    def begin(copies):
+        for copy in copies:
+            copy.start()
+
+    def end(copies):
+        for copy in copies:
+            copy.wait()
     fetch = [
         pltpu.make_async_copy(src, dst, loads.at[i])
-        for i, (src, dst) in enumerate(((gz_in, gz), (ng_in, ng), (ws_in, ws), (res_in, res)))
+        for i, (src, dst) in enumerate(((gz_in, gz), (ng_in, ng)))
     ]
-
-    def once(src, dst, sem):
-        copy = pltpu.make_async_copy(src, dst, sem)
-        copy.start()
-        copy.wait()
+    pieces = model // width
+    own_rows = first.rows
+
+    def piece(ref, p, at):
+        return ref[pl.ds(pl.multiple_of(at.start + p * own_rows, 16), at.size)]
+
+    def pieced(ref, at):
+        return jnp.concatenate([piece(ref, p, at) for p in range(pieces)], axis=1).astype(f32)
+
+    def own_copies(src, ref, sems):
+        return [
+            pltpu.make_async_copy(
+                src.at[:, pl.ds(p * width, width)], ref.at[pl.ds(p * own_rows, own_rows)], sems.at[p]
+            )
+            for p in range(pieces)
+        ]
+
+    own_res = own_copies(res_in, gz, fsem.at[0])
+    own_cot = own_copies(cot_own_in, ng, fsem.at[1])
+    half_out = line_out.at[:, pl.ds(0, width)]
+    keep_z = pltpu.make_async_copy(half_out, z_sum, osem.at[0])
+    keep_o = pltpu.make_async_copy(half_out, o_sum, osem.at[0])
+    keep_x = pltpu.make_async_copy(line_out, x_sum, osem.at[0])
+    keep_block = pltpu.make_async_copy(wide_out, block_out, osem.at[2])
+    keep_grad = pltpu.make_async_copy(wide_out, res_grad, osem.at[2])
+
+    z_part = Grads(normed_in, gz, half_parts, cbuf, csem)
+    o_part = Grads(cot_in, ng, half_parts, cbuf, csem)
+    x_part = Grads(normed_in, gxs, parts, cbuf, csem)
+    out_part = Back([(ng, wo_in, wbuf, wsem)], pparts, back, bsem)
+    in_part = Back(
+        [(gz, wz_in, wbuf, wsem), (gxs, wx_in, xbuf, xsem), (gbc_own, ws_in, sbuf, ysem)],
+        tparts, back, bsem,
+    )
 
     @pl.when(now == 0)
     def _():
+        z_part.begin()
         for copy in fetch:
             copy.start()
+        out_part.begin()
         greet_all(chips, ranks)
         fetch[0].wait()
-        stream_grads(normed_in, gz, zparts, width, cbuf, stage, csem, ssem)
+        z_part.run()
         z_job.step(0)
         fetch[1].wait()
-        stream_back([(ng, wo_in, wbuf, wsem)], [], pparts, back, bsem)
-        first.step(0)
-        z_job.step(1)
-        stream_grads(cot_in, ng, oparts, width, cbuf, stage, csem, ssem)
+        o_part.begin()
+        out_part.run(lambda: z_job.step(1))
+        first.step(0, 0)
+        first.step(0, 1)
+
+    early = [k for k in range(2, chips) if 2 * k - 2 < total - 1]
+
+    @pl.when(now == 1)
+    def _():
+        o_part.run()
         o_job.step(0)
 
-    early = [k for k in range(2, chips) if 3 * k - 4 < total - 1]
-
-    @pl.when(now == 2)
+    for k in early:
+        @pl.when(now == 2 * k - 2)
+        def _():
+            z_job.step(k)
+
+    @pl.when(now == 3)
     def _():
         o_job.step(1)
 
-    for k in early:
-        @pl.when(now == 3 * k - 4)
-        def _():
-            z_job.step(k)
+    @pl.when(now == 5)
+    def _():
+        first.step(1, 0)
+        first.step(1, 1)
+
+    @pl.when(now == total - 1)
+    def _():
+        x_part.begin()
+        in_part.begin()
 
     row = pl.multiple_of(
         (pl.program_id(0) * blocks + blocks - 1 - pl.program_id(1)) * BLOCK, BLOCK
@@ -1198,11 +1430,9 @@
     @pl.when(now == total - 1)
     def _():
         around.step(0)
-        fetch[2].wait()
-        fetch[3].wait()
-        stream_grads(normed_in, gxs, xparts, width + LANES, cbuf, stage, csem, ssem)
-        x_job.step(0)
-        pack[...] = jnp.zeros_like(pack)
+        begin(own_cot)
+        pack = land_core.at[core]
+        pack[...] = jnp.zeros(land_core.shape[1:], f32)
         for k in range(5):
             rows = slice(8 * k, 8 * k + 8)
             pack[k : k + 1, :width] = jnp.sum(gtapx[rows], axis=0, keepdims=True)
@@ -1212,135 +1442,144 @@
             pack[6:7, k * LANES : (k + 1) * LANES] = jnp.sum(
                 gpar[8 * k : 8 * k + 8], axis=0, keepdims=True
             )
-        p_line.step(0)
+        begin(by_core)
+        x_part.run()
+        x_job.step(0)
+        end(by_core)
+        land_chip[chip] = added(land_core, 2)
+        begin(by_chip)
+        depth = sparts.shape[0]
+
+        def own_columns(i):
+            columns = pl.ds(pl.multiple_of(rank * depth + i * CHUNK, CHUNK), CHUNK)
+            return pltpu.make_async_copy(normed_in.at[:, columns], cbuf.at[i], csem.at[i])
+
+        for i in range(depth // CHUNK):
+            own_columns(i).start()
         for k in range(2, chips):
             if k not in early:
                 z_job.step(k)
-        around.step(1)
         if chips > 2:
             o_job.step(2)
-        terms = [(gz, wz_in, wbuf, wsem), (gxs, wx_in, xbuf, xsem)]
-        stream_back(terms, [(gbc_own, ws)], tparts, back, bsem, 0, 0.5)
-        x_job.step(1)
-        for k in range(3, chips):
-            o_job.step(k)
-        stream_back(terms, [(gbc_own, ws)], tparts, back, bsem, 0.5, 1)
-        second.step(0)
-        for k in range(1, chips):
-            p_line.step(k)
-        around.finish()
-        for r in range(ranks):
-            once(slab(gbc_slots, r, tokens), cbuf.at[r % 2], csem.at[r % 2])
+        around.step(1)
+
+        def between():
+            second.step(0, 0)
+            around.finish()
 
             def add(at):
-                v = cbuf[r % 2, at].astype(f32)
-                gbc_sum[at] = v if r == 0 else gbc_sum[at] + v
-
-            row_loop(tokens, 64, add)
-
-        def rounded(at):
-            gbc_own[at] = gbc_sum[at].astype(bf16)
-
-        row_loop(tokens, 64, rounded)
-        depth = sparts.shape[0]
-        for i in range(depth // CHUNK):
-            columns = pl.ds(pl.multiple_of(rank * depth + i * CHUNK, CHUNK), CHUNK)
-            once(normed_in.at[:, columns], cbuf.at[0], csem.at[0])
-            state_stage[0] = mm_tn(cbuf[0], gbc_own[...])
-            once(state_stage.at[0], sparts.at[pl.ds(i * CHUNK, CHUNK)], csem.at[1])
-        s_job.step(0)
-        z_job.finish(line_out.at[:, pl.ds(0, width)])
-        once(line_out.at[:, pl.ds(0, width)], z_sum, osem.at[0])
-        s_job.step(1)
-        p_line.finish()
-        total_pack = packs[0:8]
-        for k in range(1, devices):
-            total_pack = total_pack + packs[8 * k : 8 * k + 8]
-        land_rank[rank] = total_pack
-        packed = everyone(land_rank, rank, ranks, qsend, qrecv, over_rank)
-        for copy in packed:
-            copy.start()
+                total = gbc_slots[at].astype(f32)
+                for r in range(1, ranks):
+                    there = pl.ds(pl.multiple_of(at.start + r * tokens, 128), at.size)
+                    total = total + gbc_slots[there].astype(f32)
+                gbc_slots[at] = total.astype(bf16)
+
+            row_loop(tokens, 128, add)
+            for i in range(depth // CHUNK):
+                own_columns(i).wait()
+                sparts[i * CHUNK : (i + 1) * CHUNK] = mm_tn(cbuf[i], gbc_slots[:tokens]).astype(
+                    sparts.dtype
+                )
+            s_job.step(0)
+            for k in range(3, chips):
+                o_job.step(k)
+            s_job.step(1)
+            x_job.step(1, True)
+
+        in_part.run(between)
+        second.step(0, 1)
+        begin(own_res)
+        s_job.finish(state_own)
+        s_line.step(0)
+        x_job.send_rest()
+        z_job.finish(half_out)
+        keep_z.start()
         first.arrive()
-        for r in range(ranks):
-            if r == 0:
-                once(slab(pparts, rank, first.rows), other, osem.at[1])
-            else:
-                once(pland.at[r], other, osem.at[1])
-
-            def add(at):
-                wide_out[at] = (res[at] if r == 0 else wide_out[at]).astype(f32) + other[at].astype(f32)
-
-            row_loop(first.rows, 16, add)
-        keep = pltpu.make_async_copy(wide_out, block_out, osem.at[2])
-        keep.start()
-        o_job.finish(line_out.at[:, pl.ds(0, width)])
-        once(line_out.at[:, pl.ds(0, width)], o_sum, osem.at[0])
-        for k in range(2, chips):
-            s_job.step(k)
-            x_job.step(k)
-        for copy in packed:
-            copy.wait()
+        end(own_res)
+
+        def plus(at, total):
+            wide_out[at] = pieced(gz, at) + total
+
+        first.totals(32, plus)
+        keep_block.start()
+        second.step(1, 0)
+        end(by_chip)
+        land_rank[rank] = added(land_chip, chips)
+        begin(by_rank)
+        keep_z.wait()
+        o_job.finish(half_out)
+        keep_o.start()
+        s_line.step(1)
+        s_line.finish()
+
+        def lower(at):
+            state_low[at] = state_line[at].astype(bf16)
+
+        row_loop(depth, 64, lower)
+        end(by_rank)
+        s_rank.step(0)
         shared = land_rank[0, :, width:]
         for r in range(1, ranks):
             shared = shared + land_rank[r, :, width:]
         for r in range(ranks):
             sums_ref[:, r * width : (r + 1) * width] = land_rank[r, :, :width]
         sums_ref[:, ranks * width :] = shared
-        s_job.finish(state_own)
-        for k in range(chips):
-            s_line.step(k)
-        keep.wait()
-        once(cot_own_in, other, osem.at[1])
-        once(slab(tparts, rank, second.rows), tland.at[0], osem.at[2])
+        if chips > 2:
+            x_job.step(2)
+        second.step(1, 1)
+        s_rank.step(1)
+        for k in range(3, chips):
+            x_job.step(k)
+        keep_block.wait()
+        end(own_cot)
         second.arrive()
         norm_acc[...] = jnp.zeros_like(norm_acc)
         gain = gain_ref[...]
 
-        def last(at):
-            grad = second.total(at)
-            v = res[at].astype(f32)
+        def last(at, grad):
+            v = pieced(gz, at)
             scaling = lax.rsqrt(jnp.mean(v * v, axis=1, keepdims=True) + epsilon)
             norm_acc[...] += fold(grad * v * scaling)
             grad = grad * gain
             along = jnp.sum(grad * v, axis=1, keepdims=True)
             weight = scaling * scaling * scaling * along / model
-            wide_out[at] = other[at].astype(f32) + scaling * grad - v * weight
-
-        row_loop(second.rows, 16, last)
-        keep_grad = pltpu.make_async_copy(wide_out, res_grad, osem.at[2])
+            wide_out[at] = pieced(ng, at) + scaling * grad - v * weight
+
+        second.totals(32, last)
         keep_grad.start()
         line = jnp.sum(norm_acc[...], axis=0, keepdims=True)
         eighth = model // 8
         for i in range(8):
             norm_rank[rank, i : i + 1, :] = line[:, i * eighth : (i + 1) * eighth]
-        across = everyone(norm_rank, rank, ranks, nsend, nrecv, over_rank)
-        for copy in across:
+        begin(norm_by_rank)
+        s_rank.finish()
+        buffers = (state_f, state_g)
+        stored = []
+        some = depth // 2
+        for r in range(2 * ranks):
+            if r >= 2:
+                stored[r - 2].wait()
+
+            def state(at):
+                low = pl.ds(pl.multiple_of(at.start + r * some, 64), at.size)
+                buffers[r % 2][at] = state_all[low].astype(f32)
+
+            row_loop(some, 64, state)
+            copy = pltpu.make_async_copy(
+                buffers[r % 2], state_out.at[pl.ds(r * some, some)], osem.at[1 + r % 2 * 2]
+            )
             copy.start()
-        s_line.finish()
-
-        def lower(at):
-            state_low[at] = state_line[at].astype(bf16)
-
-        row_loop(state_low.shape[0], 64, lower)
-        s_rank.step(0)
-        for copy in across:
-            copy.wait()
+            stored.append(copy)
+        end(norm_by_rank)
         norm_dp[me] = added(norm_rank, ranks)
-        along_dp = everyone(norm_dp, me, devices, msend, mrecv, over_dp)
-        for copy in along_dp:
-            copy.start()
-        s_rank.step(1)
+        begin(norm_by_dp)
+        keep_o.wait()
         x_job.finish(line_out)
-        once(line_out, x_sum, osem.at[0])
-        s_rank.finish()
-
-        def state(at):
-            state_ref[at] = state_all[at].astype(f32)
-
-        row_loop(state_ref.shape[0], 64, state)
-        for copy in along_dp:
-            copy.wait()
+        keep_x.start()
+        end(stored[-2:])
+        end(norm_by_dp)
         norm_ref[...] = added(norm_dp, devices)
+        keep_x.wait()
         keep_grad.wait()
 
 
@@ -1360,6 +1599,7 @@
     once = lambda shape: pl.BlockSpec(shape, whole)
     devices = 2 * chips
     own, depth, wide = model // devices, model // ranks, width + 2 * states
+    kind = bf16 if depth // devices % 16 == 0 else f32
     return pl.pallas_call(
         functools.partial(backward_kernel, blocks, nseq * blocks, chips, ranks),
         grid=(nseq, blocks),
@@ -1378,18 +1618,15 @@
         ]
         + [ANY] * 10,
         out_specs=[
-            once((8, width * ranks + 2 * states)), once((8, model // 8)), once((model, 2 * states)),
+            once((8, width * ranks + 2 * states)), once((8, model // 8)),
         ]
-        + [ANY] * 13,
+        + [ANY] * 10,
         out_shape=[
             shaped((8, width * ranks + 2 * states), f32), shaped((8, model // 8), f32),
-            shaped((model, 2 * states), f32),
             shaped((own, width), f32), shaped((own, width), f32), shaped((own, width + LANES), f32),
-            shaped((rows, model), f32), shaped((rows, model), f32),
-            shaped((model, width + LANES), bf16), shaped((tokens, model), bf16),
-            shaped((depth, 2 * states), f32),
-            shaped((model, width), bf16), shaped((model, width), bf16), shaped((tokens, model), bf16),
-            shaped((ranks * tokens, 2 * states), bf16), shaped((ranks, rows, model), bf16),
+            shaped((rows, model), f32), shaped((rows, model), f32), shaped((model, 2 * states), f32),
+            shaped((tokens, model), bf16), shaped((tokens, model), bf16),
+            *[shaped((ranks, rows, model) if ranks != 4 else (8, LANES), bf16)] * 2,
         ],
         scratch_shapes=[
             *scan_bwd_scratch(width, states),
@@ -1401,37 +1638,35 @@
             pltpu.VMEM((tokens, width), bf16),
             pltpu.VMEM((tokens, width), bf16),
             pltpu.VMEM((2, tokens, CHUNK), bf16),
-            pltpu.VMEM((2, CHUNK, width + LANES), bf16),
+            pltpu.VMEM((model, width + LANES), bf16),
             pltpu.VMEM((2, tokens, CHUNK), bf16),
             pltpu.VMEM((2, CHUNK, width), bf16),
             pltpu.VMEM((2, CHUNK, width + LANES), bf16),
-            pltpu.VMEM((tokens, 2 * states), f32),
-            pltpu.VMEM((model, 2 * states), bf16),
-            pltpu.VMEM((rows, model), bf16),
-            pltpu.VMEM((rows, model), bf16),
+            pltpu.VMEM((ranks * tokens, 2 * states), bf16),
+            pltpu.VMEM((2, CHUNK, 2 * states), bf16),
             pltpu.VMEM((rows, model), f32),
             pltpu.VMEM((own, width + LANES), f32),
-            pltpu.VMEM((ranks, rows, model), bf16),
-            pltpu.VMEM((2, CHUNK, 2 * states), f32),
-            pltpu.VMEM((depth // devices, 2 * states), f32),
-            pltpu.VMEM((depth, 2 * states), f32),
+            pltpu.VMEM((depth, 2 * states), kind),
+            pltpu.VMEM((depth // 2, 2 * states), f32),
+            pltpu.VMEM((depth // 2, 2 * states), f32),
+            pltpu.VMEM((depth // devices, 2 * states), kind),
+            pltpu.VMEM((depth, 2 * states), kind),
             pltpu.VMEM((depth, 2 * states), bf16),
-            pltpu.VMEM((model, 2 * states), bf16),
-            pltpu.VMEM((8, wide), f32),
-            pltpu.VMEM((8 * devices, wide), f32),
+            pltpu.VMEM((2, 8, wide), f32),
+            pltpu.VMEM((chips, 8, wide), f32),
             pltpu.VMEM((ranks, 8, wide), f32),
             pltpu.VMEM((ranks, 8, model // 8), f32),
             pltpu.VMEM((devices, 8, model // 8), f32),
             pltpu.VMEM((8, model), f32),
-            dma(4), *[dma(2)] * 5, dma(3),
-            *[dma(ranks)] * 4, *[dma(devices)] * 2,
+            dma(2), *[dma(2)] * 5, dma(4), pltpu.SemaphoreType.DMA((2, model // width)),
+            *[pltpu.SemaphoreType.DMA((2, n)) for n in (2, chips, ranks, ranks, devices)],
             *LineScatter.scratch(chips, (model, width)),
             *LineScatter.scratch(chips, (model, width)),
             *LineScatter.scratch(chips, (model, width + LANES)),
-            *LineScatter.scratch(chips, (depth, 2 * states), f32),
-            *TensorScatter.scratch(ranks), *TensorScatter.scratch(ranks),
-            *TensorGather.scratch(ranks), *LineGather.scratch(chips),
-            *TensorGather.scratch(ranks), *LineGather.scratch(chips),
+            *SmallScatter.scratch(chips, (depth, 2 * states), kind),
+            *TensorGather.scratch(ranks), *SmallGather.scratch(chips), *TensorGather.scratch(ranks),
+            HalvesScatter.temp((tokens, model)) if ranks == 4 else pltpu.VMEM((2, rows // 2, model), bf16),
+            *(HalvesScatter.scratch((tokens, model)) if ranks == 4 else DirectScatter.scratch(ranks)) * 2,
         ],
         compiler_params=params(number),
         name="backward",
@@ -1477,7 +1712,7 @@
         x, bc, st, seg, tapx, tapbc, par, spread, skip, nseq,
     )
     gz, gy, ng, ggain, wo = gate(3, chips, ranks, gain, out_weight.T, normed, wz, y, cot)
-    sums, norm_grad, state_grad, z_grad, out_grad, x_grad, block_out, residual_grad, *_ = backward(
+    sums, norm_grad, z_grad, out_grad, x_grad, block_out, residual_grad, state_grad, *_ = backward(
         4, chips, ranks, ggain, norm_gain[None], residual, cotangent, state_weight,
         gz, ng, normed, cot, wo, wz, wx,
         x, conv, bc, convbc, st, seg, gy, y, h, tapx, tapbc, par, spread, skip, nseq,

time: 400 us -> 360 us (0.900)
  Pallas kernels: 358 us -> 320 us
    pallas_call x1, Pallas kernels: 194 us -> 155 us  [backward(): pl.pallas_call(functools.partial(backward_kernel, blocks, nseq * blocks,...]
where the time goes in v5:
time: 360 us; the launch traced here: 359 us
  Pallas kernels  320 us (89%)
  local copies, waits for them, and re-layouts  34.9 us (10%)
    pallas_call x1, Pallas kernels, backward(): pl.pallas_call(functools.partial(backward_kernel, blocks, nseq * blocks,...  155 us
    pallas_call x1, Pallas kernels, gate(): pl.pallas_call(functools.partial(gate_kernel, chips, ranks), in_specs=[ON...  61.6 us
    pallas_call x1, Pallas kernels, project(): pl.pallas_call(functools.partial(project_kernel, chips, ranks), in_specs=...  57.7 us
    pallas_call x1, Pallas kernels, scan_forward_gather(): pl.pallas_call(functools.partial(scan_gather_kernel, blocks, nseq * block...  45.3 us
    unnamed x21, local copies, waits for them, and re-layouts  15.9 us

profile of v5, /device:TPU:0, one launch (start us, length us, event | category | flops | bytes accessed | tf_op | source)
XLA Modules:
  0.0 358.9 jit_solution(16595213748667334575)
XLA Ops:
  6.7 1.0 maximum_maximum_fusion
  8.9 0.8 fusion.refs_7_.refs_13_
  9.8 1.7 broadcast_in_dim.44.refs_3_.refs_5_.refs_6_
  11.4 2.0 copy.30
  13.5 1.5 fusion.4
  15.0 1.2 copy_bitcast_fusion
  16.1 1.0 concatenate.15.wx_own
  17.1 57.7 %project.1 = (f32[1024,1024]{1,0:T(8,128)}, f32[1024,128]{1,0:T(8,128)}, f32[1024,256]{1,0:T(8,128)}, bf16[1024,2048]{1,0:T(8,128)(2,1)}, bf16[2048,1152]{1,0:T(8,128)(2,1)}) custom-call(bf16[256,2048]{1,0:T(8,128)(2,1)} %refs_17_.1, f32[1,2048]{1,0:T(1,128)} %bitcast.21, bf16[2048,256]{1,0:T(8,128)(2,1)} %refs_19_.1, bf16[256,1152]{1,0:T(8,128)(2,1)} %concatenate.15.wx_own), custom_call_target="tpu_custom_call" | custom-call | tf_op jit(solution)/shard_map/project/pallas_call | solution.py:958
  74.8 45.3 %scan_forward.1 = (f32[1024,1024]{1,0:T(8,128)}, bf16[1024,1024]{1,0:T(8,128)(2,1)}, f32[1024,1024]{1,0:T(8,128)}, f32[1024,256]{1,0:T(8,128)}, bf16[2048,1024]{1,0:T(8,128)(2,1)}, /*index=5*/bf16[1024,2048]{1,0:T(8,128)(2,1)}) custom-call(f32[1024,1024]{1,0:T(8,128)} %get-tuple-element.37.refs_0_, f32[1024,256]{1,0:T(8,128)} %get-tuple-element.38.refs_1_.refs_2_, ...), custom_call_target="tpu_custom_call" | custom-call | tf_op jit(solution)/shard_map/scan_forward/pallas_call | solution.py:1015
  120.1 61.6 %gate.1 = (bf16[1024,1024]{1,0:T(8,128)(2,1)}, f32[1024,1024]{1,0:T(8,128)}, bf16[1024,1024]{1,0:T(8,128)(2,1)}, f32[8,1024]{1,0:T(8,128)}, bf16[2048,1024]{1,0:T(8,128)(2,1)}) custom-call(f32[8,1024]{1,0:T(8,128)} %broadcast_in_dim.53.gain_ref, bf16[256,1024]{1,0:T(8,128)(2,1)} %bitcast.18, bf16[1024,2048]{1,0:T(8,128)(2,1)} %get-tuple-element.42.normed_in.refs_22_, ...), custom_call_target="tpu_custom_call" | custom-call | tf_op jit(solution)/shard_map/gate/pallas_call | solution.py:1167
  181.7 155.2 %backward.1 = (f32[8,4352]{1,0:T(8,128)}, f32[8,256]{1,0:T(8,128)}, f32[256,1024]{1,0:T(8,128)}, f32[256,1024]{1,0:T(8,128)}, f32[256,1152]{1,0:T(8,128)}, /*ind...) custom-call(f32[1024,1024]{1,0:T(8,128)} %get-tuple-element.37.refs_, ...), custom_call_target="tpu_custom_call" | custom-call | tf_op jit(solution)/shard_map/backward/pallas_call | solution.py:1603
  337.0 1.4 copy.36
  338.3 1.6 slice_reduce_fusion
  339.9 1.6 fusion.5
  341.5 1.5 slice.41
  344.9 0.9 slice.40
  345.8 1.3 slice_bitcast_fusion
  348.0 2.9 copy.31
  351.0 1.3 copy.33
  352.9 1.3 copy.42
  354.2 1.0 copy-done.2
  355.3 1.3 copy.43
  356.6 1.0 copy-done.1
  357.6 1.3 copy.44
  (40 shorter events, 10.6 us)
Async XLA Ops:
  0.6 12.8 %copy-start = (bf16[256,2,1024]{2,1,0:T(2,128)(2,1)S(1)}, bf16[256,2,1024]{2,1,0:T(2,128)(2,1)}, u32[]{:S(2)}) copy-start(bf16[256,2,1024]{2,1,0:T(2,128)(2,1)} %param.17) | copy-start | bytes 3145732
  336.9 10.8 %copy-start.5 = (f32[256,1024]{1,0:T(8,128)S(1)}, f32[256,1024]{1,0:T(8,128)}, u32[]{:S(2)}) copy-start(f32[256,1024]{1,0:T(8,128)} %get-tuple-element.56) | copy-start | bytes 3145732
  348.0 3.0 copy-start.4
  351.0 2.0 copy-start.3
  352.9 2.3 copy-start.2
  355.3 2.3 copy-start.1

commit v6 on v5

--- a/solution.py
+++ b/solution.py
@@ -310,12 +310,6 @@
     ]
 
 
-def spread_matrix(heads):
-    row = lax.broadcasted_iota(jnp.int32, (LANES, heads * WIDTH), 0)
-    col = lax.broadcasted_iota(jnp.int32, (LANES, heads * WIDTH), 1)
-    return (row % (LANES // 2) == col // WIDTH).astype(bf16)
-
-
 def on_lanes(v):
     half = jnp.pad(v, [(0, 0)] * (v.ndim - 1) + [(0, LANES // 2 - v.shape[-1])])
     return jnp.concatenate([half, half], axis=-1)
@@ -443,6 +437,15 @@
                 if use is not None:
                     use(self.chip + shift)
 
+    def each(self, k, use):
+        if k == 0:
+            use(self.chip)
+            return
+        for way, there, shift in self.sides(k):
+            @pl.when(there)
+            def _():
+                use(self.chip + shift)
+
     def sent(self):
         for way in (0, 1, 2):
             self.pass_on(way, self.me, self.own, wait=True)
@@ -466,7 +469,7 @@
         self.ranks, self.rows = ranks, own.shape[0]
         chip, core, self.rank = place()
         self.me = chip * 2 + core
-        self.steps = 2
+        self.kept = False
 
     @staticmethod
     def scratch(ranks):
@@ -509,8 +512,15 @@
                 self.near(j).wait_recv()
                 self.near(2 + j).start()
 
+    def near_rows(self):
+        self.keep().wait()
+        self.kept = True
+        x, y = self.rank % 2, self.rank // 2
+        return [self.rank, y * 2 + 1 - x, (1 - y) * 2 + x], [(1 - y) * 2 + 1 - x]
+
     def finish(self):
-        self.keep().wait()
+        if not self.kept:
+            self.keep().wait()
         if self.ranks == 4:
             for j in (0, 1):
                 self.near(j).wait_send()
@@ -893,9 +903,56 @@
     return pltpu.SemaphoreType.DMA if count is None else pltpu.SemaphoreType.DMA((count,))
 
 
+def exact_mm(v, picks):
+    high = v.astype(bf16)
+    rest = v - high.astype(f32)
+    middle = rest.astype(bf16)
+    low = (rest - middle.astype(f32)).astype(bf16)
+    return mm(high, picks) + mm(middle, picks) + mm(low, picks)
+
+
+def prepare(
+    rank, heads, seg_in, taps_in, bias_in, heads_in, gain_in,
+    seg_out, tapx_out, tapbc_out, par_out, skip_out, gain_out, spread_out,
+):
+    width, inner = tapx_out.shape[1], gain_in.shape[1]
+    length = seg_in.shape[1]
+    for s in range(seg_in.shape[0]):
+        for r in range(0, length, LANES):
+            row = jnp.broadcast_to(seg_in[s : s + 1, r : r + LANES], (LANES, LANES))
+            at = s * length + r
+            seg_out[at : at + LANES] = jnp.transpose(row.astype(f32)).astype(jnp.int32)
+    own = pl.ds(pl.multiple_of(rank * width, LANES), width)
+    tapx_out[...] = jnp.zeros_like(tapx_out)
+    tapbc_out[...] = jnp.zeros_like(tapbc_out)
+    tapx_out[0:4], tapx_out[4:5] = taps_in[:, own], bias_in[:, own]
+    tapbc_out[0:4], tapbc_out[4:5] = taps_in[:, inner:], bias_in[:, inner:]
+    gain_out[...] = jnp.broadcast_to(gain_in[:, own], gain_out.shape)
+    row = lax.broadcasted_iota(jnp.int32, spread_out.shape, 0)
+    col = lax.broadcasted_iota(jnp.int32, spread_out.shape, 1)
+    half = LANES // 2
+    folded = jnp.where(row >= half, row - half, row)
+    start = folded * WIDTH
+    spread_out[...] = ((col >= start) & (col < start + WIDTH)).astype(bf16)
+    row = lax.broadcasted_iota(jnp.int32, (LANES, LANES), 0)
+    col = lax.broadcasted_iota(jnp.int32, (LANES, LANES), 1)
+    lane = jnp.where(col >= half, col - half, col)
+    picked = exact_mm(
+        heads_in[...], ((row == rank * heads + lane) & (lane < heads)).astype(bf16)
+    )
+    lane = lax.broadcasted_iota(jnp.int32, (1, LANES), 1)
+    there = jnp.where(lane >= half, lane - half, lane) < heads
+    par_out[...] = jnp.zeros_like(par_out)
+    par_out[0:1] = picked[0:1]
+    par_out[1:2] = jnp.where(there, -jnp.exp(picked[1:2]), 0.0)
+    skip = jnp.where(lane < half, picked[2:3], 0.0)
+    skip_out[...] = exact_mm(jnp.broadcast_to(skip, (8, LANES)), spread_out[...])
+
+
 def project_kernel(
-    chips, ranks, res_ref, gain_ref, ws_ref, wx_own, x_ref, st_ref, bc_ref, normed_out, wx_out,
-    own, normed, wx, *sems
+    chips, ranks, heads, res_ref, gain_ref, ws_ref, seg_in, taps_in, bias_in, heads_in, gated_in, wx_own,
+    x_ref, st_ref, bc_ref, seg_out, tapx_out, tapbc_out, par_out, skip_out, gain_out, spread_out,
+    normed_out, wx_out, own, normed, wx, *sems
 ):
     greet(chips, ranks)
     line = LineGather(wx_own, wx, *sems[:3], chips)
@@ -910,25 +967,26 @@
 
     row_loop(own.shape[0], 32, norm)
     tensor.step(0)
+    prepare(
+        line.rank, heads, seg_in, taps_in, bias_in, heads_in, gated_in,
+        seg_out, tapx_out, tapbc_out, par_out, skip_out, gain_out, spread_out,
+    )
     line.step(1)
     tensor.step(1)
     if chips > 2:
         line.step(2)
-    tensor.finish()
-    keep_normed = pltpu.make_async_copy(normed, normed_out, sems[6])
-    keep_normed.start()
     tokens, width = x_ref.shape
-    deep = 2 * line.rows
-
-    def states(at):
-        bc_ref[at] = mm(normed[at], ws_ref[...])
-
-    row_loop(tokens, CHUNK, states)
-
-    def use(first, chip):
+    deep, some = 2 * line.rows, own.shape[0]
+
+    def states(blocks):
+        for r in blocks:
+            at = pl.ds(pl.multiple_of(r * some, some), some)
+            bc_ref[at] = mm(normed[at], ws_ref[...])
+
+    def use(first, blocks, chip):
         ks = pl.ds(pl.multiple_of(chip * deep, deep), deep)
-
-        def rows(at):
+        for r in blocks:
+            at = pl.ds(pl.multiple_of(r * some, some), some)
             left = normed[at, ks]
             x, st = mm(left, wx[ks, :width]), mm(left, wx[ks, width:])
             if first:
@@ -937,14 +995,21 @@
                 x_ref[at] += x
                 st_ref[at] += st
 
-        row_loop(tokens, CHUNK, rows)
-
-    line.arrive(0, functools.partial(use, True))
-    line.arrive(1, functools.partial(use, False))
+    every = list(range(ranks))
+    early, late = tensor.near_rows() if ranks == 4 else ([], every)
+    for k in (0, 1):
+        line.arrive(k, functools.partial(use, k == 0, early))
+    states(early)
+    tensor.finish()
+    keep_normed = pltpu.make_async_copy(normed, normed_out, sems[6])
+    keep_normed.start()
+    for k in (0, 1):
+        line.each(k, functools.partial(use, k == 0, late))
+    states(late)
     for k in range(2, chips):
         if k + 1 < chips:
             line.step(k + 1)
-        line.arrive(k, functools.partial(use, False))
+        line.arrive(k, functools.partial(use, False, every))
     keep_wx = pltpu.make_async_copy(wx, wx_out, sems[7])
     keep_wx.start()
     line.sent()
@@ -952,17 +1017,23 @@
     keep_wx.wait()
 
 
-def project(number, chips, ranks, residual, norm_gain, ws, wx_own):
+def project(
+    number, chips, ranks, heads, residual, norm_gain, ws, segments, taps, bias, by_head, gated_gain, wx_own
+):
     rows, model = residual.shape
     tokens, width = rows * ranks, wx_own.shape[1]
+    inner = width - LANES
     return pl.pallas_call(
-        functools.partial(project_kernel, chips, ranks),
-        in_specs=[ONCHIP, ONCHIP, ONCHIP, ANY],
-        out_specs=[ONCHIP, ONCHIP, ONCHIP, ANY, ANY],
+        functools.partial(project_kernel, chips, ranks, heads),
+        in_specs=[ONCHIP] * 8 + [ANY],
+        out_specs=[ONCHIP] * 10 + [ANY, ANY],
         out_shape=[
-            shaped((tokens, width - LANES), f32), shaped((tokens, LANES), f32),
-            shaped((tokens, ws.shape[1]), f32), shaped((tokens, model), bf16),
-            shaped((model, width), bf16),
+            shaped((tokens, inner), f32), shaped((tokens, LANES), f32),
+            shaped((tokens, ws.shape[1]), f32),
+            shaped((tokens, LANES), jnp.int32), shaped((8, inner), f32), shaped((8, ws.shape[1]), f32),
+            shaped((8, LANES), f32), shaped((8, inner), f32), shaped((8, inner), f32),
+            shaped((LANES, inner), bf16),
+            shaped((tokens, model), bf16), shaped((model, width), bf16),
         ],
         scratch_shapes=[
             pltpu.VMEM((rows, model), bf16), pltpu.VMEM((tokens, model), bf16),
@@ -971,7 +1042,7 @@
         ],
         compiler_params=params(number),
         name="project",
-    )(residual, norm_gain, ws, wx_own)
+    )(residual, norm_gain, ws, segments, taps, bias, by_head, gated_gain, wx_own)
 
 
 def scan_gather_kernel(blocks, total, chips, ranks, *refs):
@@ -1090,6 +1161,13 @@
 
     row_loop(tokens, CHUNK, gate)
     load[2].wait()
+
+    def square(at):
+        zz = z[at]
+        gated = y[at] * (zz * sigmoid(zz))
+        squares[at] = lane_sums(gated * gated)
+
+    row_loop(tokens, 32, square)
     load[3].wait()
     deep = 2 * line.rows
 
@@ -1115,11 +1193,9 @@
 
     def sums(at):
         zz = z[at]
-        gated = y[at] * (zz * sigmoid(zz))
-        squares[at] = lane_sums(gated * gated)
-        dots[at] = lane_sums(gng[at] * gain * gated)
-
-    row_loop(tokens, 16, sums)
+        dots[at] = lane_sums(gng[at] * gain * (y[at] * (zz * sigmoid(zz))))
+
+    row_loop(tokens, 32, sums)
     half = lax.broadcasted_iota(jnp.int32, (8, LANES), 0) < 4
     one, other = half.astype(bf16), jnp.logical_not(half).astype(bf16)
     for r in range(0, tokens, CHUNK):
@@ -1157,7 +1233,7 @@
         gz_ref[at] = (grad * yy * (sig * (1.0 + zz * (1.0 - sig)))).astype(bf16)
         gy_ref[at] = grad * silu
 
-    row_loop(tokens, 16, grads)
+    row_loop(tokens, 32, grads)
     keep.wait()
 
 
@@ -1680,32 +1756,17 @@
     residual, segment_ids, norm_gain, inner_weight, state_weight, step_weight, conv_weight,
     conv_bias, step_bias, decay_log, skip_gain, gated_gain, out_weight, cotangent,
 ):
-    rank = lax.axis_index("tensor")
     chips, ranks = lax.axis_size("dp") // 2, lax.axis_size("tensor")
     width = inner_weight.shape[2]
     heads = step_weight.shape[1]
     inner_width = gated_gain.shape[0]
-    nseq, length = segment_ids.shape
-    tokens = nseq * length
-    inner_start, head_start = rank * width, rank * heads
-    taps = jnp.concatenate([conv_weight, conv_bias[None], jnp.zeros((3, conv_bias.shape[0]), f32)], axis=0)
-    tapx = lax.dynamic_slice_in_dim(taps, inner_start, width, 1)
-    tapbc = taps[:, inner_width:]
-    local = lambda v: lax.dynamic_slice_in_dim(v, head_start, heads, 0)
-    rates = -jnp.exp(local(decay_log))
-    par = jnp.concatenate(
-        [on_lanes(local(step_bias)[None]), on_lanes(rates[None]), jnp.zeros((6, LANES), f32)], axis=0
-    )
-    skip = jnp.broadcast_to(jnp.repeat(local(skip_gain), WIDTH)[None], (8, width))
-    gain = jnp.broadcast_to(
-        lax.dynamic_slice_in_dim(gated_gain, inner_start, width, 0)[None], (8, width)
-    )
-    spread = spread_matrix(heads)
-    seg = jnp.broadcast_to(segment_ids.reshape(tokens, 1), (tokens, LANES))
-
+    nseq = segment_ids.shape[0]
     wx_own = jnp.concatenate([inner_weight[:, 1], on_lanes(step_weight)], axis=1)
-    x, st, bc, normed, wx = project(
-        1, chips, ranks, residual, norm_gain[None], state_weight, wx_own
+    by_head = jnp.stack([step_bias, decay_log, skip_gain])
+    by_head = jnp.pad(by_head, ((0, 5), (0, LANES - by_head.shape[1])))
+    x, st, bc, seg, tapx, tapbc, par, skip, gain, spread, normed, wx = project(
+        1, chips, ranks, heads, residual, norm_gain[None], state_weight, segment_ids,
+        conv_weight, conv_bias[None], by_head, gated_gain[None], wx_own,
     )
     y, h, conv, convbc, wz, cot = scan_forward_gather(
         2, chips, ranks, inner_weight[:, 0], cotangent,

time: 360 us -> 345 us (0.958)
  Pallas kernels: 320 us -> 311 us
  local copies, waits for them, and re-layouts: 34.9 us -> 29.5 us
where the time goes in v6:
time: 345 us; the launch traced here: 343 us
  Pallas kernels  311 us (90%)
  local copies, waits for them, and re-layouts  29.5 us (9%)
    pallas_call x1, Pallas kernels, backward(): pl.pallas_call(functools.partial(backward_kernel, blocks, nseq * blocks,...  152 us
    pallas_call x1, Pallas kernels, gate(): pl.pallas_call(functools.partial(gate_kernel, chips, ranks), in_specs=[ON...  58 us
    pallas_call x1, Pallas kernels, project(): pl.pallas_call(functools.partial(project_kernel, chips, ranks, heads), in...  56.4 us
    pallas_call x1, Pallas kernels, scan_forward_gather(): pl.pallas_call(functools.partial(scan_gather_kernel, blocks, nseq * block...  44.6 us
    unnamed x21, local copies, waits for them, and re-layouts  15.9 us

profile of v6, /device:TPU:0, one launch (start us, length us, event | category | flops | bytes accessed | tf_op | source)
XLA Modules:
  0.0 343.2 jit_solution(8748796122647577749)
XLA Ops:
  0.7 1.4 select_maximum_fusion.heads_in
  2.0 1.3 broadcast_in_dim.11.bias_in
  3.4 0.8 copy.28
  4.2 2.0 copy.30
  6.3 1.5 fusion
  7.8 1.2 copy_bitcast_fusion
  8.9 1.0 concatenate.3.wx_own
  9.9 56.4 %project.1 = (f32[1024,1024]{1,0:T(8,128)}, f32[1024,128]{1,0:T(8,128)}, f32[1024,256]{1,0:T(8,128)}, s32[1024,128]{1,0:T(8,128)}, f32[8,1024]{1,0:T(8,128)}, /*...) custom-call(bf16[256,2048]{1,0:T(8,128)(2,1)} %refs_17_.1, ...), custom_call_target="tpu_custom_call" | custom-call | tf_op jit(solution)/shard_map/project/pallas_call | solution.py:1026
  66.3 44.6 %scan_forward.1 = (f32[1024,1024]{1,0:T(8,128)}, bf16[1024,1024]{1,0:T(8,128)(2,1)}, f32[1024,1024]{1,0:T(8,128)}, f32[1024,256]{1,0:T(8,128)}, bf16[2048,1024]{1,0:T(8,128)(2,1)}, /*index=5*/bf16[1024,2048]{1,0:T(8,128)(2,1)}) custom-call(f32[1024,1024]{1,0:T(8,128)} %get-tuple-element.44.refs_0_, f32[1024,256]{1,0:T(8,128)} %get-tuple-element.45.refs_1_.refs_2_, ...), custom_call_target="tpu_custom_call" | custom-call | tf_op jit(solution)/shard_map/scan_forward/pallas_call | solution.py:1086
  110.9 58.0 %gate.1 = (bf16[1024,1024]{1,0:T(8,128)(2,1)}, f32[1024,1024]{1,0:T(8,128)}, bf16[1024,1024]{1,0:T(8,128)(2,1)}, f32[8,1024]{1,0:T(8,128)}, bf16[2048,1024]{1,0:T(8,128)(2,1)}) custom-call(f32[8,1024]{1,0:T(8,128)} %get-tuple-element.55.gain_ref, bf16[256,1024]{1,0:T(8,128)(2,1)} %bitcast.17, bf16[1024,2048]{1,0:T(8,128)(2,1)} %get-tuple-element.56.normed_in.refs_22_, ...), custom_call_target="tpu_custom_call" | custom-call | tf_op jit(solution)/shard_map/gate/pallas_call | solution.py:1243
  168.9 152.3 %backward.1 = (f32[8,4352]{1,0:T(8,128)}, f32[8,256]{1,0:T(8,128)}, f32[256,1024]{1,0:T(8,128)}, f32[256,1024]{1,0:T(8,128)}, f32[256,1152]{1,0:T(8,128)}, /*ind...) custom-call(f32[1024,1024]{1,0:T(8,128)} %get-tuple-element.44.refs_, ...), custom_call_target="tpu_custom_call" | custom-call | tf_op jit(solution)/shard_map/backward/pallas_call | solution.py:1679
  321.2 1.4 copy.36
  322.6 1.6 slice_reduce_fusion
  324.2 1.6 fusion.1
  325.8 1.5 slice.37
  329.2 0.9 slice.36
  330.1 1.3 slice_bitcast_fusion
  332.3 2.9 copy.31
  335.2 1.3 copy.33
  337.2 1.3 copy.42
  338.5 1.0 copy-done.2
  339.6 1.3 copy.43
  340.9 1.0 copy-done.1
  341.9 1.3 copy.44
  (18 shorter events, 3.4 us)
Async XLA Ops:
  0.6 5.6 %copy-start = (bf16[256,2,1024]{2,1,0:T(2,128)(2,1)S(1)}, bf16[256,2,1024]{2,1,0:T(2,128)(2,1)}, u32[]{:S(2)}) copy-start(bf16[256,2,1024]{2,1,0:T(2,128)(2,1)} %param.17) | copy-start | bytes 3145732
  321.2 10.8 %copy-start.5 = (f32[256,1024]{1,0:T(8,128)S(1)}, f32[256,1024]{1,0:T(8,128)}, u32[]{:S(2)}) copy-start(f32[256,1024]{1,0:T(8,128)} %get-tuple-element.70) | copy-start | bytes 3145732
  332.3 3.0 copy-start.4
  335.2 2.0 copy-start.3
  337.2 2.3 copy-start.2
  339.6 2.3 copy-start.1

commit v7 on v6

--- a/solution.py
+++ b/solution.py
@@ -1752,6 +1752,74 @@
     )
 
 
+def emit_kernel(
+    ranks, heads, sums_ref, norm_ref, z_ref, x_ref, o_ref, block_in, res_in, state_in,
+    inner_ref, step_ref, out_ref, taps_ref, bias_ref, gated_ref, norm_out, a_ref, b_ref, c_ref,
+    block_out, res_out, state_out, block, res, state, sems
+):
+    moves = [
+        (
+            pltpu.make_async_copy(src, held, sems.at[0, i]),
+            pltpu.make_async_copy(held, dst, sems.at[1, i]),
+        )
+        for i, (src, held, dst) in enumerate(
+            ((block_in, block, block_out), (res_in, res, res_out), (state_in, state, state_out))
+        )
+    ]
+    for come, _ in moves:
+        come.start()
+    width, inner = z_ref.shape[1], gated_ref.shape[0]
+    row = lax.broadcasted_iota(jnp.int32, (LANES, LANES), 0)
+    col = lax.broadcasted_iota(jnp.int32, (LANES, LANES), 1)
+    total = jnp.zeros((8, LANES), f32)
+    for r in range(ranks):
+        line = [sums_ref[6:7, r * width + k * LANES : r * width + (k + 1) * LANES] for k in range(3)]
+        picks = ((col == r * heads + row) & (row < heads)).astype(bf16)
+        total = total + exact_mm(
+            jnp.concatenate(line + [jnp.zeros((5, LANES), f32)], axis=0), picks
+        )
+    for k, ref in enumerate((a_ref, b_ref, c_ref)):
+        ref[...] = total[k, : ranks * heads]
+    taps_ref[...] = sums_ref[0:4]
+    bias_ref[...] = sums_ref[4]
+    gated_ref[...] = sums_ref[5, :inner]
+    eighth = norm_ref.shape[1]
+    for i in range(8):
+        norm_out[i * eighth : (i + 1) * eighth] = norm_ref[i]
+    step_ref[...] = x_ref[:, width : width + heads]
+    for come, go in moves:
+        come.wait()
+        go.start()
+    inner_ref[:, 0, :] = z_ref[...]
+    inner_ref[:, 1, :] = x_ref[:, :width]
+    out_ref[...] = jnp.transpose(o_ref[...])
+    for _, go in moves:
+        go.wait()
+
+
+def emit(ranks, heads, sums, norm, z, x, o, block, res, state):
+    own, width = z.shape
+    inner = width * ranks
+    vector = lambda n: shaped((n,), f32)
+    return pl.pallas_call(
+        functools.partial(emit_kernel, ranks, heads),
+        in_specs=[ONCHIP] * 5 + [ANY] * 3,
+        out_specs=[ONCHIP] * 10 + [ANY] * 3,
+        out_shape=[
+            shaped((own, 2, width), f32), shaped((own, heads), f32), shaped((width, own), f32),
+            shaped((4, sums.shape[1]), f32), vector(sums.shape[1]), vector(inner),
+            vector(norm.size), *[vector(ranks * heads)] * 3,
+            shaped(block.shape, f32), shaped(res.shape, f32), shaped(state.shape, f32),
+        ],
+        scratch_shapes=[
+            pltpu.VMEM(block.shape, f32), pltpu.VMEM(res.shape, f32), pltpu.VMEM(state.shape, f32),
+            pltpu.SemaphoreType.DMA((2, 3)),
+        ],
+        compiler_params=pltpu.CompilerParams(vmem_limit_bytes=VMEM_BYTES),
+        name="emit",
+    )(sums, norm, z, x, o, block, res, state)
+
+
 def per_device(
     residual, segment_ids, norm_gain, inner_weight, state_weight, step_weight, conv_weight,
     conv_bias, step_bias, decay_log, skip_gain, gated_gain, out_weight, cotangent,
@@ -1778,13 +1846,15 @@
         gz, ng, normed, cot, wo, wz, wx,
         x, conv, bc, convbc, st, seg, gy, y, h, tapx, tapbc, par, spread, skip, nseq,
     )
-    inner_grad = jnp.stack([z_grad, x_grad[:, :width]], axis=1)
-    by_head = sums[6, :inner_width].reshape(ranks, width)
-    by_head = [by_head[:, k * LANES : k * LANES + heads].reshape(-1) for k in range(3)]
+    (
+        inner_grad, step_grad, out_grad, tap_grad, bias_grad, gated_grad, norm_grad,
+        step_bias_grad, decay_grad, skip_grad, block_out, residual_grad, state_grad,
+    ) = emit(
+        ranks, heads, sums, norm_grad, z_grad, x_grad, out_grad, block_out, residual_grad, state_grad
+    )
     return (
-        block_out, residual_grad, norm_grad.reshape(-1), inner_grad, state_grad,
-        x_grad[:, width : width + heads], sums[:4], sums[4], *by_head,
-        sums[5, :inner_width], out_grad.T,
+        block_out, residual_grad, norm_grad, inner_grad, state_grad, step_grad, tap_grad, bias_grad,
+        step_bias_grad, decay_grad, skip_grad, gated_grad, out_grad,
     )
 
 

time: 345 us -> 334 us (0.968)
  local copies, waits for them, and re-layouts: 29.5 us -> 11.3 us
  Pallas kernels: 311 us -> 320 us
    unnamed x21 -> x3, local copies, waits for them, and re-layouts: 15.9 us -> 4.44 us
    pallas_call x0 -> x1, Pallas kernels: none -> 8.59 us  [emit(): pl.pallas_call(functools.partial(emit_kernel, ranks, heads), in_specs=[ON...]
    slice x5 -> x0, local copies, waits for them, and re-layouts: 5.64 us -> none  [the longest x1 1.61 us: per_device(): sums[5, :inner_width]]
where the time goes in v7:
time: 334 us; the launch traced here: 333 us
  Pallas kernels  320 us (96%)
  local copies, waits for them, and re-layouts  11.3 us (3%)
    pallas_call x1, Pallas kernels, backward(): pl.pallas_call(functools.partial(backward_kernel, blocks, nseq * blocks,...  152 us
    pallas_call x1, Pallas kernels, gate(): pl.pallas_call(functools.partial(gate_kernel, chips, ranks), in_specs=[ON...  57.8 us
    pallas_call x1, Pallas kernels, project(): pl.pallas_call(functools.partial(project_kernel, chips, ranks, heads), in...  56.4 us
    pallas_call x1, Pallas kernels, scan_forward_gather(): pl.pallas_call(functools.partial(scan_gather_kernel, blocks, nseq * block...  44.6 us
    pallas_call x1, Pallas kernels, emit(): pl.pallas_call(functools.partial(emit_kernel, ranks, heads), in_specs=[ON...  8.59 us

profile of v7, /device:TPU:0, one launch (start us, length us, event | category | flops | bytes accessed | tf_op | source)
XLA Modules:
  0.0 332.9 jit_solution(7932356352771104800)
XLA Ops:
  0.6 1.3 select_maximum_fusion.heads_in
  1.9 1.3 broadcast_in_dim.11.bias_in
  3.3 0.8 copy.28
  4.1 2.0 copy.30
  6.2 3.4 %fusion = (bf16[256,1,1024]{2,1,0:T(2,128)(2,1)S(1)}, bf16[256,1,1024]{2,1,0:T(2,128)(2,1)S(1)}) fusion(bf16[256,2,1024]{2,1,0:T(2,128)(2,1)} %param.17), kind=kLoop, calls=%fused_computation.6 | loop fusion | bytes 2097152 | tf_op jit(solution)/shard_map/slice | solution.py:1840
  9.6 1.2 copy_bitcast_fusion
  10.7 1.0 concatenate.3.wx_own
  11.7 56.4 %project.1 = (f32[1024,1024]{1,0:T(8,128)}, f32[1024,128]{1,0:T(8,128)}, f32[1024,256]{1,0:T(8,128)}, s32[1024,128]{1,0:T(8,128)}, f32[8,1024]{1,0:T(8,128)}, /*...) custom-call(bf16[256,2048]{1,0:T(8,128)(2,1)} %refs_17_.1, ...), custom_call_target="tpu_custom_call" | custom-call | tf_op jit(solution)/shard_map/project/pallas_call | solution.py:1026
  68.1 44.6 %scan_forward.1 = (f32[1024,1024]{1,0:T(8,128)}, bf16[1024,1024]{1,0:T(8,128)(2,1)}, f32[1024,1024]{1,0:T(8,128)}, f32[1024,256]{1,0:T(8,128)}, bf16[2048,1024]{1,0:T(8,128)(2,1)}, /*index=5*/bf16[1024,2048]{1,0:T(8,128)(2,1)}) custom-call(f32[1024,1024]{1,0:T(8,128)} %get-tuple-element.57.refs_0_, f32[1024,256]{1,0:T(8,128)} %get-tuple-element.58.refs_1_.refs_2_, ...), custom_call_target="tpu_custom_call" | custom-call | tf_op jit(solution)/shard_map/scan_forward/pallas_call | solution.py:1086
  112.7 57.8 %gate.1 = (bf16[1024,1024]{1,0:T(8,128)(2,1)}, f32[1024,1024]{1,0:T(8,128)}, bf16[1024,1024]{1,0:T(8,128)(2,1)}, f32[8,1024]{1,0:T(8,128)}, bf16[2048,1024]{1,0:T(8,128)(2,1)}) custom-call(f32[8,1024]{1,0:T(8,128)} %get-tuple-element.68.gain_ref, bf16[256,1024]{1,0:T(8,128)(2,1)} %bitcast.10, bf16[1024,2048]{1,0:T(8,128)(2,1)} %get-tuple-element.69.normed_in.refs_22_, ...), custom_call_target="tpu_custom_call" | custom-call | tf_op jit(solution)/shard_map/gate/pallas_call | solution.py:1243
  170.5 152.2 %backward.1 = (f32[8,4352]{1,0:T(8,128)}, f32[8,256]{1,0:T(8,128)}, f32[256,1024]{1,0:T(8,128)}, f32[256,1024]{1,0:T(8,128)}, f32[256,1152]{1,0:T(8,128)}, /*ind...) custom-call(f32[1024,1024]{1,0:T(8,128)} %get-tuple-element.57.refs_, ...), custom_call_target="tpu_custom_call" | custom-call | tf_op jit(solution)/shard_map/backward/pallas_call | solution.py:1679
  322.7 8.6 %emit.1 = (f32[256,2,1024]{2,1,0:T(2,128)}, f32[256,16]{1,0:T(8,128)}, f32[1024,256]{1,0:T(8,128)}, f32[4,4352]{1,0:T(4,128)}, f32[4352]{0:T(1024)}, /*index=5*/...) custom-call(f32[8,4352]{1,0:T(8,128)} %get-tuple-element.80.sums_ref, ...), custom_call_target="tpu_custom_call" | custom-call | tf_op jit(solution)/shard_map/emit/pallas_call | solution.py:1804
  331.3 1.6 copy.31
  (1 shorter events, 0.0 us)

commit v8 on v7

--- a/solution.py
+++ b/solution.py
@@ -912,10 +912,12 @@
 
 
 def prepare(
-    rank, heads, seg_in, taps_in, bias_in, heads_in, gain_in,
+    rank, heads, seg_in, taps_in, bias_in, heads_in, gain_in, wo_in, bias_row, wo_out,
     seg_out, tapx_out, tapbc_out, par_out, skip_out, gain_out, spread_out,
 ):
     width, inner = tapx_out.shape[1], gain_in.shape[1]
+    bias_row[0:1] = bias_in[...][None]
+    wo_out[...] = jnp.transpose(wo_in[...].astype(f32)).astype(bf16)
     length = seg_in.shape[1]
     for s in range(seg_in.shape[0]):
         for r in range(0, length, LANES):
@@ -925,8 +927,8 @@
     own = pl.ds(pl.multiple_of(rank * width, LANES), width)
     tapx_out[...] = jnp.zeros_like(tapx_out)
     tapbc_out[...] = jnp.zeros_like(tapbc_out)
-    tapx_out[0:4], tapx_out[4:5] = taps_in[:, own], bias_in[:, own]
-    tapbc_out[0:4], tapbc_out[4:5] = taps_in[:, inner:], bias_in[:, inner:]
+    tapx_out[0:4], tapx_out[4:5] = taps_in[:, own], bias_row[0:1, own]
+    tapbc_out[0:4], tapbc_out[4:5] = taps_in[:, inner:], bias_row[0:1, inner:]
     gain_out[...] = jnp.broadcast_to(gain_in[:, own], gain_out.shape)
     row = lax.broadcasted_iota(jnp.int32, spread_out.shape, 0)
     col = lax.broadcasted_iota(jnp.int32, spread_out.shape, 1)
@@ -937,8 +939,12 @@
     row = lax.broadcasted_iota(jnp.int32, (LANES, LANES), 0)
     col = lax.broadcasted_iota(jnp.int32, (LANES, LANES), 1)
     lane = jnp.where(col >= half, col - half, col)
+    lines = [ref[...][None] for ref in heads_in]
+    lines = jnp.concatenate(lines + [jnp.zeros((5, lines[0].shape[1]), f32)], axis=0)
+    if lines.shape[1] < LANES:
+        lines = jnp.concatenate([lines, jnp.zeros((8, LANES - lines.shape[1]), f32)], axis=1)
     picked = exact_mm(
-        heads_in[...], ((row == rank * heads + lane) & (lane < heads)).astype(bf16)
+        lines, ((row == rank * heads + lane) & (lane < heads)).astype(bf16)
     )
     lane = lax.broadcasted_iota(jnp.int32, (1, LANES), 1)
     there = jnp.where(lane >= half, lane - half, lane) < heads
@@ -950,9 +956,10 @@
 
 
 def project_kernel(
-    chips, ranks, heads, res_ref, gain_ref, ws_ref, seg_in, taps_in, bias_in, heads_in, gated_in, wx_own,
+    chips, ranks, heads, res_ref, gain_ref, ws_ref, seg_in, taps_in, bias_in, a_in, b_in, c_in, gated_in, wo_in,
+    wx_own,
     x_ref, st_ref, bc_ref, seg_out, tapx_out, tapbc_out, par_out, skip_out, gain_out, spread_out,
-    normed_out, wx_out, own, normed, wx, *sems
+    wo_out, normed_out, wx_out, own, normed, wx, bias_row, *sems
 ):
     greet(chips, ranks)
     line = LineGather(wx_own, wx, *sems[:3], chips)
@@ -968,7 +975,7 @@
     row_loop(own.shape[0], 32, norm)
     tensor.step(0)
     prepare(
-        line.rank, heads, seg_in, taps_in, bias_in, heads_in, gated_in,
+        line.rank, heads, seg_in, taps_in, bias_in, (a_in, b_in, c_in), gated_in, wo_in, bias_row, wo_out,
         seg_out, tapx_out, tapbc_out, par_out, skip_out, gain_out, spread_out,
     )
     line.step(1)
@@ -1018,31 +1025,32 @@
 
 
 def project(
-    number, chips, ranks, heads, residual, norm_gain, ws, segments, taps, bias, by_head, gated_gain, wx_own
+    number, chips, ranks, heads, residual, norm_gain, ws, segments, taps, bias, by_head, gated_gain,
+    out_weight, wx_own,
 ):
     rows, model = residual.shape
     tokens, width = rows * ranks, wx_own.shape[1]
     inner = width - LANES
     return pl.pallas_call(
         functools.partial(project_kernel, chips, ranks, heads),
-        in_specs=[ONCHIP] * 8 + [ANY],
-        out_specs=[ONCHIP] * 10 + [ANY, ANY],
+        in_specs=[ONCHIP] * 11 + [ANY],
+        out_specs=[ONCHIP] * 11 + [ANY, ANY],
         out_shape=[
             shaped((tokens, inner), f32), shaped((tokens, LANES), f32),
             shaped((tokens, ws.shape[1]), f32),
             shaped((tokens, LANES), jnp.int32), shaped((8, inner), f32), shaped((8, ws.shape[1]), f32),
             shaped((8, LANES), f32), shaped((8, inner), f32), shaped((8, inner), f32),
-            shaped((LANES, inner), bf16),
+            shaped((LANES, inner), bf16), shaped(out_weight.shape[::-1], bf16),
             shaped((tokens, model), bf16), shaped((model, width), bf16),
         ],
         scratch_shapes=[
             pltpu.VMEM((rows, model), bf16), pltpu.VMEM((tokens, model), bf16),
-            pltpu.VMEM((model, width), bf16),
+            pltpu.VMEM((model, width), bf16), pltpu.VMEM((8, taps.shape[1]), f32),
             *LineGather.scratch(chips), *TensorGather.scratch(ranks), dma(), dma(),
         ],
         compiler_params=params(number),
         name="project",
-    )(residual, norm_gain, ws, segments, taps, bias, by_head, gated_gain, wx_own)
+    )(residual, norm_gain, ws, segments, taps, bias, *by_head, gated_gain, out_weight, wx_own)
 
 
 def scan_gather_kernel(blocks, total, chips, ranks, *refs):
@@ -1830,17 +1838,15 @@
     inner_width = gated_gain.shape[0]
     nseq = segment_ids.shape[0]
     wx_own = jnp.concatenate([inner_weight[:, 1], on_lanes(step_weight)], axis=1)
-    by_head = jnp.stack([step_bias, decay_log, skip_gain])
-    by_head = jnp.pad(by_head, ((0, 5), (0, LANES - by_head.shape[1])))
-    x, st, bc, seg, tapx, tapbc, par, skip, gain, spread, normed, wx = project(
+    x, st, bc, seg, tapx, tapbc, par, skip, gain, spread, wo_own, normed, wx = project(
         1, chips, ranks, heads, residual, norm_gain[None], state_weight, segment_ids,
-        conv_weight, conv_bias[None], by_head, gated_gain[None], wx_own,
+        conv_weight, conv_bias, (step_bias, decay_log, skip_gain), gated_gain[None], out_weight, wx_own,
     )
     y, h, conv, convbc, wz, cot = scan_forward_gather(
         2, chips, ranks, inner_weight[:, 0], cotangent,
         x, bc, st, seg, tapx, tapbc, par, spread, skip, nseq,
     )
-    gz, gy, ng, ggain, wo = gate(3, chips, ranks, gain, out_weight.T, normed, wz, y, cot)
+    gz, gy, ng, ggain, wo = gate(3, chips, ranks, gain, wo_own, normed, wz, y, cot)
     sums, norm_grad, z_grad, out_grad, x_grad, block_out, residual_grad, state_grad, *_ = backward(
         4, chips, ranks, ggain, norm_gain[None], residual, cotangent, state_weight,
         gz, ng, normed, cot, wo, wz, wx,

time: 334 us -> 330 us (0.988)
  local copies, waits for them, and re-layouts: 11.3 us -> 7.94 us
where the time goes in v8:
time: 330 us; the launch traced here: 329 us
  Pallas kernels  320 us (97%)
  local copies, waits for them, and re-layouts  7.94 us (2%)
    pallas_call x1, Pallas kernels, backward(): pl.pallas_call(functools.partial(backward_kernel, blocks, nseq * blocks,...  152 us
    pallas_call x1, Pallas kernels, gate(): pl.pallas_call(functools.partial(gate_kernel, chips, ranks), in_specs=[ON...  57.8 us
    pallas_call x1, Pallas kernels, project(): pl.pallas_call(functools.partial(project_kernel, chips, ranks, heads), in...  56.6 us
    pallas_call x1, Pallas kernels, scan_forward_gather(): pl.pallas_call(functools.partial(scan_gather_kernel, blocks, nseq * block...  44.6 us
    pallas_call x1, Pallas kernels, emit(): pl.pallas_call(functools.partial(emit_kernel, ranks, heads), in_specs=[ON...  8.59 us

profile of v8, /device:TPU:0, one launch (start us, length us, event | category | flops | bytes accessed | tf_op | source)
XLA Modules:
  0.0 328.5 jit_solution(16510662246607009845)
XLA Ops:
  0.6 0.8 copy.28
  1.5 3.4 %fusion = (bf16[256,1,1024]{2,1,0:T(2,128)(2,1)S(1)}, bf16[256,1,1024]{2,1,0:T(2,128)(2,1)S(1)}) fusion(bf16[256,2,1024]{2,1,0:T(2,128)(2,1)} %param.17), kind=kLoop, calls=%fused_computation.2 | loop fusion | bytes 2097152 | tf_op jit(solution)/shard_map/slice | solution.py:1846
  4.9 1.2 copy_bitcast_fusion
  6.1 1.0 concatenate.3.wx_own
  7.0 56.6 %project.1 = (f32[1024,1024]{1,0:T(8,128)}, f32[1024,128]{1,0:T(8,128)}, f32[1024,256]{1,0:T(8,128)}, s32[1024,128]{1,0:T(8,128)}, f32[8,1024]{1,0:T(8,128)}, /*...) custom-call(bf16[256,2048]{1,0:T(8,128)(2,1)} %refs_17_.1, ...), custom_call_target="tpu_custom_call" | custom-call | tf_op jit(solution)/shard_map/project/pallas_call | solution.py:1034
  63.6 44.6 %scan_forward.1 = (f32[1024,1024]{1,0:T(8,128)}, bf16[1024,1024]{1,0:T(8,128)(2,1)}, f32[1024,1024]{1,0:T(8,128)}, f32[1024,256]{1,0:T(8,128)}, bf16[2048,1024]{1,0:T(8,128)(2,1)}, /*index=5*/bf16[1024,2048]{1,0:T(8,128)(2,1)}) custom-call(f32[1024,1024]{1,0:T(8,128)} %get-tuple-element.58.refs_0_, f32[1024,256]{1,0:T(8,128)} %get-tuple-element.59.refs_1_.refs_2_, ...), custom_call_target="tpu_custom_call" | custom-call | tf_op jit(solution)/shard_map/scan_forward/pallas_call | solution.py:1094
  108.2 57.8 %gate.1 = (bf16[1024,1024]{1,0:T(8,128)(2,1)}, f32[1024,1024]{1,0:T(8,128)}, bf16[1024,1024]{1,0:T(8,128)(2,1)}, f32[8,1024]{1,0:T(8,128)}, bf16[2048,1024]{1,0:T(8,128)(2,1)}) custom-call(f32[8,1024]{1,0:T(8,128)} %get-tuple-element.69.gain_ref, bf16[256,1024]{1,0:T(8,128)(2,1)} %get-tuple-element.70.wo_own, ...), custom_call_target="tpu_custom_call" | custom-call | tf_op jit(solution)/shard_map/gate/pallas_call | solution.py:1251
  166.1 152.3 %backward.1 = (f32[8,4352]{1,0:T(8,128)}, f32[8,256]{1,0:T(8,128)}, f32[256,1024]{1,0:T(8,128)}, f32[256,1024]{1,0:T(8,128)}, f32[256,1152]{1,0:T(8,128)}, /*ind...) custom-call(f32[1024,1024]{1,0:T(8,128)} %get-tuple-element.58.refs_, ...), custom_call_target="tpu_custom_call" | custom-call | tf_op jit(solution)/shard_map/backward/pallas_call | solution.py:1687
  318.3 8.6 %emit.1 = (f32[256,2,1024]{2,1,0:T(2,128)}, f32[256,16]{1,0:T(8,128)}, f32[1024,256]{1,0:T(8,128)}, f32[4,4352]{1,0:T(4,128)}, f32[4352]{0:T(1024)}, /*index=5*/...) custom-call(f32[8,4352]{1,0:T(8,128)} %get-tuple-element.82.sums_ref, ...), custom_call_target="tpu_custom_call" | custom-call | tf_op jit(solution)/shard_map/emit/pallas_call | solution.py:1812
  326.9 1.6 copy.30
  (1 shorter events, 0.0 us)

commit v9 on v8

--- a/solution.py
+++ b/solution.py
@@ -957,10 +957,14 @@
 
 def project_kernel(
     chips, ranks, heads, res_ref, gain_ref, ws_ref, seg_in, taps_in, bias_in, a_in, b_in, c_in, gated_in, wo_in,
-    wx_own,
+    inner_in, step_in,
     x_ref, st_ref, bc_ref, seg_out, tapx_out, tapbc_out, par_out, skip_out, gain_out, spread_out,
-    wo_out, normed_out, wx_out, own, normed, wx, bias_row, *sems
+    wo_out, wz_out, normed_out, wx_out, own, normed, wx, bias_row, wx_own, *sems
 ):
+    step = step_in[...]
+    gap = jnp.zeros((step.shape[0], LANES // 2 - heads), bf16)
+    wx_own[:, : x_ref.shape[1]] = inner_in[:, 1, :]
+    wx_own[:, x_ref.shape[1] :] = jnp.concatenate([step, gap, step, gap], axis=1)
     greet(chips, ranks)
     line = LineGather(wx_own, wx, *sems[:3], chips)
     tensor = TensorGather(own, normed, *sems[3:6], ranks)
@@ -978,6 +982,7 @@
         line.rank, heads, seg_in, taps_in, bias_in, (a_in, b_in, c_in), gated_in, wo_in, bias_row, wo_out,
         seg_out, tapx_out, tapbc_out, par_out, skip_out, gain_out, spread_out,
     )
+    wz_out[...] = inner_in[:, 0, :]
     line.step(1)
     tensor.step(1)
     if chips > 2:
@@ -1026,31 +1031,33 @@
 
 def project(
     number, chips, ranks, heads, residual, norm_gain, ws, segments, taps, bias, by_head, gated_gain,
-    out_weight, wx_own,
+    out_weight, inner_weight, step_weight,
 ):
     rows, model = residual.shape
-    tokens, width = rows * ranks, wx_own.shape[1]
-    inner = width - LANES
+    tokens, inner = rows * ranks, inner_weight.shape[2]
+    width = inner + LANES
     return pl.pallas_call(
         functools.partial(project_kernel, chips, ranks, heads),
-        in_specs=[ONCHIP] * 11 + [ANY],
-        out_specs=[ONCHIP] * 11 + [ANY, ANY],
+        in_specs=[ONCHIP] * 13,
+        out_specs=[ONCHIP] * 12 + [ANY, ANY],
         out_shape=[
             shaped((tokens, inner), f32), shaped((tokens, LANES), f32),
             shaped((tokens, ws.shape[1]), f32),
             shaped((tokens, LANES), jnp.int32), shaped((8, inner), f32), shaped((8, ws.shape[1]), f32),
             shaped((8, LANES), f32), shaped((8, inner), f32), shaped((8, inner), f32),
             shaped((LANES, inner), bf16), shaped(out_weight.shape[::-1], bf16),
+            shaped((inner_weight.shape[0], inner), bf16),
             shaped((tokens, model), bf16), shaped((model, width), bf16),
         ],
         scratch_shapes=[
             pltpu.VMEM((rows, model), bf16), pltpu.VMEM((tokens, model), bf16),
             pltpu.VMEM((model, width), bf16), pltpu.VMEM((8, taps.shape[1]), f32),
+            pltpu.VMEM((step_weight.shape[0], width), bf16),
             *LineGather.scratch(chips), *TensorGather.scratch(ranks), dma(), dma(),
         ],
         compiler_params=params(number),
         name="project",
-    )(residual, norm_gain, ws, segments, taps, bias, *by_head, gated_gain, out_weight, wx_own)
+    )(residual, norm_gain, ws, segments, taps, bias, *by_head, gated_gain, out_weight, inner_weight, step_weight)
 
 
 def scan_gather_kernel(blocks, total, chips, ranks, *refs):
@@ -1837,13 +1844,12 @@
     heads = step_weight.shape[1]
     inner_width = gated_gain.shape[0]
     nseq = segment_ids.shape[0]
-    wx_own = jnp.concatenate([inner_weight[:, 1], on_lanes(step_weight)], axis=1)
-    x, st, bc, seg, tapx, tapbc, par, skip, gain, spread, wo_own, normed, wx = project(
+    x, st, bc, seg, tapx, tapbc, par, skip, gain, spread, wo_own, wz_own, normed, wx = project(
         1, chips, ranks, heads, residual, norm_gain[None], state_weight, segment_ids,
-        conv_weight, conv_bias, (step_bias, decay_log, skip_gain), gated_gain[None], out_weight, wx_own,
+        conv_weight, conv_bias, (step_bias, decay_log, skip_gain), gated_gain[None], out_weight, inner_weight, step_weight,
     )
     y, h, conv, convbc, wz, cot = scan_forward_gather(
-        2, chips, ranks, inner_weight[:, 0], cotangent,
+        2, chips, ranks, wz_own, cotangent,
         x, bc, st, seg, tapx, tapbc, par, spread, skip, nseq,
     )
     gz, gy, ng, ggain, wo = gate(3, chips, ranks, gain, wo_own, normed, wz, y, cot)

time: 330 us -> 326 us (0.988)
  local copies, waits for them, and re-layouts: 7.94 us -> 3.01 us
    slice x1 -> x0, local copies, waits for them, and re-layouts: 3.4 us -> none  [per_device(): inner_weight[:, 0]]
where the time goes in v9:
time: 326 us; the launch traced here: 325 us
  Pallas kernels  322 us (99%)
    pallas_call x1, Pallas kernels, backward(): pl.pallas_call(functools.partial(backward_kernel, blocks, nseq * blocks,...  152 us
    pallas_call x1, Pallas kernels, project(): pl.pallas_call(functools.partial(project_kernel, chips, ranks, heads), in...  58.2 us
    pallas_call x1, Pallas kernels, gate(): pl.pallas_call(functools.partial(gate_kernel, chips, ranks), in_specs=[ON...  58 us
    pallas_call x1, Pallas kernels, scan_forward_gather(): pl.pallas_call(functools.partial(scan_gather_kernel, blocks, nseq * block...  44.6 us
    pallas_call x1, Pallas kernels, emit(): pl.pallas_call(functools.partial(emit_kernel, ranks, heads), in_specs=[ON...  8.59 us

profile of v9, /device:TPU:0, one launch (start us, length us, event | category | flops | bytes accessed | tf_op | source)
XLA Modules:
  0.0 325.3 jit_solution(13086910324457791891)
XLA Ops:
  0.6 1.4 copy.27.step_in
  2.1 58.2 %project.1 = (f32[1024,1024]{1,0:T(8,128)}, f32[1024,128]{1,0:T(8,128)}, f32[1024,256]{1,0:T(8,128)}, s32[1024,128]{1,0:T(8,128)}, f32[8,1024]{1,0:T(8,128)}, /*...) custom-call(bf16[256,2048]{1,0:T(8,128)(2,1)} %refs_17_.1, ...), custom_call_target="tpu_custom_call" | custom-call | tf_op jit(solution)/shard_map/project/pallas_call | solution.py:1039
  60.3 44.6 %scan_forward.1 = (f32[1024,1024]{1,0:T(8,128)}, bf16[1024,1024]{1,0:T(8,128)(2,1)}, f32[1024,1024]{1,0:T(8,128)}, f32[1024,256]{1,0:T(8,128)}, bf16[2048,1024]{1,0:T(8,128)(2,1)}, /*index=5*/bf16[1024,2048]{1,0:T(8,128)(2,1)}) custom-call(f32[1024,1024]{1,0:T(8,128)} %get-tuple-element.59.refs_0_, f32[1024,256]{1,0:T(8,128)} %get-tuple-element.60.refs_1_.refs_2_, ...), custom_call_target="tpu_custom_call" | custom-call | tf_op jit(solution)/shard_map/scan_forward/pallas_call | solution.py:1101
  104.9 58.0 %gate.1 = (bf16[1024,1024]{1,0:T(8,128)(2,1)}, f32[1024,1024]{1,0:T(8,128)}, bf16[1024,1024]{1,0:T(8,128)(2,1)}, f32[8,1024]{1,0:T(8,128)}, bf16[2048,1024]{1,0:T(8,128)(2,1)}) custom-call(f32[8,1024]{1,0:T(8,128)} %get-tuple-element.71.gain_ref, bf16[256,1024]{1,0:T(8,128)(2,1)} %get-tuple-element.72.wo_own, ...), custom_call_target="tpu_custom_call" | custom-call | tf_op jit(solution)/shard_map/gate/pallas_call | solution.py:1258
  162.9 152.2 %backward.1 = (f32[8,4352]{1,0:T(8,128)}, f32[8,256]{1,0:T(8,128)}, f32[256,1024]{1,0:T(8,128)}, f32[256,1024]{1,0:T(8,128)}, f32[256,1152]{1,0:T(8,128)}, /*ind...) custom-call(f32[1024,1024]{1,0:T(8,128)} %get-tuple-element.59.refs_, ...), custom_call_target="tpu_custom_call" | custom-call | tf_op jit(solution)/shard_map/backward/pallas_call | solution.py:1694
  315.1 8.6 %emit.1 = (f32[256,2,1024]{2,1,0:T(2,128)}, f32[256,16]{1,0:T(8,128)}, f32[1024,256]{1,0:T(8,128)}, f32[4,4352]{1,0:T(4,128)}, f32[4352]{0:T(1024)}, /*index=5*/...) custom-call(f32[8,4352]{1,0:T(8,128)} %get-tuple-element.84.sums_ref, ...), custom_call_target="tpu_custom_call" | custom-call | tf_op jit(solution)/shard_map/emit/pallas_call | solution.py:1819
  323.7 1.6 copy.28
